TPU v7x, 32 devices: a whole 2x2x4 slice. The times are simulated.
32 devices in a mesh: dp: 4 (over y, x), space: 8 (over z, core).
Axes of the slice: x: 2, y: 2, z: 4, core: 2. Of those that a mesh axis runs over, the one named last changes fastest.
Arguments:
- node_scalar: bfloat16 [4096, 1024], P(('dp', 'space')), may hold values from -6 to 6
- node_vector: bfloat16 [3, 4096, 256], P(None, ('dp', 'space')), may hold values from -6 to 6
- edge_scalar: bfloat16 [4096, 960], P(('dp', 'space')), may hold values from -6 to 6
- edge_vector: bfloat16 [3, 122880], P(None, ('dp', 'space')), may hold values from -6 to 6
- neighbours: int32 [4096, 30], P(('dp', 'space')), may hold values from 0 to 255, as said below
- send_rows: int32 [32, 8, 16], P(('dp', 'space')), may hold values from -1 to 127, as said below
- complex_id: int32 [4096], P('dp'), may hold values 0 or 1
- cotangent: bfloat16 [4096, 512], P(('dp', 'space')), may hold values from -6 to 6
- w_node: bfloat16 [1024, 2048], replicated, may hold values from -0.1875 to 0.1875
- w_edge: bfloat16 [32, 1024], replicated, may hold values from -1 to 1
- w_norms: bfloat16 [513, 1024], replicated, may hold values from -0.25 to 0.25
- vec_node: bfloat16 [256, 1026], replicated, may hold values from -0.375 to 0.375
- vec_edge: bfloat16 [1, 513], replicated, may hold values from -6 to 6
- vec_out: bfloat16 [513, 256], replicated, may hold values from -0.25 to 0.25
- norm_gain: bfloat16 [1024], replicated, may hold values from 0.5 to 1.5
- ff_vec: bfloat16 [256, 256], replicated, may hold values from -0.375 to 0.375
- ff_scalar: bfloat16 [1280, 1024], replicated, may hold values from -0.15625 to 0.15625
- ff_up: bfloat16 [256, 256], replicated, may hold values from -0.375 to 0.375
- w_embed: bfloat16 [1280, 512], replicated, may hold values from -0.15625 to 0.15625
- attn_gain: bfloat16 [512], replicated, may hold values from 0.5 to 1.5
- w_qkv: bfloat16 [512, 1536], replicated, may hold values from -0.25 to 0.25
- w_out: bfloat16 [512, 512], replicated, may hold values from -6 to 6
- ffn_gain: bfloat16 [512], replicated, may hold values from 0.5 to 1.5
- w_up: bfloat16 [512, 2048], replicated, may hold values from -0.25 to 0.25
- w_down: bfloat16 [2048, 512], replicated, may hold values from -0.125 to 0.125
Outputs:
- stream_out: bfloat16 [4096, 512], P(('dp', 'space'))
- grad_scalar: bfloat16 [4096, 1024], P(('dp', 'space'))
- grad_vector: bfloat16 [3, 4096, 256], P(None, ('dp', 'space'))
- grad_w_node: float32 [1024, 2048], P('space')
- grad_w_edge: float32 [32, 1024], P(None, 'space')
- grad_w_norms: float32 [513, 1024], P(None, 'space')
- grad_vec_node: float32 [256, 1026], P('space')
- grad_vec_edge: float32 [1, 513], replicated
- grad_vec_out: float32 [513, 256], P(None, 'space')
- grad_norm_gain: float32 [1024], P('space')
- grad_ff_vec: float32 [256, 256], P('space')
- grad_ff_scalar: float32 [1280, 1024], P('space')
- grad_ff_up: float32 [256, 256], P('space')
- grad_w_embed: float32 [1280, 512], P('space')
- grad_attn_gain: float32 [512], P('space')
- grad_w_qkv: float32 [512, 1536], P('space')
- grad_w_out: float32 [512, 512], P('space')
- grad_ffn_gain: float32 [512], P('space')
- grad_w_up: float32 [512, 2048], P('space')
- grad_w_down: float32 [2048, 512], P('space')
Inputs may be any that keep to these rules, and one draw needn't show every extreme that they name: `neighbours`: an entry below 128 is a row of the residue's own device; any other entry is 128 + d * 16 + c with send_rows[d, p, c] not -1 (a live slot sent to this device p by device d of the same batch). For device q of a space group, send_rows[q, d] holds the rows sent to device d: the live ones first, then -1. Rows may repeat. Blocks form a periodic cube grid of 8 blocks; live rows go only to the up to 26 adjacent blocks, between 8 and 16 to each, and some pair has 16 in every draw.
All inputs are finite; a program needn't handle non-finite values. No bound on the sum of `complex_id` on one device may be relied on, other than what follows from the above.
Results may differ from a plain program's by a relative error of at most 0.018.
Values may be sent and summed in bfloat16 or wider, within the bound.
A program may use at most 320 MiB of HBM per device.

v0:
```python
import functools
import math

import jax
import jax.numpy as jnp
from jax import lax
from jax.experimental import pallas as pl
from jax.experimental.pallas import tpu as pltpu
from jax.sharding import PartitionSpec as P

D_S = 1024
D_V = 256
H_V = 513
H_P = 640
D_E = 32
NEIGH = 30
D_MODEL = 512
HEADS = 8
HEAD_DIM = 64
CAP = 16
GROUP = 5
VMEM_LIMIT = 60 * 1024 * 1024

MESH = pl.DeviceIdType.MESH
BF = jnp.bfloat16
F32 = jnp.float32


def layer_norm(values, gain_row):
    centred = values - jnp.mean(values, axis=-1, keepdims=True)
    spread = jnp.mean(centred * centred, axis=-1, keepdims=True)
    return centred * lax.rsqrt(spread + 1e-05) * gain_row


def vector_norm(vectors):
    mean_power = jnp.mean(jnp.sum(vectors * vectors, axis=0), axis=-1, keepdims=True)
    return vectors * lax.rsqrt(mean_power + 1e-05)[None]


def length_plus(vectors):
    return jnp.sqrt(jnp.sum(vectors * vectors, axis=0) + 1.0)


def vector_gate(vectors):
    return vectors * jax.nn.sigmoid(length_plus(vectors))[None]


def gelu_exact(values):
    return jax.nn.gelu(values, approximate=False)


def product(former, latter):
    return jnp.dot(former, latter, preferred_element_type=F32)


def product_lead(former, latter):
    leading = tuple(range(former.ndim - 1))
    return lax.dot_general(
        former, latter, ((leading, leading), ((), ())), preferred_element_type=F32
    )


def product_back(former, latter):
    return lax.dot_general(
        former, latter, (((former.ndim - 1,), (1,)), ((), ())), preferred_element_type=F32
    )


def pullback(function, at_point, cotangent_in):
    unused, puller = jax.vjp(function, at_point)
    return puller(cotangent_in)[0]


def sigmoid(values):
    return 0.5 * jnp.tanh(0.5 * values) + 0.5


LANE_BLOCKS = ((0, 256), (256, 256), (512, 128))
ROW_TILE = 64


def edge_forward_kernel(
    near_ref, es_ref, ev_ref, a_ref, b_ref, p_ref, q_ref, ve_ref, vo_ref,
    aggs_ref, aggv_ref, h_ref, lx_ref, ds_ref, z_ref, x_scr,
):
    nodes = b_ref.shape[0]
    table = p_ref.shape[1]
    rows = GROUP * nodes
    idx = near_ref[...].reshape(rows, 1)
    x_scr[:, :table] = (idx == lax.broadcasted_iota(jnp.int32, (rows, table), 1)).astype(BF)
    one_hot = x_scr[:, :table]
    for start, width in LANE_BLOCKS:
        cols = pl.ds(start, width)
        gathered = [product(one_hot, p_ref[c, :, cols]) for c in range(3)]
        for k in range(GROUP):
            for first in range(0, nodes, ROW_TILE):
                at = k * nodes + first
                evk = ev_ref[k, pl.ds(first, ROW_TILE), :]
                total = None
                for c in range(3):
                    h = (
                        gathered[c][at : at + ROW_TILE]
                        + q_ref[c, pl.ds(first, ROW_TILE), cols]
                        + evk[:, c : c + 1] * ve_ref[:, cols]
                    )
                    h_ref[k, c, pl.ds(first, ROW_TILE), cols] = h.astype(BF)
                    total = h * h + 1.0 if total is None else total + h * h
                length = total * lax.rsqrt(total)
                if start == 512:
                    lane = lax.broadcasted_iota(jnp.int32, (ROW_TILE, width), 1)
                    length = jnp.where(
                        lane == 0, length, es_ref[k, pl.ds(first, ROW_TILE), :].astype(F32)
                    )
                length = length.astype(BF)
                x_scr[pl.ds(at, ROW_TILE), pl.ds(table + start, width)] = length
                lx_ref[k, pl.ds(first, ROW_TILE), cols] = length

    @pl.when(pl.program_id(0) == 0)
    def _():
        aggs_ref[...] = jnp.zeros_like(aggs_ref)
        aggv_ref[...] = jnp.zeros_like(aggv_ref)

    full = x_scr[...]
    for start in range(0, D_S, 256):
        cols = pl.ds(start, 256)
        pre = product(full, a_ref[:, cols])
        for first in range(0, nodes, ROW_TILE):
            part = pl.ds(first, ROW_TILE)
            acc = None
            for k in range(GROUP):
                at = k * nodes + first
                x = pre[at : at + ROW_TILE] + b_ref[part, cols]
                s = sigmoid(x)
                y = x * s
                ds_ref[k, part, cols] = (s + y * (1.0 - s)).astype(BF)
                acc = y if acc is None else acc + y
            aggs_ref[part, cols] += acc * (1.0 / NEIGH)
    ups = [
        product(h_ref[:, c, :, :].reshape(rows, H_P), vo_ref[...]) for c in range(3)
    ]
    for first in range(0, nodes, ROW_TILE):
        part = pl.ds(first, ROW_TILE)
        acc = [None] * 3
        for k in range(GROUP):
            at = k * nodes + first
            z = [ups[c][at : at + ROW_TILE] for c in range(3)]
            power = z[0] * z[0] + z[1] * z[1] + z[2] * z[2] + 1.0
            s = sigmoid(power * lax.rsqrt(power))
            for c in range(3):
                z_ref[k, c, part, :] = z[c].astype(BF)
                gated = z[c] * s
                acc[c] = gated if acc[c] is None else acc[c] + gated
        for c in range(3):
            aggv_ref[c, part, :] += acc[c] * (1.0 / NEIGH)


def edge_forward(near_col, es_pad, ev_col, mix, b_target, p_source, q_target, ve_row, vout):
    nodes = b_target.shape[0]
    table = p_source.shape[1]
    whole = lambda shape: pl.BlockSpec(shape, lambda g: (0,) * len(shape))
    slots = lambda *shape: pl.BlockSpec((GROUP,) + shape, lambda g: (g,) + (0,) * len(shape))
    return pl.pallas_call(
        edge_forward_kernel,
        grid=(NEIGH // GROUP,),
        in_specs=[
            slots(nodes, 1),
            slots(nodes, 128),
            slots(nodes, 3),
            whole((table + H_P, D_S)),
            whole((nodes, D_S)),
            whole((3, table, H_P)),
            whole((3, nodes, H_P)),
            whole((1, H_P)),
            whole((H_P, D_V)),
        ],
        out_specs=[
            whole((nodes, D_S)),
            whole((3, nodes, D_V)),
            slots(3, nodes, H_P),
            slots(nodes, H_P),
            slots(nodes, D_S),
            slots(3, nodes, D_V),
        ],
        out_shape=[
            jax.ShapeDtypeStruct((nodes, D_S), F32),
            jax.ShapeDtypeStruct((3, nodes, D_V), F32),
            jax.ShapeDtypeStruct((NEIGH, 3, nodes, H_P), BF),
            jax.ShapeDtypeStruct((NEIGH, nodes, H_P), BF),
            jax.ShapeDtypeStruct((NEIGH, nodes, D_S), BF),
            jax.ShapeDtypeStruct((NEIGH, 3, nodes, D_V), BF),
        ],
        scratch_shapes=[pltpu.VMEM((GROUP * nodes, table + H_P), BF)],
        compiler_params=pltpu.CompilerParams(vmem_limit_bytes=VMEM_LIMIT),
        name="edge_forward",
    )(near_col, es_pad, ev_col, mix, b_target, p_source, q_target, ve_row, vout)


def message_kernel(
    near_ref, es_ref, ev_ref, a_ref, b_ref, p_ref, q_ref, ve_ref, vo_ref,
    aggs_ref, aggv_ref, h_ref, lx_ref, ds_ref, z_ref, x_scr, turn_scr,
):
    nodes = b_ref.shape[0]
    table = p_ref.shape[1]
    rows = GROUP * nodes
    first_slot = pl.program_id(0) * GROUP

    @pl.when(pl.program_id(0) == 0)
    def _():
        for n in range(4):
            ref = near_ref if n == 3 else ev_ref.at[n]
            turn_scr[n, pl.ds(0, NEIGH), :] = ref[...].astype(F32)
            turn_scr[n] = jnp.transpose(turn_scr[n])

    back = lax.rem(128 - first_slot, 128)
    ev = [pltpu.roll(turn_scr[n], back, 1) for n in range(4)]
    slots = ev[3]
    places = lax.broadcasted_iota(jnp.int32, (nodes, table), 1).astype(F32)
    edges_in = []
    for k in range(GROUP):
        x_scr[pl.ds(k * nodes, nodes), :table] = (slots[:, k : k + 1] == places).astype(BF)
        rows_in = pl.ds(pl.multiple_of((first_slot + k) * D_E, D_E), D_E)
        edges_in.append(
            jnp.transpose(
                jnp.concatenate(
                    [
                        jnp.zeros((16, nodes), F32),
                        es_ref[rows_in, :].astype(F32),
                        jnp.zeros((112 - D_E, nodes), F32),
                    ],
                    0,
                )
            )
        )
    one_hot = x_scr[:, :table]
    for start, width in LANE_BLOCKS:
        cols = pl.ds(start, width)
        gathered = [product(one_hot, p_ref[c, :, cols]) for c in range(3)]
        for k in range(GROUP):
            for first in range(0, nodes, ROW_TILE):
                at = k * nodes + first
                total = None
                for c in range(3):
                    h = (
                        gathered[c][at : at + ROW_TILE]
                        + q_ref[c, pl.ds(first, ROW_TILE), cols]
                        + ev[c][first : first + ROW_TILE, k : k + 1]
                        * ve_ref[:, pl.ds(D_S + 2 * D_MODEL + start, width)]
                    )
                    h_ref[k, c, pl.ds(first, ROW_TILE), cols] = h.astype(BF)
                    total = h * h + 1.0 if total is None else total + h * h
                length = total * lax.rsqrt(total)
                if start == 512:
                    lane = lax.broadcasted_iota(jnp.int32, (ROW_TILE, width), 1)
                    length = jnp.where(
                        lane == 0, length, edges_in[k][first : first + ROW_TILE]
                    )
                length = length.astype(BF)
                x_scr[pl.ds(at, ROW_TILE), pl.ds(table + start, width)] = length
                lx_ref[k, pl.ds(first, ROW_TILE), cols] = length

    @pl.when(pl.program_id(0) == 0)
    def _():
        aggs_ref[...] = jnp.zeros_like(aggs_ref)
        aggv_ref[...] = jnp.zeros_like(aggv_ref)

    full = x_scr[...]
    for start in range(0, D_S, 256):
        cols = pl.ds(start, 256)
        pre = product(full, a_ref[:, cols])
        for first in range(0, nodes, ROW_TILE):
            part = pl.ds(first, ROW_TILE)
            acc = None
            for k in range(GROUP):
                at = k * nodes + first
                x = pre[at : at + ROW_TILE] + b_ref[part, cols]
                s = sigmoid(x)
                y = x * s
                ds_ref[k, part, cols] = (s + y * (1.0 - s)).astype(BF)
                acc = y if acc is None else acc + y
            aggs_ref[part, cols] += acc * (1.0 / NEIGH)
    ups = [
        product(h_ref[:, c, :, :].reshape(rows, H_P), vo_ref[...]) for c in range(3)
    ]
    for first in range(0, nodes, ROW_TILE):
        part = pl.ds(first, ROW_TILE)
        acc = [None] * 3
        for k in range(GROUP):
            at = k * nodes + first
            z = [ups[c][at : at + ROW_TILE] for c in range(3)]
            power = z[0] * z[0] + z[1] * z[1] + z[2] * z[2] + 1.0
            s = sigmoid(power * lax.rsqrt(power))
            for c in range(3):
                z_ref[k, c, part, :] = z[c].astype(BF)
                gated = z[c] * s
                acc[c] = gated if acc[c] is None else acc[c] + gated
        for c in range(3):
            aggv_ref[c, part, :] += acc[c] * (1.0 / NEIGH)


def message(near, edge_scalar, ev, mix, b_target, p_source, q_target, ve_row, vout):
    nodes = b_target.shape[0]
    table = p_source.shape[1]
    whole = lambda shape: pl.BlockSpec(shape, lambda g: (0,) * len(shape))
    slots = lambda *shape: pl.BlockSpec((GROUP,) + shape, lambda g: (g,) + (0,) * len(shape))
    return pl.pallas_call(
        message_kernel,
        grid=(NEIGH // GROUP,),
        in_specs=[
            whole(near.shape),
            whole(edge_scalar.shape),
            whole(ev.shape),
            whole((table + H_P, D_S)),
            whole((nodes, D_S)),
            whole((3, table, H_P)),
            whole((3, nodes, H_P)),
            whole(ve_row.shape),
            whole((H_P, D_V)),
        ],
        out_specs=[
            whole((nodes, D_S)),
            whole((3, nodes, D_V)),
            slots(3, nodes, H_P),
            slots(nodes, H_P),
            slots(nodes, D_S),
            slots(3, nodes, D_V),
        ],
        out_shape=[
            jax.ShapeDtypeStruct((nodes, D_S), F32),
            jax.ShapeDtypeStruct((3, nodes, D_V), F32),
            jax.ShapeDtypeStruct((NEIGH, 3, nodes, H_P), BF),
            jax.ShapeDtypeStruct((NEIGH, nodes, H_P), BF),
            jax.ShapeDtypeStruct((NEIGH, nodes, D_S), BF),
            jax.ShapeDtypeStruct((NEIGH, 3, nodes, D_V), BF),
        ],
        scratch_shapes=[
            pltpu.VMEM((GROUP * nodes, table + H_P), BF),
            pltpu.VMEM((4, 128, nodes), F32),
        ],
        compiler_params=pltpu.CompilerParams(vmem_limit_bytes=VMEM_LIMIT),
        name="message",
    )(near, edge_scalar, ev, mix, b_target, p_source, q_target, ve_row, vout)


def edge_backward_kernel(
    near_ref, ev_ref, evr_ref, h_ref, lx_ref, ds_ref, z_ref, gs_ref, gv_ref, wn_ref, vo_ref,
    ga_ref, gw_ref, gb_ref, gp_ref, gq_ref, gvo_ref, pre_scr, up_scr, gh_scr,
):
    nodes = gs_ref.shape[0]
    table = ga_ref.shape[0]
    rows = GROUP * nodes

    @pl.when(pl.program_id(0) == 0)
    def _():
        for ref in (ga_ref, gw_ref, gb_ref, gp_ref, gq_ref, gvo_ref):
            ref[...] = jnp.zeros_like(ref)

    for start in range(0, D_S, 256):
        cols = pl.ds(start, 256)
        for first in range(0, nodes, ROW_TILE):
            part = pl.ds(first, ROW_TILE)
            share = gs_ref[part, cols]
            acc = None
            for k in range(GROUP):
                g = (ds_ref[k, part, cols].astype(F32) * share).astype(BF)
                pre_scr[pl.ds(k * nodes + first, ROW_TILE), cols] = g
                g = g.astype(F32)
                acc = g if acc is None else acc + g
            gb_ref[part, cols] += acc
    for first in range(0, nodes, ROW_TILE):
        part = pl.ds(first, ROW_TILE)
        share = [gv_ref[c, part, :] for c in range(3)]
        for k in range(GROUP):
            z = [z_ref[k, c, part, :].astype(F32) for c in range(3)]
            power = z[0] * z[0] + z[1] * z[1] + z[2] * z[2] + 1.0
            inverse = lax.rsqrt(power)
            s = sigmoid(power * inverse)
            dot = z[0] * share[0] + z[1] * share[1] + z[2] * share[2]
            factor = dot * inverse * (s * (1.0 - s))
            for c in range(3):
                up_scr[c, pl.ds(k * nodes + first, ROW_TILE), :] = (
                    share[c] * s + z[c] * factor
                ).astype(BF)

    near = near_ref[0]
    one_hot = (lax.broadcasted_iota(jnp.int32, (table, rows), 0) == near).astype(BF)
    grad_pre = pre_scr[...]
    ga_ref[...] += product(one_hot, grad_pre)
    lx = lx_ref[...].reshape(rows, H_P)
    gw_ref[...] += lax.dot_general(
        lx, grad_pre, (((0,), (0,)), ((), ())), preferred_element_type=F32
    )
    for start, width in LANE_BLOCKS:
        cols = pl.ds(start, width)
        grad_length = product_back(grad_pre, wn_ref[cols, :])
        grad_direct = [product_back(up_scr[c], vo_ref[cols, :]) for c in range(3)]
        for first in range(0, nodes, ROW_TILE):
            part = pl.ds(first, ROW_TILE)
            acc = [None] * 3
            for k in range(GROUP):
                at = k * nodes + first
                ratio = grad_length[at : at + ROW_TILE] * pl.reciprocal(
                    lx_ref[k, part, cols].astype(F32), approx=True
                )
                if start == 512:
                    lane = lax.broadcasted_iota(jnp.int32, (ROW_TILE, width), 1)
                    ratio = jnp.where(lane == 0, ratio, 0.0)
                for c in range(3):
                    g = grad_direct[c][at : at + ROW_TILE] + ratio * h_ref[
                        k, c, part, cols
                    ].astype(F32)
                    gh_scr[c, pl.ds(at, ROW_TILE), cols] = g.astype(BF)
                    acc[c] = g if acc[c] is None else acc[c] + g
            for c in range(3):
                gq_ref[c, part, cols] += acc[c]
    for c in range(3):
        evr = jnp.broadcast_to(evr_ref[0, c : c + 1, :], (16, rows))
        lead = jnp.concatenate([one_hot, evr.astype(BF)], axis=0)
        gp_ref[c] += product(lead, gh_scr[c])
        gvo_ref[...] += lax.dot_general(
            up_scr[c],
            h_ref[:, c, :, :].reshape(rows, H_P),
            (((0,), (0,)), ((), ())),
            preferred_element_type=F32,
        )


def edge_backward(near_row, ev_col, ev_row, hidden, lx, dsilu, update, gs, gv, wn, vout, table):
    nodes = gs.shape[0]
    rows = GROUP * nodes
    whole = lambda shape: pl.BlockSpec(shape, lambda g: (0,) * len(shape))
    slots = lambda *shape: pl.BlockSpec((GROUP,) + shape, lambda g: (g,) + (0,) * len(shape))
    steps = lambda *shape: pl.BlockSpec((1,) + shape, lambda g: (g,) + (0,) * len(shape))
    outs = [
        (table, D_S),
        (H_P, D_S),
        (nodes, D_S),
        (3, table + 16, H_P),
        (3, nodes, H_P),
        (D_V, H_P),
    ]
    return pl.pallas_call(
        edge_backward_kernel,
        grid=(NEIGH // GROUP,),
        in_specs=[
            steps(1, rows),
            slots(nodes, 3),
            steps(3, rows),
            slots(3, nodes, H_P),
            slots(nodes, H_P),
            slots(nodes, D_S),
            slots(3, nodes, D_V),
            whole((nodes, D_S)),
            whole((3, nodes, D_V)),
            whole((H_P, D_S)),
            whole((H_P, D_V)),
        ],
        out_specs=[whole(shape) for shape in outs],
        out_shape=[jax.ShapeDtypeStruct(shape, F32) for shape in outs],
        scratch_shapes=[
            pltpu.VMEM((rows, D_S), BF),
            pltpu.VMEM((3, rows, D_V), BF),
            pltpu.VMEM((3, rows, H_P), BF),
        ],
        compiler_params=pltpu.CompilerParams(vmem_limit_bytes=VMEM_LIMIT),
        name="edge_backward",
    )(near_row, ev_col, ev_row, hidden, lx, dsilu, update, gs, gv, wn, vout)


AT_AIN, AT_EMB, AT_FFIN, AT_FFH, AT_NV, FAC_NODE = 0, 512, 1792, 3072, 3840, 4608
AT_GELU, AT_GUP, AT_FIN, AT_COT, AT_ATT, AT_GBR, FAC_FEED = 0, 2048, 4096, 4608, 5120, 5632, 6144
AT_GQKV, AT_STREAM, AT_GPRE, AT_GFU, AT_GFH, FAC_BACK = 0, 1536, 2048, 3072, 3840, 4608
ROWS_F, ROWS_M, ROWS_S, ROWS_T = 512, 768, 640, 128

def full_block(shape):
    return pl.BlockSpec(shape, lambda: (0,) * len(shape))


def lead_product(former, latter):
    return lax.dot_general(
        former, latter, (((0,), (0,)), ((), ())), preferred_element_type=F32
    )


def swap_halves(values):
    return pltpu.roll(values, 64, 1)


def lower_half(shape):
    return lax.broadcasted_iota(jnp.int32, shape, 1) < 64


def pack_tall(tile, odd):
    rows = tile.shape[0] // 2
    top, low = tile[:rows], tile[rows:]
    side = lower_half((rows, 128))
    if odd:
        return jnp.where(side, swap_halves(top), low)
    return jnp.where(side, top, swap_halves(low))


def unpack_tall(block):
    rows = block.shape[0]
    side = lower_half((rows, 128))
    return jnp.concatenate(
        [jnp.where(side, block, 0.0), jnp.where(side, swap_halves(block), 0.0)], 0
    )


def centre(values):
    centred = values - jnp.mean(values, axis=-1, keepdims=True)
    inverse = lax.rsqrt(jnp.mean(centred * centred, axis=-1, keepdims=True) + 1e-05)
    return centred * inverse, inverse


def centre_back(hat, inverse, grad):
    return inverse * (
        grad
        - jnp.mean(grad, axis=-1, keepdims=True)
        - hat * jnp.mean(grad * hat, axis=-1, keepdims=True)
    )


def power_of(parts):
    return parts[0] * parts[0] + parts[1] * parts[1] + parts[2] * parts[2]


def node_forward_kernel(
    ns_ref, nv_ref, as_ref, av_ref, ng_ref, fv_ref, fs_ref, fu_ref, we_ref, ag_ref, wq_ref,
    s1_ref, v1_ref, ffh_ref, ffp_ref, ffu_ref, v2_ref, sz_ref, fac_ref, out_ref,
):
    nodes = ns_ref.shape[0]
    s1 = ns_ref[...].astype(F32) + as_ref[...]
    s1_ref[...] = s1
    hat, unused = centre(s1)
    normed_s = hat * ng_ref[...]
    v1 = [nv_ref[c].astype(F32) + av_ref[c] for c in range(3)]
    scale = lax.rsqrt(jnp.mean(power_of(v1), axis=-1, keepdims=True) + 1e-05)
    normed_v = [v * scale for v in v1]
    ffh = [product(v.astype(BF), fv_ref[...]) for v in normed_v]
    power = power_of(ffh) + 1.0
    fac_ref[:, pl.ds(AT_FFIN, D_S)] = normed_s.astype(BF)
    fac_ref[:, pl.ds(AT_FFIN + D_S, D_V)] = (power * lax.rsqrt(power)).astype(BF)
    ffp = product(fac_ref[:, pl.ds(AT_FFIN, D_S + D_V)], fs_ref[...])
    ffu = [product(h.astype(BF), fu_ref[...]) for h in ffh]
    for c in range(3):
        v1_ref[c] = v1[c]
        fac_ref[:, pl.ds(AT_FFH + c * D_V, D_V)] = ffh[c].astype(BF)
        fac_ref[:, pl.ds(AT_NV + c * D_V, D_V)] = normed_v[c].astype(BF)
        ffh_ref[c] = ffh[c]
        ffu_ref[c] = ffu[c]
    ffp_ref[...] = ffp
    s2 = normed_s + ffp * sigmoid(ffp)
    power = power_of(ffu) + 1.0
    gate = sigmoid(power * lax.rsqrt(power))
    v2 = [normed_v[c] + ffu[c] * gate for c in range(3)]
    for c in range(3):
        v2_ref[c] = v2[c]
    power = power_of(v2) + 1.0
    fac_ref[:, pl.ds(AT_EMB, D_S)] = s2.astype(BF)
    fac_ref[:, pl.ds(AT_EMB + D_S, D_V)] = (power * lax.rsqrt(power)).astype(BF)
    sz = product(fac_ref[:, pl.ds(AT_EMB, D_S + D_V)], we_ref[...])
    sz_ref[...] = sz
    hat, unused = centre(sz)
    attn_in = (hat * ag_ref[...]).astype(BF)
    fac_ref[:, pl.ds(AT_AIN, D_MODEL)] = attn_in
    q, k, v = [product(attn_in, wq_ref[:, pl.ds(n * D_MODEL, D_MODEL)]) for n in range(3)]
    pack_heads(q, k, v, out_ref)


def pack_heads(q, k, v, out_ref):
    nodes = q.shape[0]
    side = lower_half((nodes, 128))
    for pair in range(HEADS // 2):
        cols = slice(pair * 128, pair * 128 + 128)
        qp, kp, vp = q[:, cols], k[:, cols], v[:, cols]
        even = jnp.where(side, qp, swap_halves(kp))
        odd = jnp.where(side, swap_halves(qp), kp)
        for n, block in enumerate((even, odd)):
            head = 2 * pair + n
            out_ref[head, pl.ds(0, nodes), :] = block.astype(BF)
            out_ref[head, pl.ds(nodes, nodes // 2), :] = pack_tall(vp, n == 1).astype(BF)


def split_heads(x_ref, nodes):
    spaces = x_ref.shape[0]
    both = x_ref[:, pl.ds(0, nodes), :].reshape(spaces * nodes, 128).astype(F32)
    queries = jnp.where(lower_half(both.shape), both, 0.0).astype(BF)
    keys = swap_halves(both).astype(BF)
    values = jnp.concatenate(
        [unpack_tall(x_ref[d, pl.ds(nodes, nodes // 2), :].astype(F32)) for d in range(spaces)], 0
    ).astype(BF)
    return queries, keys, values


def attend_kernel(x_ref, id_ref, probs_ref, att_ref, out_ref):
    spaces = x_ref.shape[0]
    nodes = x_ref.shape[1] * 2 // 3
    count = spaces * nodes
    queries, keys, values = split_heads(x_ref, nodes)
    row_ids = id_ref[...]
    column_ids = jnp.transpose(jnp.broadcast_to(row_ids, (8, count)))[:, 0:1]
    block = 2 * nodes
    for first in range(0, count, block):
        scores = product_back(queries[first : first + block], keys) * HEAD_DIM ** (-0.5)
        same = column_ids[first : first + block] == row_ids
        scores = jnp.where(same, scores, -1000000000.0)
        shifted = jnp.exp(scores - jnp.max(scores, axis=-1, keepdims=True))
        probs = (shifted / jnp.sum(shifted, axis=-1, keepdims=True)).astype(BF)
        probs_ref[pl.ds(first, block), :] = probs
        att = product(probs, values)
        att_ref[pl.ds(first, block), :] = att
        for n in range(block // nodes):
            tile = att[n * nodes : (n + 1) * nodes]
            out_ref[first // nodes + n] = pack_tall(tile, False).astype(BF)


def attend_backward_kernel(x_ref, probs_ref, att_ref, g_ref, out_ref, gs_scr):
    spaces = x_ref.shape[0]
    nodes = x_ref.shape[1] * 2 // 3
    count = spaces * nodes
    queries, keys, values = split_heads(x_ref, nodes)
    grad = jnp.concatenate(
        [unpack_tall(g_ref[d].astype(F32)) for d in range(spaces)], 0
    )
    dots = jnp.sum(grad * att_ref[...], axis=-1, keepdims=True)
    grad = grad.astype(BF)
    block = 2 * nodes
    scale = HEAD_DIM ** (-0.5)
    grad_queries = []
    for first in range(0, count, block):
        grad_probs = product_back(grad[first : first + block], values)
        part = probs_ref[pl.ds(first, block), :].astype(F32)
        grad_scores = (part * (grad_probs - dots[first : first + block])).astype(BF)
        gs_scr[pl.ds(first, block), :] = grad_scores
        grad_queries.append(product(grad_scores, keys))
    grad_queries = jnp.concatenate(grad_queries, 0) * scale
    grad_keys = jnp.transpose(lead_product(queries, gs_scr[...])) * scale
    grad_values = jnp.transpose(lead_product(grad, probs_ref[...]))
    side = lower_half((nodes, 128))
    for d in range(spaces):
        rows = slice(d * nodes, (d + 1) * nodes)
        out_ref[d, pl.ds(0, nodes), :] = jnp.where(
            side, grad_queries[rows], swap_halves(grad_keys[rows])
        ).astype(BF)
        out_ref[d, pl.ds(nodes, nodes // 2), :] = pack_tall(grad_values[rows], False).astype(BF)


def merge_heads(block_ref, first, half):
    tiles = []
    for pair in range(HEADS // 2):
        even = unpack_tall(block_ref[2 * pair, pl.ds(first, half), :].astype(F32))
        odd = unpack_tall(block_ref[2 * pair + 1, pl.ds(first, half), :].astype(F32))
        tiles.append(even + swap_halves(odd))
    return jnp.concatenate(tiles, 1)


def feed_kernel(
    att_ref, sz_ref, wo_ref, fg_ref, wu_ref, wd_ref, cot_ref,
    out_ref, gatt_ref, gs1_ref, ggain_ref, fac_ref,
):
    nodes = sz_ref.shape[0]
    att = merge_heads(att_ref, 0, nodes // 2).astype(BF)
    fac_ref[:, pl.ds(AT_ATT, D_MODEL)] = att
    stream_one = sz_ref[...] + product(att, wo_ref[...])
    hat, inverse = centre(stream_one)
    ffn_in = (hat * fg_ref[...]).astype(BF)
    fac_ref[:, pl.ds(AT_FIN, D_MODEL)] = ffn_in
    ffn = wu_ref.shape[1]
    cot = cot_ref[...]
    fac_ref[:, pl.ds(AT_COT, D_MODEL)] = cot
    for start in range(0, ffn, 512):
        cols = pl.ds(start, 512)
        x = product(ffn_in, wu_ref[:, cols])
        cdf = 0.5 * (1.0 + lax.erf(x * (0.5**0.5)))
        fac_ref[:, pl.ds(AT_GELU + start, 512)] = (x * cdf).astype(BF)
        slope = cdf + x * jnp.exp(-0.5 * x * x) * ((0.5 / math.pi) ** 0.5)
        fac_ref[:, pl.ds(AT_GUP + start, 512)] = (
            product_back(cot, wd_ref[cols, :]) * slope
        ).astype(BF)
    out_ref[...] = (
        stream_one + product(fac_ref[:, pl.ds(AT_GELU, ffn)], wd_ref[...])
    ).astype(BF)
    grad_in = product_back(fac_ref[:, pl.ds(AT_GUP, ffn)], wu_ref[...])
    ggain_ref[...] = jnp.sum(grad_in * hat, axis=0, keepdims=True)
    grad_one = cot.astype(F32) + centre_back(hat, inverse, grad_in * fg_ref[...])
    gs1_ref[...] = grad_one
    branch = grad_one.astype(BF)
    fac_ref[:, pl.ds(AT_GBR, D_MODEL)] = branch
    grad_att = product_back(branch, wo_ref[...])
    for head in range(HEADS):
        tile = grad_att[:, head // 2 * 128 : head // 2 * 128 + 128]
        gatt_ref[head] = pack_tall(tile, head % 2 == 1).astype(BF)


def core_columns(values, core):
    values = values.astype(F32)
    side = lower_half((values.shape[0], 128))
    tiles = []
    for n in range(0, 512, 256):
        one, two = values[:, n : n + 128], values[:, n + 128 : n + 256]
        even = jnp.where(side, one, swap_halves(two))
        odd = jnp.where(side, swap_halves(one), two)
        tiles.append(jnp.where(core == 0, even, odd))
    return jnp.concatenate(tiles, 1).astype(BF)


def both_rows(own_ref, other_ref, start, width):
    return jnp.concatenate(
        [own_ref[:, pl.ds(start, width)], other_ref[:, pl.ds(start, width)]], 0
    )


def feed_grads_kernel(own_ref, other_ref, pack_ref):
    quads = pack_ref.shape[0]
    core = lax.rem(lax.axis_index("space"), 2)
    cot = both_rows(own_ref, other_ref, AT_COT, D_MODEL)
    for z in range(quads):
        start = pl.multiple_of(AT_GELU + (2 * z + core) * 256, 256)
        block = lead_product(both_rows(own_ref, other_ref, start, 256), cot)
        pack_ref[z, pl.ds(0, 256), :] = block.astype(BF)
    left = core_columns(both_rows(own_ref, other_ref, AT_FIN, D_MODEL), core)
    for n in range(4):
        block = lead_product(left, both_rows(own_ref, other_ref, AT_GUP + n * 512, 512)).astype(BF)
        for z in range(quads):
            pack_ref[z, pl.ds(256 + n * 64, 64), :] = block[z * 64 : (z + 1) * 64]


def node_grads_kernel(
    node_ref, node_other, back_ref, back_other, feed_ref, feed_other, pack_ref, tall_scr, low_scr
):
    quads = pack_ref.shape[0]
    core = lax.rem(lax.axis_index("space"), 2)
    left = core_columns(both_rows(node_ref, node_other, AT_AIN, D_MODEL), core)
    pairs = [
        (left, both_rows(back_ref, back_other, AT_GQKV + n * D_MODEL, D_MODEL)) for n in range(3)
    ]
    pairs.append(
        (
            core_columns(both_rows(feed_ref, feed_other, AT_ATT, D_MODEL), core),
            both_rows(feed_ref, feed_other, AT_GBR, D_MODEL),
        )
    )
    for n, (one, two) in enumerate(pairs):
        block = lead_product(one, two).astype(BF)
        for z in range(quads):
            pack_ref[z, pl.ds(n * 64, 64), :] = block[z * 64 : (z + 1) * 64]
    emb = both_rows(node_ref, node_other, AT_EMB, D_S + D_V)
    ffin = both_rows(node_ref, node_other, AT_FFIN, D_S + D_V)
    rights = [(emb, back_ref, back_other, AT_STREAM)]
    rights += [(ffin, back_ref, back_other, AT_GPRE + n * 512) for n in range(2)]
    for n, (one, own, other, start) in enumerate(rights):
        tall_scr[...] = lead_product(one, both_rows(own, other, start, 512)).astype(BF)
        for z in range(quads):
            rows = pl.ds(pl.multiple_of((2 * z + core) * 160, 32), 160)
            pack_ref[z, pl.ds(256 + n * 160, 160), :] = tall_scr[rows, :]
    vec = up = None
    for c in range(3):
        one = lead_product(
            both_rows(node_ref, node_other, AT_NV + c * D_V, D_V),
            both_rows(back_ref, back_other, AT_GFH + c * D_V, D_V),
        )
        vec = one if vec is None else vec + one
        one = lead_product(
            both_rows(node_ref, node_other, AT_FFH + c * D_V, D_V),
            both_rows(back_ref, back_other, AT_GFU + c * D_V, D_V),
        )
        up = one if up is None else up + one
    low_scr[...] = jnp.concatenate([vec, up], 1).astype(BF)
    for z in range(quads):
        rows = pl.ds(pl.multiple_of((2 * z + core) * 32, 32), 32)
        pack_ref[z, pl.ds(736, 32), :] = low_scr[rows, :]


def node_backward_kernel(
    gq_ref, gs1_ref, s1_ref, v1_ref, ffh_ref, ffp_ref, ffu_ref, v2_ref,
    sz_ref, ng_ref, fv_ref, fs_ref, fu_ref, we_ref, ag_ref, wq_ref, fgain_ref,
    gsone_ref, gvone_ref, gains_ref, back_ref,
):
    nodes = gs1_ref.shape[0]
    shards = gq_ref.shape[0]
    side = lower_half((nodes, 128))
    tiles = [[], []]
    for pair in range(HEADS // 2):
        even = gq_ref[2 * pair, pl.ds(0, nodes), :].astype(F32)
        odd = gq_ref[2 * pair + 1, pl.ds(0, nodes), :].astype(F32)
        tiles[0].append(jnp.where(side, even, swap_halves(odd)))
        tiles[1].append(jnp.where(side, swap_halves(even), odd))
    grads = [jnp.concatenate(tile, 1).astype(BF) for tile in tiles]
    grads.append(merge_heads(gq_ref, nodes, nodes // 2).astype(BF))
    for n in range(3):
        back_ref[:, pl.ds(AT_GQKV + n * D_MODEL, D_MODEL)] = grads[n]
    grad_in = product_back(back_ref[:, pl.ds(AT_GQKV, 3 * D_MODEL)], wq_ref[...])
    hat, inverse = centre(sz_ref[...])
    grad_attn_gain = jnp.sum(grad_in * hat, axis=0, keepdims=True)
    stream = gs1_ref[...] + centre_back(hat, inverse, grad_in * ag_ref[...])
    stream = stream.astype(BF)
    back_ref[:, pl.ds(AT_STREAM, D_MODEL)] = stream
    grad_emb = product_back(stream, we_ref[...])
    grad_s2, grad_len = grad_emb[:, :D_S], grad_emb[:, D_S:]
    v2 = [v2_ref[c] for c in range(3)]
    factor = grad_len * lax.rsqrt(power_of(v2) + 1.0)
    grad_v2 = [factor * v for v in v2]
    x = ffp_ref[...]
    s = sigmoid(x)
    grad_pre = (grad_s2 * (s + x * s * (1.0 - s))).astype(BF)
    back_ref[:, pl.ds(AT_GPRE, D_S)] = grad_pre
    grad_ffin = product_back(grad_pre, fs_ref[...])
    z = [ffu_ref[c] for c in range(3)]
    power = power_of(z) + 1.0
    inverse = lax.rsqrt(power)
    s = sigmoid(power * inverse)
    dot = z[0] * grad_v2[0] + z[1] * grad_v2[1] + z[2] * grad_v2[2]
    factor = dot * inverse * (s * (1.0 - s))
    grad_up = [(grad_v2[c] * s + z[c] * factor).astype(BF) for c in range(3)]
    h = [ffh_ref[c] for c in range(3)]
    factor = grad_ffin[:, D_S:] * lax.rsqrt(power_of(h) + 1.0)
    v1 = [v1_ref[c] for c in range(3)]
    scale = lax.rsqrt(jnp.mean(power_of(v1), axis=-1, keepdims=True) + 1e-05)
    grad_nv = []
    for c in range(3):
        back_ref[:, pl.ds(AT_GFU + c * D_V, D_V)] = grad_up[c]
        grad_h = (product_back(grad_up[c], fu_ref[...]) + factor * h[c]).astype(BF)
        back_ref[:, pl.ds(AT_GFH + c * D_V, D_V)] = grad_h
        grad_nv.append(grad_v2[c] + product_back(grad_h, fv_ref[...]))
    grad_ns = grad_s2 + grad_ffin[:, :D_S]
    hat, inverse = centre(s1_ref[...])
    grad_norm_gain = jnp.sum(grad_ns * hat, axis=0, keepdims=True)
    gsone_ref[...] = centre_back(hat, inverse, grad_ns * ng_ref[...])
    dot = grad_nv[0] * v1[0] + grad_nv[1] * v1[1] + grad_nv[2] * v1[2]
    dot = jnp.mean(dot, axis=-1, keepdims=True) * scale * scale
    for c in range(3):
        gvone_ref[c] = scale * (grad_nv[c] - v1[c] * dot)
    gains_ref[...] = jnp.zeros_like(gains_ref)
    gains_ref[0:1, :] = grad_norm_gain
    for p in range(shards):
        pair = slice(p // 2 * 128, p // 2 * 128 + 128)
        left = jnp.broadcast_to(grad_attn_gain[:, pair], (8, 128))
        right = jnp.broadcast_to(fgain_ref[:, pair], (8, 128))
        if p % 2 == 0:
            both = jnp.where(lower_half((8, 128)), left, swap_halves(right))
        else:
            both = jnp.where(lower_half((8, 128)), swap_halves(left), right)
        gains_ref[1:2, pl.ds(p * 128, 128)] = both[0:1]


def place():
    dp, space = lax.axis_index("dp"), lax.axis_index("space")
    return {"x": lax.rem(dp, 2), "y": dp // 2, "z": space // 2, "core": lax.rem(space, 2)}


def peer(way, shift=1):
    at = place()
    if way == "x":
        return {"dp": 2 * at["y"] + 1 - at["x"]}
    if way == "y":
        return {"dp": 2 * (1 - at["y"]) + at["x"]}
    if way == "diagonal":
        return {"dp": 2 * (1 - at["y"]) + 1 - at["x"]}
    if way == "core":
        return {"space": 2 * at["z"] + 1 - at["core"]}
    if way == "z":
        return {"space": 2 * lax.rem(at["z"] + shift, 4) + at["core"]}
    return {"space": lax.rem(lax.axis_index("space") + shift, lax.axis_size("space"))}


def greet(peers):
    barrier = pltpu.get_barrier_semaphore()
    for one in peers:
        pl.semaphore_signal(barrier, inc=1, device_id=one, device_id_type=MESH)
    pl.semaphore_wait(barrier, len(peers))


class Wires:
    def __init__(self, send_sem, recv_sem):
        self.send_sem, self.recv_sem, self.used = send_sem, recv_sem, 0

    def copy(self, source, target, to):
        n = self.used
        self.used += 1
        return pltpu.make_async_remote_copy(
            src_ref=source,
            dst_ref=target,
            send_sem=self.send_sem.at[n],
            recv_sem=self.recv_sem.at[n],
            device_id=to,
            device_id_type=MESH,
        )


def rows_at(ref, start, count):
    return ref.at[:, pl.ds(start, count), :]


def first_cut(wires, share_ref, got_ref):
    at = place()
    quarter = share_ref.shape[1] // 4
    return [
        wires.copy(rows_at(share_ref, (1 - at["x"]) * quarter, quarter), got_ref.at[0], peer("x")),
        wires.copy(
            rows_at(share_ref, (3 - at["y"]) * quarter, quarter), got_ref.at[1], peer("y")
        ),
    ]


def own_quarters(share_ref, own_ref, sems):
    at = place()
    quarter = share_ref.shape[1] // 4
    starts = (at["x"] * quarter, (2 + at["y"]) * quarter)
    return [
        pltpu.make_async_copy(rows_at(share_ref, start, quarter), own_ref.at[n], sems.at[n])
        for n, start in enumerate(starts)
    ]


def first_add(own_ref, got_ref, sum_ref):
    for n in range(2):
        sum_ref[n] = (own_ref[n].astype(F32) + got_ref[n].astype(F32)).astype(BF)


def first_add_whole(share_ref, got_ref, sum_ref):
    at = place()
    quarter = share_ref.shape[1] // 4
    for n, start in enumerate((at["x"] * quarter, (2 + at["y"]) * quarter)):
        own = share_ref[:, pl.ds(pl.multiple_of(start, 16), quarter), :]
        sum_ref[n] = (own.astype(F32) + got_ref[n].astype(F32)).astype(BF)


def second_cut(wires, sum_ref, got_ref):
    at = place()
    eighth = sum_ref.shape[2] // 2
    return [
        wires.copy(
            rows_at(sum_ref.at[0], (1 - at["y"]) * eighth, eighth), got_ref.at[0], peer("y")
        ),
        wires.copy(
            rows_at(sum_ref.at[1], (1 - at["x"]) * eighth, eighth), got_ref.at[1], peer("x")
        ),
    ]


def second_add(sum_ref, got_ref, out_ref, base=0):
    at = place()
    eighth = sum_ref.shape[2] // 2
    for n, start in enumerate((at["y"] * eighth, at["x"] * eighth)):
        own = sum_ref[n, :, pl.ds(pl.multiple_of(start, 16), eighth), :]
        out_ref[:, pl.ds(base + n * eighth, eighth), :] = (
            own.astype(F32) + got_ref[n].astype(F32)
        ).astype(BF)


def z_send(wires, part_ref, got_ref):
    at = place()
    return [
        wires.copy(
            part_ref.at[lax.rem(at["z"] + shift, 4)], got_ref.at[shift - 1], peer("z", shift)
        )
        for shift in (1, 2, 3)
    ]


def z_add(own, got_ref):
    total = own.astype(F32)
    for n in range(3):
        total = total + got_ref[n].astype(F32)
    return total.astype(BF)


def start_all(copies):
    for copy in copies:
        copy.start()
    return copies


def wait_all(copies):
    for copy in copies:
        copy.wait()


def sent_row(sent_ref, scr):
    spaces = sent_ref.shape[0]
    scr[...] = jnp.zeros_like(scr)
    scr[pl.ds(0, spaces), pl.ds(0, CAP)] = sent_ref[...].astype(F32)
    row = scr[0:1, :]
    for d in range(1, spaces):
        row = row + pltpu.roll(scr[d : d + 1, :], d * CAP, 1)
    return row


def pick_matrix(row, nodes):
    places = lax.broadcasted_iota(jnp.int32, (nodes, row.shape[1]), 0).astype(F32)
    return (places == row).astype(BF)


def prepare_kernel(
    ns_ref, nv_ref, sent_ref, vn_ref, we_ref, vout_ref, norms_ref, wnode_hbm,
    b_ref, p_ref, q_ref, ts_ref, tv_ref, vs_ref, vt_ref, vo_ref, mix_ref, wn_ref,
    wnode, row_scr, vt_scr, out_scr, in_scr, send_sem, recv_sem, load_sem,
):
    nodes = ns_ref.shape[0]
    table = ts_ref.shape[0]
    spaces = lax.axis_size("space")
    me = lax.axis_index("space")
    wires = Wires(send_sem, recv_sem)
    ring = [peer("group", shift) for shift in range(1, spaces)]
    load = pltpu.make_async_copy(wnode_hbm, wnode, load_sem)
    load.start()
    pick = pick_matrix(sent_row(sent_ref, row_scr), nodes)
    rows = lead_product(pick, ns_ref[...]).astype(BF)
    for d in range(spaces):
        out_scr[d, :, pl.ds(0, D_S)] = rows[d * CAP : (d + 1) * CAP]
    for c in range(3):
        rows = lead_product(pick, nv_ref[c]).astype(BF)
        for d in range(spaces):
            out_scr[d, :, pl.ds(D_S + c * D_V, D_V)] = rows[d * CAP : (d + 1) * CAP]
    greet(ring)
    copies = start_all(
        [
            wires.copy(out_scr.at[lax.rem(me + n + 1, spaces)], in_scr.at[me], ring[n])
            for n in range(spaces - 1)
        ]
    )
    in_scr[me] = out_scr[me]
    vs_ref[pl.ds(0, 512), :] = vn_ref[pl.ds(0, 512), :]
    vt_scr[...] = jnp.zeros_like(vt_scr)
    vt_scr[pl.ds(0, H_V + 1), :] = vn_ref[pl.ds(512, H_V + 1), :].astype(F32)
    row = lax.broadcasted_iota(jnp.int32, (H_P, D_V), 0)
    vt_ref[...] = jnp.where(row < H_V, pltpu.roll(vt_scr[...], H_P - 1, 0), 0.0).astype(BF)
    low = row[: H_P - 512]
    first = jnp.broadcast_to(vt_scr[0:1, :], low.shape)
    vs_ref[pl.ds(512, H_P - 512), :] = jnp.where(low == 0, first, 0.0).astype(BF)
    vo_ref[pl.ds(0, 512), :] = vout_ref[pl.ds(0, 512), :]
    first = jnp.broadcast_to(vout_ref[pl.ds(512, 1), :].astype(F32), low.shape)
    vo_ref[pl.ds(512, H_P - 512), :] = jnp.where(low == 0, first, 0.0).astype(BF)
    for c in range(3):
        q_ref[c] = product_back(nv_ref[c], vt_ref[...])
        p_ref[c, pl.ds(0, nodes), :] = product_back(nv_ref[c], vs_ref[...]).astype(BF)
        tv_ref[c, pl.ds(0, nodes), :] = nv_ref[c]
    ts_ref[pl.ds(0, nodes), :] = ns_ref[...]
    first = jnp.broadcast_to(norms_ref[pl.ds(512, 1), :].astype(F32), (16, D_S))
    row = lax.broadcasted_iota(jnp.int32, (16, D_S), 0)
    wn_ref[pl.ds(0, 512), :] = norms_ref[pl.ds(0, 512), :]
    wn_ref[pl.ds(512, 16), :] = jnp.where(row == 0, first, 0.0).astype(BF)
    wn_ref[pl.ds(528, D_E), :] = we_ref[...]
    wn_ref[pl.ds(528 + D_E, H_P - 528 - D_E), :] = jnp.zeros((H_P - 528 - D_E, D_S), BF)
    mix_ref[pl.ds(table, H_P), :] = wn_ref[...]
    load.wait()
    b_ref[...] = product(ns_ref[...], wnode[:, pl.ds(D_S, D_S)])
    mix_ref[pl.ds(0, nodes), :] = product(ns_ref[...], wnode[:, pl.ds(0, D_S)]).astype(BF)
    wait_all(copies)
    got = in_scr[...].reshape(spaces * CAP, D_S + 3 * D_V)
    ts_ref[pl.ds(nodes, table - nodes), :] = got[:, :D_S]
    mix_ref[pl.ds(nodes, table - nodes), :] = product(
        got[:, :D_S], wnode[:, pl.ds(0, D_S)]
    ).astype(BF)
    for c in range(3):
        rows = got[:, D_S + c * D_V : D_S + (c + 1) * D_V]
        tv_ref[c, pl.ds(nodes, table - nodes), :] = rows
        p_ref[c, pl.ds(nodes, table - nodes), :] = product_back(rows, vs_ref[...]).astype(BF)


def prepare(node_scalar, node_vector, sent, vec_node, w_edge, vec_out, w_norms, w_node):
    nodes = node_scalar.shape[0]
    spaces = sent.shape[0]
    table = nodes + spaces * CAP
    hbm = pl.BlockSpec(memory_space=pl.ANY)
    vmem = pl.BlockSpec(memory_space=pltpu.VMEM)
    outs = [
        ((nodes, D_S), F32),
        ((3, table, H_P), BF),
        ((3, nodes, H_P), F32),
        ((table, D_S), BF),
        ((3, table, D_V), BF),
        ((H_P, D_V), BF),
        ((H_P, D_V), BF),
        ((H_P, D_V), BF),
        ((table + H_P, D_S), BF),
        ((H_P, D_S), BF),
    ]
    blocks = (spaces, CAP, D_S + 3 * D_V)
    return pl.pallas_call(
        prepare_kernel,
        out_shape=[jax.ShapeDtypeStruct(shape, kind) for shape, kind in outs],
        in_specs=[vmem] * 7 + [hbm],
        out_specs=[vmem] * 10,
        scratch_shapes=[
            pltpu.VMEM(w_node.shape, BF),
            pltpu.VMEM((8, 128), F32),
            pltpu.VMEM((H_P, D_V), F32),
            pltpu.VMEM(blocks, BF),
            pltpu.VMEM(blocks, BF),
            pltpu.SemaphoreType.DMA((spaces - 1,)),
            pltpu.SemaphoreType.DMA((spaces - 1,)),
            pltpu.SemaphoreType.DMA,
        ],
        compiler_params=pltpu.CompilerParams(
            collective_id=3, has_side_effects=True, vmem_limit_bytes=VMEM_LIMIT
        ),
        name="prepare",
    )(node_scalar, node_vector, sent, vec_node, w_edge, vec_out, w_norms, w_node)


def middle_kernel(
    ns_ref, nv_ref, as_ref, av_ref, gains_in, fv_ref, fs_ref, fu_ref, we_ref, wq_ref, id_ref, cot_ref, wo_hbm, wu_hbm, wd_hbm, ts_hbm, ns_hbm,
    out_ref, gsone_ref, gvone_ref, gains_ref, m_ref, f_ref, tso_hbm, nso_hbm,
    s1, v1, ffh, ffp, ffu, v2, sz, fac_node, fac_node_o, heads_out, heads_in,
    probs, att, att_out, att_in, wo_ref, wu_ref, wd_ref, gatt, gatt_in, gs1, fgain,
    fac_feed, fac_feed_o, gs_scr, ghead, ghead_in, fac_back, fac_back_o,
    first, first_got, first_sum, first_got2, tall_scr, low_scr,
    send_sem, recv_sem, load_sem,
):
    spaces = lax.axis_size("space")
    quads = spaces // 2
    me = lax.axis_index("space")
    ng_ref = gains_in.at[:, pl.ds(0, D_S)]
    ag_ref = gains_in.at[:, pl.ds(D_S, D_MODEL)]
    fg_ref = gains_in.at[:, pl.ds(D_S + D_MODEL, D_MODEL)]
    wires = Wires(send_sem, recv_sem)
    ring = [peer("group", shift) for shift in range(1, spaces)]

    def exchange(source, target):
        return [
            wires.copy(source.at[lax.rem(me + n + 1, spaces)], target.at[me], ring[n])
            for n in range(spaces - 1)
        ]

    def keep(source, target):
        target[me] = source[me]

    loads = [
        pltpu.make_async_copy(source, target, load_sem.at[n])
        for n, (source, target) in enumerate(
            ((wo_hbm, wo_ref), (wu_hbm, wu_ref), (wd_hbm, wd_ref))
        )
    ]
    start_all(loads)
    greet(ring + [peer("x"), peer("y")])
    swaps = start_all(
        [wires.copy(ts_hbm, tso_hbm, peer("core")), wires.copy(ns_hbm, nso_hbm, peer("core"))]
    )
    node_forward_kernel(
        ns_ref, nv_ref, as_ref, av_ref, ng_ref, fv_ref, fs_ref, fu_ref, we_ref, ag_ref, wq_ref,
        s1, v1, ffh, ffp, ffu, v2, sz, fac_node, heads_out,
    )
    copies = start_all(exchange(heads_out, heads_in))
    swaps += start_all([wires.copy(fac_node, fac_node_o, peer("core"))])
    keep(heads_out, heads_in)
    wait_all(copies)
    attend_kernel(heads_in, id_ref, probs, att, att_out)
    copies = start_all(exchange(att_out, att_in))
    keep(att_out, att_in)
    wait_all(loads)
    wait_all(copies)
    feed_kernel(
        att_in, sz, wo_ref, fg_ref, wu_ref, wd_ref, cot_ref, out_ref, gatt, gs1, fgain, fac_feed
    )
    copies = start_all(exchange(gatt, gatt_in))
    feed_swap = start_all([wires.copy(fac_feed, fac_feed_o, peer("core"))])
    keep(gatt, gatt_in)
    wait_all(copies)
    attend_backward_kernel(heads_in, probs, att, gatt_in, ghead, gs_scr)
    copies = start_all(exchange(ghead, ghead_in))
    keep(ghead, ghead_in)
    wait_all(feed_swap)
    feed_grads_kernel(fac_feed, fac_feed_o, first)
    cuts = start_all(first_cut(wires, first, first_got))
    wait_all(copies)
    node_backward_kernel(
        ghead_in, gs1, s1, v1, ffh, ffp, ffu, v2, sz,
        ng_ref, fv_ref, fs_ref, fu_ref, we_ref, ag_ref, wq_ref, fgain,
        gsone_ref, gvone_ref, gains_ref, fac_back,
    )
    swaps += start_all([wires.copy(fac_back, fac_back_o, peer("core"))])
    wait_all(cuts)
    first_add_whole(first, first_got, first_sum)
    cuts = start_all(second_cut(wires, first_sum, first_got2))
    wait_all(swaps)
    node_grads_kernel(
        fac_node, fac_node_o, fac_back, fac_back_o, fac_feed, fac_feed_o, m_ref, tall_scr, low_scr
    )
    wait_all(cuts)
    second_add(first_sum, first_got2, f_ref)


def middle(vmem_operands, hbm_operands, table_s, node_scalar, quads):
    nodes = node_scalar.shape[0]
    spaces = 2 * quads
    count = spaces * nodes
    hbm = pl.BlockSpec(memory_space=pl.ANY)
    vmem = pl.BlockSpec(memory_space=pltpu.VMEM)
    operands = tuple(vmem_operands) + tuple(hbm_operands) + (table_s, node_scalar)
    bits = lambda *shape: pltpu.VMEM(shape, BF)
    wide = lambda *shape: pltpu.VMEM(shape, F32)
    packed = (spaces, nodes + nodes // 2, 128)
    small = (spaces, nodes // 2, 128)
    outs = [
        ((nodes, D_MODEL), BF),
        ((nodes, D_S), F32),
        ((3, nodes, D_V), F32),
        ((8, D_S), F32),
        ((quads, ROWS_M, 512), BF),
        ((quads, ROWS_F // 4, 512), BF),
        (table_s.shape, BF),
        (node_scalar.shape, BF),
    ]
    wires = 4 * (spaces - 1) + 9
    return pl.pallas_call(
        middle_kernel,
        out_shape=[jax.ShapeDtypeStruct(shape, kind) for shape, kind in outs],
        in_specs=[vmem] * len(vmem_operands) + [hbm] * (len(hbm_operands) + 2),
        out_specs=[vmem] * 6 + [hbm] * 2,
        scratch_shapes=[
            wide(nodes, D_S), wide(3, nodes, D_V), wide(3, nodes, D_V), wide(nodes, D_S),
            wide(3, nodes, D_V), wide(3, nodes, D_V), wide(nodes, D_MODEL),
            bits(nodes, FAC_NODE), bits(nodes, FAC_NODE), bits(*packed), bits(*packed),
            bits(count, count), wide(count, 128), bits(*small), bits(*small),
        ]
        + [bits(*one.shape) for one in hbm_operands]
        + [
            bits(*small), bits(*small), wide(nodes, D_MODEL), wide(1, D_MODEL),
            bits(nodes, FAC_FEED), bits(nodes, FAC_FEED), bits(count, count),
            bits(*packed), bits(*packed), bits(nodes, FAC_BACK), bits(nodes, FAC_BACK),
            bits(quads, ROWS_F, 512), bits(2, quads, ROWS_F // 4, 512),
            bits(2, quads, ROWS_F // 4, 512), bits(2, quads, ROWS_F // 8, 512),
            bits(D_S + D_V, 512), bits(D_V, 512),
            pltpu.SemaphoreType.DMA((wires,)),
            pltpu.SemaphoreType.DMA((wires,)),
            pltpu.SemaphoreType.DMA((len(hbm_operands),)),
        ],
        compiler_params=pltpu.CompilerParams(
            collective_id=0, has_side_effects=True, vmem_limit_bytes=VMEM_LIMIT
        ),
        name="middle",
    )(*operands)


def slot_rows(rows_scr, first_slot, nodes):
    return jnp.concatenate([rows_scr[pl.ds(first_slot + k, 1), :] for k in range(GROUP)], 1)


def one_hot_rows(rows_scr, first_slot, table, nodes):
    row = slot_rows(rows_scr, first_slot, nodes)
    return (lax.broadcasted_iota(jnp.int32, (table, row.shape[1]), 0).astype(F32) == row).astype(BF)


def keep_rows(ref, rows_scr):
    rows_scr[pl.ds(0, ref.shape[0]), :] = ref[...].astype(F32)


def scalar_backward_kernel(
    near_ref, lx_ref, ds_ref, gsone_ref, wn_ref, ts_hbm, ns_hbm, wnode_hbm, tso_hbm, nso_hbm,
    m_ref, f_ref,
    ratio_ref, pack_ref, rest_ref, gscal_ref, back_ref, m2_ref, ffin_ref,
    ga_ref, gw_ref, gb_ref, pre_scr, grads_scr, grads_got, mix_scr, mix_got, rest_scr, rest_got,
    m_own, m_got, m_sum, m_got2, f_own, f_got, ts_ref, ns_ref, wnode_ref, tso_ref, nso_ref,
    send_sem, recv_sem, load_sem, near_scr,
):
    nodes = gsone_ref.shape[0]
    table = ts_ref.shape[0]
    rows = GROUP * nodes
    quads = pack_ref.shape[0]
    step = pl.program_id(0)
    last = pl.num_programs(0) - 1
    wires = Wires(send_sem, recv_sem)
    f_copies = z_send(wires, f_ref, f_got)
    m_copies = first_cut(wires, m_ref, m_got)
    pairs = (
        (ts_hbm, ts_ref), (ns_hbm, ns_ref), (wnode_hbm, wnode_ref), (tso_hbm, tso_ref),
        (nso_hbm, nso_ref), (f_ref.at[place()["z"]], f_own),
    )
    loads = [
        pltpu.make_async_copy(source, target, load_sem.at[2 + n])
        for n, (source, target) in enumerate(pairs)
    ]
    m_loads = own_quarters(m_ref, m_own, load_sem)
    m_copies2 = second_cut(wires, m_sum, m_got2)
    pair_copies = [
        wires.copy(source, target, peer("core"))
        for source, target in ((grads_scr, grads_got), (mix_scr, mix_got), (rest_scr, rest_got))
    ]

    @pl.when(step == 0)
    def _():
        greet([peer("x"), peer("y"), peer("core")] + [peer("z", shift) for shift in (1, 2, 3)])
        start_all(m_copies)
        start_all(f_copies)
        start_all(m_loads)
        start_all(loads)
        keep_rows(near_ref, near_scr)
        for ref in (ga_ref, gw_ref, gb_ref):
            ref[...] = jnp.zeros_like(ref)

    @pl.when(step == 4)
    def _():
        wait_all(m_loads)
        wait_all(m_copies)
        first_add(m_own, m_got, m_sum)
        start_all(m_copies2)

    for start in range(0, D_S, 256):
        cols = pl.ds(start, 256)
        for first in range(0, nodes, ROW_TILE):
            part = pl.ds(first, ROW_TILE)
            share = gsone_ref[part, cols] * (1.0 / NEIGH)
            acc = None
            for k in range(GROUP):
                g = (ds_ref[k, part, cols].astype(F32) * share).astype(BF)
                pre_scr[pl.ds(k * nodes + first, ROW_TILE), cols] = g
                g = g.astype(F32)
                acc = g if acc is None else acc + g
            gb_ref[part, cols] += acc
    one_hot = one_hot_rows(near_scr, step * GROUP, table, nodes)
    grad_pre = pre_scr[...]
    ga_ref[...] += product(one_hot, grad_pre)
    lx = lx_ref[...].reshape(rows, H_P)
    gw_ref[...] += lead_product(lx, grad_pre)
    for start, width in LANE_BLOCKS:
        cols = pl.ds(start, width)
        grad_length = product_back(grad_pre, wn_ref[cols, :])
        for first in range(0, nodes, ROW_TILE):
            part = pl.ds(first, ROW_TILE)
            for k in range(GROUP):
                at = k * nodes + first
                ratio = grad_length[at : at + ROW_TILE] * pl.reciprocal(
                    lx_ref[k, part, cols].astype(F32), approx=True
                )
                if start == 512:
                    lane = lax.broadcasted_iota(jnp.int32, (ROW_TILE, width), 1)
                    ratio = jnp.where(lane == 0, ratio, 0.0)
                ratio_ref[k, part, cols] = ratio.astype(BF)

    @pl.when(step == last)
    def _():
        core = place()["core"]
        grads_scr[pl.ds(0, table), :] = ga_ref[...].astype(BF)
        grads_scr[pl.ds(table, nodes), :] = gb_ref[...].astype(BF)
        for z in range(quads):
            away = pl.ds(pl.multiple_of((2 * z + 1 - core) * 128, 128), 128)
            for r in range(4):
                mix_scr[z, :, pl.ds(r * 128, 128)] = gw_ref[pl.ds(r * 128, 128), away].astype(BF)
            rest_scr[z] = gw_ref[pl.ds(512, 64), away].astype(BF)
        start_all(pair_copies)
        wait_all(loads)
        ga = grads_scr[pl.ds(0, table), :]
        gb = grads_scr[pl.ds(table, nodes), :]
        projected = product_back(ga, wnode_ref[:, pl.ds(0, D_S)])
        gscal_ref[...] = (
            gsone_ref[...] + product_back(gb, wnode_ref[:, pl.ds(D_S, D_S)]) + projected[:nodes]
        )
        back_ref[...] = projected[nodes:].astype(BF)
        wait_all(pair_copies)
        gao = grads_got[pl.ds(0, table), :]
        gbo = grads_got[pl.ds(table, nodes), :]
        for z in range(quads):
            own = pl.ds(pl.multiple_of((2 * z + core) * 128, 128), 128)
            for half, (left, right, lefto, righto) in enumerate(
                ((ts_ref, ga, tso_ref, gao), (ns_ref, gb, nso_ref, gbo))
            ):
                block = lead_product(left[:, own], right) + lead_product(lefto[:, own], righto)
                block = block.astype(BF)
                for n in range(2):
                    pack_ref[z, pl.ds((2 * half + n) * 128, 128), :] = block[
                        :, n * 512 : (n + 1) * 512
                    ]
            for r in range(4):
                lanes = pl.ds(r * 128, 128)
                pack_ref[z, pl.ds(512, 128), lanes] = (
                    gw_ref[pl.ds(r * 128, 128), own] + mix_got[z, :, lanes].astype(F32)
                ).astype(BF)
            rest_ref[z] = gw_ref[pl.ds(512, 64), own] + rest_got[z].astype(F32)
        wait_all(m_copies2)
        second_add(m_sum, m_got2, m2_ref)
        wait_all(f_copies)
        ffin_ref[...] = z_add(f_own[...], f_got)


def scalar_backward(near, lx, dsilu, gsone, wn, ts, ns, w_node, ts_other, ns_other, m, f):
    nodes = gsone.shape[0]
    table = ts.shape[0]
    quads = m.shape[0]
    rows = GROUP * nodes
    once = pl.Buffered(1)
    whole = lambda shape: pl.BlockSpec(shape, lambda g: (0,) * len(shape), pipeline_mode=once)
    slots = lambda *shape: pl.BlockSpec((GROUP,) + shape, lambda g: (g,) + (0,) * len(shape))
    steps = lambda *shape: pl.BlockSpec((1,) + shape, lambda g: (g,) + (0,) * len(shape))
    outs = [
        ((quads, ROWS_S, 512), BF),
        ((quads, 64, 128), F32),
        ((nodes, D_S), F32),
        ((table - nodes, D_S), BF),
        ((quads, ROWS_M // 4, 512), BF),
        ((ROWS_F // 4, 512), BF),
    ]
    return pl.pallas_call(
        scalar_backward_kernel,
        grid=(NEIGH // GROUP,),
        in_specs=[whole(near.shape), slots(nodes, H_P), slots(nodes, D_S)]
        + [whole(one.shape) for one in (gsone, wn)]
        + [pl.BlockSpec(memory_space=pl.ANY)] * 7,
        out_specs=[slots(nodes, H_P)] + [whole(shape) for shape, kind in outs],
        out_shape=[jax.ShapeDtypeStruct((NEIGH, nodes, H_P), BF)]
        + [jax.ShapeDtypeStruct(shape, kind) for shape, kind in outs],
        scratch_shapes=[
            pltpu.VMEM((table, D_S), F32),
            pltpu.VMEM((H_P, D_S), F32),
            pltpu.VMEM((nodes, D_S), F32),
            pltpu.VMEM((rows, D_S), BF),
            pltpu.VMEM((table + nodes, D_S), BF),
            pltpu.VMEM((table + nodes, D_S), BF),
            pltpu.VMEM((quads, 128, 512), BF),
            pltpu.VMEM((quads, 128, 512), BF),
            pltpu.VMEM((quads, 64, 128), BF),
            pltpu.VMEM((quads, 64, 128), BF),
            pltpu.VMEM((2, quads, ROWS_M // 4, 512), BF),
            pltpu.VMEM((2, quads, ROWS_M // 4, 512), BF),
            pltpu.VMEM((2, quads, ROWS_M // 4, 512), BF),
            pltpu.VMEM((2, quads, ROWS_M // 8, 512), BF),
            pltpu.VMEM((ROWS_F // 4, 512), BF),
            pltpu.VMEM((3, ROWS_F // 4, 512), BF),
        ]
        + [pltpu.VMEM(one.shape, BF) for one in (ts, ns, w_node, ts_other, ns_other)]
        + [
            pltpu.SemaphoreType.DMA((10,)),
            pltpu.SemaphoreType.DMA((10,)),
            pltpu.SemaphoreType.DMA((8,)),
            pltpu.VMEM((32, 128), F32),
        ],
        compiler_params=pltpu.CompilerParams(
            collective_id=1, has_side_effects=True, vmem_limit_bytes=VMEM_LIMIT
        ),
        name="scalar_backward",
    )(near, lx, dsilu, gsone, wn, ts, ns, w_node, ts_other, ns_other, m, f)


def vector_backward_kernel(
    near_ref, ev_ref, h_ref, ratio_ref, z_ref, gvone_ref, vo_ref, tv_ref,
    nv_ref, vs_ref, vt_ref, rest_ref, gains_ref, s_ref, m_ref, f_ref, backs_ref,
    plane_ref, gvec_ref, got_ref, gp_ref, gq_ref, gvo_ref, up_scr, gh_scr,
    s_own, s_got, s_sum, s_got2, s_part, s_gotz, m_own, m_gotz, t_scr, t_got, t_half, t_got1, t_sum, t_got2,
    t_part, t_gotz, back_scr, fin_scr, own_sem, send_sem, recv_sem, load_sem, near_scr, ev_scr,
):
    nodes = gvone_ref.shape[1]
    table = tv_ref.shape[1]
    rows = GROUP * nodes
    spaces = lax.axis_size("space")
    quads = spaces // 2
    step = pl.program_id(0)
    last = pl.num_programs(0) - 1
    at = place()
    me = lax.axis_index("space")
    mine = 2 * at["x"] + at["y"]
    wires = Wires(send_sem, recv_sem)
    early, late = ROWS_F // 4 + ROWS_M // 4, ROWS_S // 4 + ROWS_T // 4
    ring = [peer("group", shift) for shift in range(1, spaces)]
    plane = [peer("x"), peer("y"), peer("diagonal")]
    s_copies = first_cut(wires, s_ref, s_got)
    s_copies2 = second_cut(wires, s_sum, s_got2)
    s_copiesz = z_send(wires, s_part, s_gotz)
    m_copiesz = z_send(wires, m_ref, m_gotz)
    early_rows, late_rows = pl.ds(0, early), pl.ds(early, late)
    early_copies = [
        wires.copy(fin_scr.at[early_rows, :], plane_ref.at[mine, early_rows, :], to) for to in plane
    ]
    late_copies = [
        wires.copy(fin_scr.at[late_rows, :], plane_ref.at[mine, late_rows, :], to) for to in plane
    ]
    back_scalar, back_vector = pl.ds(0, D_S), pl.ds(D_S, 3 * D_V)
    scalar_copies = [
        wires.copy(
            backs_ref.at[pl.ds(lax.rem(me + n + 1, spaces) * CAP, CAP), :],
            got_ref.at[me, :, back_scalar],
            ring[n],
        )
        for n in range(spaces - 1)
    ]
    back_copies = [
        wires.copy(
            back_scr.at[lax.rem(me + n + 1, spaces)], got_ref.at[me, :, back_vector], ring[n]
        )
        for n in range(spaces - 1)
    ]
    s_loads = own_quarters(s_ref, s_own, load_sem)
    m_load = pltpu.make_async_copy(m_ref.at[at["z"]], m_own, load_sem.at[2])
    f_load = pltpu.make_async_copy(f_ref, fin_scr.at[pl.ds(0, ROWS_F // 4), :], load_sem.at[3])
    own_scalar = pltpu.make_async_copy(
        backs_ref.at[pl.ds(me * CAP, CAP), :], got_ref.at[me, :, back_scalar], load_sem.at[4]
    )
    t_pair = [wires.copy(t_scr.at[:, 1 - at["core"]], t_got, peer("core"))]
    t_copies = first_cut(wires, t_half, t_got1)
    t_copies2 = second_cut(wires, t_sum, t_got2)
    t_copiesz = z_send(wires, t_part, t_gotz)

    @pl.when(step == 0)
    def _():
        greet(ring + plane)
        start_all(s_copies)
        start_all(m_copiesz)
        start_all(s_loads + [m_load, f_load, own_scalar])
        keep_rows(near_ref, near_scr)
        for c in range(3):
            keep_rows(ev_ref.at[c], ev_scr.at[c])
        for ref in (gp_ref, gq_ref, gvo_ref):
            ref[...] = jnp.zeros_like(ref)

    @pl.when(step == 3)
    def _():
        wait_all(s_loads)
        wait_all(s_copies)
        first_add(s_own, s_got, s_sum)
        start_all(s_copies2)
        start_all(scalar_copies)

    @pl.when(step == 4)
    def _():
        wait_all([m_load, f_load])
        wait_all(m_copiesz)
        fin_scr[pl.ds(ROWS_F // 4, ROWS_M // 4), :] = z_add(m_own[...], m_gotz)
        start_all(early_copies)

    @pl.when(step == last)
    def _():
        wait_all(s_copies2)
        second_add(s_sum, s_got2, s_part)
        start_all(s_copiesz)

    for first in range(0, nodes, ROW_TILE):
        part = pl.ds(first, ROW_TILE)
        share = [gvone_ref[c, part, :] * (1.0 / NEIGH) for c in range(3)]
        for k in range(GROUP):
            z = [z_ref[k, c, part, :].astype(F32) for c in range(3)]
            power = power_of(z) + 1.0
            inverse = lax.rsqrt(power)
            s = sigmoid(power * inverse)
            dot = z[0] * share[0] + z[1] * share[1] + z[2] * share[2]
            factor = dot * inverse * (s * (1.0 - s))
            for c in range(3):
                up_scr[c, pl.ds(k * nodes + first, ROW_TILE), :] = (
                    share[c] * s + z[c] * factor
                ).astype(BF)
    for start, width in LANE_BLOCKS:
        cols = pl.ds(start, width)
        grad_direct = [product_back(up_scr[c], vo_ref[cols, :]) for c in range(3)]
        for first in range(0, nodes, ROW_TILE):
            part = pl.ds(first, ROW_TILE)
            acc = [None] * 3
            for k in range(GROUP):
                row = k * nodes + first
                ratio = ratio_ref[k, part, cols].astype(F32)
                for c in range(3):
                    g = grad_direct[c][row : row + ROW_TILE] + ratio * h_ref[
                        k, c, part, cols
                    ].astype(F32)
                    gh_scr[c, pl.ds(row, ROW_TILE), cols] = g.astype(BF)
                    acc[c] = g if acc[c] is None else acc[c] + g
            for c in range(3):
                gq_ref[c, part, cols] += acc[c]
    one_hot = one_hot_rows(near_scr, step * GROUP, table, nodes)
    for c in range(3):
        evr = jnp.broadcast_to(slot_rows(ev_scr.at[c], step * GROUP, nodes), (16, rows))
        lead = jnp.concatenate([one_hot, evr.astype(BF)], axis=0)
        gp_ref[c] += product(lead, gh_scr[c])
        gvo_ref[...] += lead_product(up_scr[c], h_ref[:, c, :, :].reshape(rows, H_P))

    @pl.when(step == last)
    def _():
        tall = D_V // spaces
        gp = [gp_ref[c, pl.ds(0, table), :].astype(BF) for c in range(3)]
        gq = [gq_ref[c].astype(BF) for c in range(3)]
        for c in range(3):
            projected = product(gp[c], vs_ref[...])
            gvec_ref[c] = gvone_ref[c] + product(gq[c], vt_ref[...]) + projected[:nodes]
            for d in range(spaces):
                back_scr[d, :, pl.ds(c * D_V, D_V)] = projected[
                    nodes + d * CAP : nodes + (d + 1) * CAP
                ].astype(BF)
        start_all(back_copies)
        own = pltpu.make_async_copy(
            back_scr.at[me], got_ref.at[me, :, back_vector], load_sem.at[5]
        )
        own.start()
        grads = []
        for lead_ref, right in ((tv_ref, gp), (nv_ref, gq)):
            total = None
            for c in range(3):
                one = lead_product(lead_ref[c], right[c])
                total = one if total is None else total + one
            grads.append(total)
        grads.append(gvo_ref[...])
        lane = lax.broadcasted_iota(jnp.int32, (D_V, 128), 1)
        tails = jnp.zeros((D_V, 128), F32)
        for n, grad in enumerate(grads):
            for p in range(spaces):
                t_scr[p // 2, p % 2, pl.ds(n * tall, tall), :] = grad[
                    p * tall : (p + 1) * tall, :512
                ].astype(BF)
            tails = tails + jnp.where(
                lane == n, jnp.broadcast_to(grad[:, 512:513], (D_V, 128)), 0.0
            )
        tails = tails.astype(BF)
        vedge = gp_ref[0, pl.ds(table, 8), :] + gp_ref[1, pl.ds(table, 8), :]
        vedge = vedge + gp_ref[2, pl.ds(table, 8), :]
        row = lax.broadcasted_iota(jnp.int32, (tall, 128), 0)
        below = pl.ds(3 * tall, tall)
        for p in range(spaces):
            rest = jnp.where(at["core"] == p % 2, rest_ref[p // 2], 0.0)
            t_scr[p // 2, p % 2, below, pl.ds(0, 128)] = tails[p * tall : (p + 1) * tall]
            t_scr[p // 2, p % 2, below, pl.ds(128, 128)] = rest[16 : 16 + tall].astype(BF)
            extra = jnp.where(row == 0, jnp.broadcast_to(rest[0:1], (tall, 128)), 0.0)
            for n in range(5):
                piece = jnp.broadcast_to(vedge[0:1, n * 128 : (n + 1) * 128], (tall, 128))
                extra = jnp.where(row == 1 + n, piece, extra)
            for n in range(2):
                piece = jnp.broadcast_to(
                    gains_ref[n : n + 1, p * 128 : (p + 1) * 128], (tall, 128)
                )
                extra = jnp.where(row == 6 + n, piece, extra)
            t_scr[p // 2, p % 2, below, pl.ds(256, 128)] = extra.astype(BF)
            t_scr[p // 2, p % 2, below, pl.ds(384, 128)] = jnp.zeros((tall, 128), BF)
        start_all(t_pair)
        wait_all(t_pair)
        t_half[...] = (t_scr[:, at["core"]].astype(F32) + t_got[...].astype(F32)).astype(BF)
        start_all(t_copies)
        wait_all(t_copies)
        first_add_whole(t_half, t_got1, t_sum)
        start_all(t_copies2)
        wait_all(t_copies2)
        second_add(t_sum, t_got2, t_part)
        start_all(t_copiesz)
        wait_all(s_copiesz)
        fin_scr[pl.ds(early, ROWS_S // 4), :] = z_add(s_part[at["z"]], s_gotz)
        wait_all(t_copiesz)
        fin_scr[pl.ds(early + ROWS_S // 4, ROWS_T // 4), :] = z_add(t_part[at["z"]], t_gotz)
        start_all(late_copies)
        own.wait()
        own_scalar.wait()
        wait_all(scalar_copies)
        own_plane = pltpu.make_async_copy(fin_scr, plane_ref.at[mine], own_sem)
        own_plane.start()
        own_plane.wait()
        wait_all(back_copies)
        wait_all(early_copies)
        wait_all(late_copies)


def vector_backward(
    near, ev, hidden, ratio, update, gvone, vout, tv, nv, vs, vt, rest, gains,
    s, m, f, back,
):
    nodes = gvone.shape[1]
    table = tv.shape[1]
    quads = s.shape[0]
    spaces = 2 * quads
    rows = GROUP * nodes
    once = pl.Buffered(1)
    whole = lambda shape: pl.BlockSpec(shape, lambda g: (0,) * len(shape), pipeline_mode=once)
    slots = lambda *shape: pl.BlockSpec((GROUP,) + shape, lambda g: (g,) + (0,) * len(shape))
    steps = lambda *shape: pl.BlockSpec((1,) + shape, lambda g: (g,) + (0,) * len(shape))
    outs = [
        ((4, (ROWS_F + ROWS_M + ROWS_S + ROWS_T) // 4, 512), BF),
        ((3, nodes, D_V), F32),
        ((spaces, CAP, D_S + 3 * D_V), BF),
    ]
    bits = lambda *shape: pltpu.VMEM(shape, BF)
    return pl.pallas_call(
        vector_backward_kernel,
        grid=(NEIGH // GROUP,),
        in_specs=[
            whole(near.shape),
            whole(ev.shape),
            slots(3, nodes, H_P),
            slots(nodes, H_P),
            slots(3, nodes, D_V),
        ]
        + [whole(one.shape) for one in (gvone, vout, tv, nv, vs, vt, rest, gains)]
        + [pl.BlockSpec(memory_space=pl.ANY)] * 4,
        out_specs=[
            pl.BlockSpec(memory_space=pl.ANY),
            whole(outs[1][0]),
            pl.BlockSpec(memory_space=pl.ANY),
        ],
        out_shape=[jax.ShapeDtypeStruct(shape, kind) for shape, kind in outs],
        scratch_shapes=[
            pltpu.VMEM((3, table + 16, H_P), F32),
            pltpu.VMEM((3, nodes, H_P), F32),
            pltpu.VMEM((D_V, H_P), F32),
            bits(3, rows, D_V),
            bits(3, rows, H_P),
            bits(2, quads, ROWS_S // 4, 512),
            bits(2, quads, ROWS_S // 4, 512),
            bits(2, quads, ROWS_S // 4, 512),
            bits(2, quads, ROWS_S // 8, 512),
            bits(quads, ROWS_S // 4, 512),
            bits(3, ROWS_S // 4, 512),
            bits(ROWS_M // 4, 512),
            bits(3, ROWS_M // 4, 512),
            bits(quads, 2, ROWS_T, 512),
            bits(quads, ROWS_T, 512),
            bits(quads, ROWS_T, 512),
            bits(2, quads, ROWS_T // 4, 512),
            bits(2, quads, ROWS_T // 4, 512),
            bits(2, quads, ROWS_T // 8, 512),
            bits(quads, ROWS_T // 4, 512),
            bits(3, ROWS_T // 4, 512),
            bits(spaces, CAP, 3 * D_V),
            bits((ROWS_F + ROWS_M + ROWS_S + ROWS_T) // 4, 512),
            pltpu.SemaphoreType.DMA,
            pltpu.SemaphoreType.DMA((38,)),
            pltpu.SemaphoreType.DMA((38,)),
            pltpu.SemaphoreType.DMA((6,)),
            pltpu.VMEM((32, 128), F32),
            pltpu.VMEM((3, 32, 128), F32),
        ],
        compiler_params=pltpu.CompilerParams(
            collective_id=2, has_side_effects=True, vmem_limit_bytes=VMEM_LIMIT
        ),
        name="vector_backward",
    )(
        near, ev, hidden, ratio, update, gvone, vout, tv, nv, vs, vt, rest, gains,
        s, m, f, back,
    )


def finish_kernel(
    plane_ref, got_ref, sent_ref, gscal_ref, gvec_ref,
    gs_ref, gv_ref, node_ref, edge_ref, norms_ref, vnode_ref, vedge_ref, vout_ref, ffv_ref, ffs_ref,
    ffu_ref, embed_ref, qkv_ref, out_ref, up_ref, down_ref, gains_ref, row_scr, sent_scr,
):
    base = 0
    for rows in (ROWS_F, ROWS_M, ROWS_S, ROWS_T):
        eighth = rows // 8
        for half, order in enumerate(((0, 1, 2, 3), (0, 2, 1, 3))):
            for n, q in enumerate(order):
                row_scr[pl.ds(4 * base + (4 * half + n) * eighth, eighth), :] = plane_ref[
                    q, pl.ds(base + half * eighth, eighth), :
                ]
        base += rows // 4

    def take(start, rows, lane=0, width=512):
        return row_scr[pl.ds(start, rows), pl.ds(lane, width)].astype(F32)

    at = 0
    down_ref[...] = take(at, 256)
    for n in range(4):
        up_ref[:, pl.ds(n * 512, 512)] = take(at + 256 + n * 64, 64)
    at = ROWS_F
    for n in range(3):
        qkv_ref[:, pl.ds(n * 512, 512)] = take(at + n * 64, 64)
    out_ref[...] = take(at + 192, 64)
    embed_ref[...] = take(at + 256, 160)
    for n in range(2):
        ffs_ref[:, pl.ds(n * 512, 512)] = take(at + 416 + n * 160, 160)
    ffv_ref[...] = take(at + 736, 32, 0, 256)
    ffu_ref[...] = take(at + 736, 32, 256, 256)
    at += ROWS_M
    for n in range(4):
        node_ref[:, pl.ds(n * 512, 512)] = take(at + n * 128, 128)
        norms_ref[pl.ds(n * 128, 128), :] = take(at + 512, 128, n * 128, 128)
    at += ROWS_S
    tails = take(at + 96, 32, 0, 128)
    edge_ref[...] = take(at + 96, 32, 128, 128)
    extra = take(at + 96, 32, 256, 128)
    norms_ref[pl.ds(512, 1), :] = extra[0:1]
    for n in range(5):
        width = min(128, H_V - n * 128)
        vedge_ref[:, pl.ds(n * 128, width)] = extra[1 + n : 2 + n, :width]
    gains_ref[...] = extra[0:8]
    vnode_ref[:, pl.ds(0, 512)] = take(at, 32)
    wide = jnp.concatenate([take(at + 32, 32), jnp.zeros((32, 128), F32)], 1)
    lane = lax.broadcasted_iota(jnp.int32, (32, 640), 1)
    wide = pltpu.roll(wide, 1, 1)
    wide = jnp.where(lane == 0, tails[:, 0:1], wide)
    wide = jnp.where(lane == 513, tails[:, 1:2], wide)
    vnode_ref[:, pl.ds(512, 514)] = wide[:, :514]
    flat = jnp.concatenate([take(at + 64, 32), jnp.zeros((96, 512), F32)], 0)
    vout_ref[pl.ds(0, 512), :] = jnp.transpose(flat)[:, :32]
    flat = jnp.concatenate([tails, jnp.zeros((96, 128), F32)], 0)
    vout_ref[pl.ds(512, 1), :] = jnp.transpose(flat)[2:3, :32]
    nodes = gscal_ref.shape[0]
    slots = got_ref.shape[0] * got_ref.shape[1]
    got = got_ref[...].reshape(slots, D_S + 3 * D_V)
    pick = pick_matrix(sent_row(sent_ref, sent_scr), nodes)
    added = product(pick, got)
    gs_ref[...] = (gscal_ref[...] + added[:, :D_S]).astype(BF)
    for c in range(3):
        gv_ref[c] = (
            gvec_ref[c] + added[:, D_S + c * D_V : D_S + (c + 1) * D_V]
        ).astype(BF)


def finish(plane, got, sent, gscal, gvec):
    nodes = gscal.shape[0]
    outs = [
        ((nodes, D_S), BF),
        ((3, nodes, D_V), BF),
        ((128, 2048), F32),
        ((32, 128), F32),
        ((513, 128), F32),
        ((32, 1026), F32),
        ((1, 513), F32),
        ((513, 32), F32),
        ((32, 256), F32),
        ((160, 1024), F32),
        ((32, 256), F32),
        ((160, 512), F32),
        ((64, 1536), F32),
        ((64, 512), F32),
        ((64, 2048), F32),
        ((256, 512), F32),
        ((8, 128), F32),
    ]
    return pl.pallas_call(
        finish_kernel,
        out_shape=[jax.ShapeDtypeStruct(shape, kind) for shape, kind in outs],
        scratch_shapes=[
            pltpu.VMEM((ROWS_F + ROWS_M + ROWS_S + ROWS_T, 512), BF),
            pltpu.VMEM((8, 128), F32),
        ],
        compiler_params=pltpu.CompilerParams(vmem_limit_bytes=VMEM_LIMIT),
        name="finish",
    )(plane, got, sent, gscal, gvec)


def pad_to(values, size, axis):
    pads = [(0, 0)] * values.ndim
    pads[axis] = (0, size - values.shape[axis])
    return jnp.pad(values, pads)


def fold(blocks, width=512):
    shards, rows, columns = blocks.shape
    parts = columns // width
    return jnp.moveaxis(blocks.reshape(shards, rows, parts, width), 2, 1).reshape(
        shards, parts * rows, width
    )


def unfold(rows_in, rows, columns, width=512):
    parts = columns // width
    return jnp.moveaxis(rows_in.reshape(parts, rows, width), 0, 1).reshape(rows, columns)


def body(
    node_scalar, node_vector, edge_scalar, edge_vector, neighbours, send_rows, complex_id, cotangent,
    w_node, w_edge, w_norms, vec_node, vec_edge, vec_out, norm_gain, ff_vec, ff_scalar, ff_up,
    w_embed, attn_gain, w_qkv, w_out, ffn_gain, w_up, w_down,
):
    local_rows = node_scalar.shape[0]
    spaces = lax.axis_size("space")
    extra_rows = spaces * CAP
    table_count = local_rows + extra_rows
    all_nodes = complex_id.shape[0]
    steps = NEIGH // GROUP

    if spaces == HEADS and lax.axis_size("dp") == 4 and local_rows == 128:
        quads = spaces // 2
        sent = send_rows[0]
        near = neighbours.T
        ev = edge_vector.reshape(3, local_rows, NEIGH).transpose(0, 2, 1).astype(F32)
        gain_row = jnp.concatenate(
            [norm_gain, attn_gain, ffn_gain, vec_edge[0], jnp.zeros((H_P - H_V,), BF)]
        )
        gain_row = gain_row.astype(F32)[None]
        (
            b_target, p_source, q_target, table_s, table_v, vec_source, vec_target, vout, mix, wn_mix,
        ) = prepare(
            node_scalar, node_vector, sent, vec_node.T, w_edge, vec_out, w_norms, w_node
        )
        agg_s, agg_v, hidden, lx, dsilu, update = message(
            near, edge_scalar.T, ev, mix, b_target, p_source, q_target, gain_row, vout
        )
        stream_out, gsone, gvone, gains, middle_share, first_share, table_o, node_o = middle(
            (
                node_scalar, node_vector, agg_s, agg_v, gain_row, ff_vec, ff_scalar, ff_up,
                w_embed, w_qkv, complex_id[None], cotangent,
            ),
            (w_out, w_up, w_down), table_s, node_scalar, quads,
        )
        ratio, second_share, rest, gscal, back_s, middle_part, first_part = scalar_backward(
            near, lx, dsilu, gsone, wn_mix, table_s, node_scalar, w_node, table_o, node_o,
            middle_share, first_share,
        )
        plane, gvec, got = vector_backward(
            near, ev, hidden, ratio, update, gvone, vout, table_v, node_vector,
            vec_source, vec_target, rest, gains, second_share, middle_part, first_part, back_s,
        )
        (
            grad_scalar, grad_vector, out_node, out_edge, out_norms, out_vnode, out_vedge, out_vout,
            out_ffv, out_ffs, out_ffu, out_embed, out_qkv, out_out, out_up, out_down, rows,
        ) = finish(plane, got, sent, gscal, gvec)
        return (
            stream_out, grad_scalar, grad_vector, out_node, out_edge, out_norms, out_vnode,
            out_vedge, out_vout, rows[6], out_ffv, out_ffs, out_ffu, out_embed, rows[7, :64],
            out_qkv, out_out, rows[7, 64:], out_up, out_down,
        )

    sent_index = send_rows[0].reshape(-1)
    sent_live = sent_index >= 0
    pick = sent_index[:, None] == jnp.arange(local_rows, dtype=jnp.int32)[None, :]
    pick = pick.astype(BF)
    flat_nodes = jnp.concatenate([node_scalar] + [node_vector[c] for c in range(3)], 1)
    outgoing = product(pick, flat_nodes).astype(BF).reshape(spaces, CAP, D_S + 3 * D_V)
    incoming = lax.all_to_all(outgoing, "space", split_axis=0, concat_axis=0, tiled=True)
    incoming = incoming.reshape(extra_rows, D_S + 3 * D_V)
    table_s = jnp.concatenate([node_scalar, incoming[:, :D_S]], 0)
    table_v = jnp.stack(
        [
            jnp.concatenate(
                [node_vector[c], incoming[:, D_S + c * D_V : D_S + (c + 1) * D_V]], 0
            )
            for c in range(3)
        ]
    )
    vec_source = pad_to(vec_node[:, :H_V], H_P, 1)
    vec_target = pad_to(vec_node[:, H_V:], H_P, 1)
    a_source = product(table_s, w_node[:, :D_S]).astype(BF)
    b_target = product(node_scalar, w_node[:, D_S:])
    p_source = product(table_v, vec_source).astype(BF)
    q_target = product(node_vector, vec_target)
    ve_row = pad_to(vec_edge.astype(F32), H_P, 1)
    vout = pad_to(vec_out, H_P, 0)
    wn_mix = pad_to(jnp.concatenate([w_norms, w_edge], 0), H_P, 0)
    mix = jnp.concatenate([a_source, wn_mix], 0)

    near = neighbours.T
    near_col = near[:, :, None]
    near_row = near.reshape(steps, 1, GROUP * local_rows)
    es_k = edge_scalar.reshape(local_rows, NEIGH, D_E).transpose(1, 0, 2)
    es_pad = jnp.pad(es_k, ((0, 0), (0, 0), (1, 128 - 1 - D_E)))
    ev_k = edge_vector.reshape(3, local_rows, NEIGH)
    ev_col = ev_k.transpose(2, 1, 0).astype(F32)
    ev_row = ev_k.transpose(2, 0, 1).reshape(steps, GROUP, 3, local_rows)
    ev_row = ev_row.transpose(0, 2, 1, 3).reshape(steps, 3, GROUP * local_rows)

    agg_s, agg_v, hidden, lx, dsilu, update = edge_forward(
        near_col, es_pad, ev_col, mix, b_target, p_source, q_target, ve_row, vout
    )

    scalar_one = node_scalar.astype(F32) + agg_s
    vector_one = node_vector.astype(F32) + agg_v
    gain_norm = norm_gain.astype(F32)
    normed_s = layer_norm(scalar_one, gain_norm)
    normed_v = vector_norm(vector_one)
    normed_vr = normed_v.astype(BF)
    ff_hidden = product(normed_vr, ff_vec)
    ff_hidden_r = ff_hidden.astype(BF)
    ff_length = length_plus(ff_hidden)
    ff_input = jnp.concatenate([normed_s.astype(BF), ff_length.astype(BF)], -1)
    ff_preact = product(ff_input, ff_scalar)
    ff_update = product(ff_hidden_r, ff_up)
    scalar_two = normed_s + jax.nn.silu(ff_preact)
    vector_two = normed_v + vector_gate(ff_update)
    embed_input = jnp.concatenate([scalar_two.astype(BF), length_plus(vector_two).astype(BF)], -1)
    stream_zero = product(embed_input, w_embed)
    gain_attn = attn_gain.astype(F32)
    attn_in = layer_norm(stream_zero, gain_attn).astype(BF)
    qkv = product(attn_in, w_qkv).astype(BF)
    queries = qkv[:, :D_MODEL]
    keys_own = qkv[:, D_MODEL : 2 * D_MODEL]
    values_own = qkv[:, 2 * D_MODEL :]
    full_qkv = lax.all_gather(qkv, "space", axis=0, tiled=True)
    heads = lambda values: values.reshape(values.shape[0], HEADS, HEAD_DIM)
    full_queries = heads(full_qkv[:, :D_MODEL])
    full_keys = heads(full_qkv[:, D_MODEL : 2 * D_MODEL])
    full_values = heads(full_qkv[:, 2 * D_MODEL :])
    position = lax.axis_index("space")
    own_ids = lax.dynamic_slice_in_dim(complex_id, position * local_rows, local_rows, 0)
    same = own_ids[:, None] == complex_id[None, :]
    score_scale = HEAD_DIM ** (-0.5)
    scores = jnp.einsum("qhd,khd->hqk", heads(queries), full_keys, preferred_element_type=F32)
    scores = jnp.where(same[None], scores * score_scale, -1000000000.0)
    row_peak = jnp.max(scores, axis=-1, keepdims=True)
    shifted = jnp.exp(scores - row_peak)
    totals = jnp.sum(shifted, axis=-1, keepdims=True)
    probs = shifted / totals
    log_total = row_peak + jnp.log(totals)
    attended = jnp.einsum(
        "hqk,khd->qhd", probs.astype(BF), full_values, preferred_element_type=F32
    ).reshape(local_rows, D_MODEL)
    attended_r = attended.astype(BF)
    stream_one = stream_zero + product(attended_r, w_out)
    gain_ffn = ffn_gain.astype(F32)
    ffn_in = layer_norm(stream_one, gain_ffn).astype(BF)
    hidden_up = product(ffn_in, w_up)
    gelu_r = gelu_exact(hidden_up).astype(BF)
    stream_out = (stream_one + product(gelu_r, w_down)).astype(BF)
    grad_w_down = product_lead(gelu_r, cotangent)
    grad_gelu = product_back(cotangent, w_down)
    grad_up_r = pullback(gelu_exact, hidden_up, grad_gelu).astype(BF)
    grad_w_up = product_lead(ffn_in, grad_up_r)
    grad_ffn_in = product_back(grad_up_r, w_up)
    unused, ffn_pull = jax.vjp(layer_norm, stream_one, gain_ffn)
    grad_stream_ln, grad_ffn_gain = ffn_pull(grad_ffn_in)
    grad_stream_one = cotangent.astype(F32) + grad_stream_ln
    grad_branch = grad_stream_one.astype(BF)
    grad_w_out = product_lead(attended_r, grad_branch)
    grad_attended = product_back(grad_branch, w_out).astype(BF)
    row_dots = jnp.sum(heads(grad_attended).astype(F32) * heads(attended), axis=-1).T

    def halves(values):
        high = lax.reduce_precision(values, exponent_bits=8, mantissa_bits=7)
        return [high.astype(BF), (values - high).astype(BF)]

    numbers = jnp.concatenate(halves(log_total[:, :, 0]) + halves(row_dots), 0)
    packed = jnp.concatenate([grad_attended, pad_to(numbers.T, 128, 1)], 1)
    full_packed = lax.all_gather(packed, "space", axis=0, tiled=True)
    full_grad = heads(full_packed[:, :D_MODEL])
    numbers = full_packed[:, D_MODEL : D_MODEL + 4 * HEADS].astype(F32).T
    full_log = numbers[:HEADS] + numbers[HEADS : 2 * HEADS]
    full_dots = numbers[2 * HEADS : 3 * HEADS] + numbers[3 * HEADS :]

    grad_probs = jnp.einsum(
        "qhd,khd->hqk", heads(grad_attended), full_values, preferred_element_type=F32
    )
    grad_scores = (probs * (grad_probs - row_dots[:, :, None])).astype(BF)
    grad_query = jnp.einsum("hqk,khd->qhd", grad_scores, full_keys, preferred_element_type=F32)
    own_scores = jnp.einsum(
        "khd,qhd->hkq", heads(keys_own), full_queries, preferred_element_type=F32
    )
    own_scores = jnp.where(same[None], own_scores * score_scale, -1000000000.0)
    own_probs = jnp.exp(own_scores - full_log[:, None, :])
    own_grad_probs = jnp.einsum(
        "khd,qhd->hkq", heads(values_own), full_grad, preferred_element_type=F32
    )
    own_grad_scores = (own_probs * (own_grad_probs - full_dots[:, None, :])).astype(BF)
    grad_keys = jnp.einsum(
        "hkq,qhd->khd", own_grad_scores, full_queries, preferred_element_type=F32
    )
    grad_values = jnp.einsum(
        "hkq,qhd->khd", own_probs.astype(BF), full_grad, preferred_element_type=F32
    )
    flat = lambda values: values.reshape(local_rows, D_MODEL)
    grad_qkv = jnp.concatenate(
        [flat(grad_query) * score_scale, flat(grad_keys) * score_scale, flat(grad_values)], -1
    ).astype(BF)
    grad_w_qkv = product_lead(attn_in, grad_qkv)
    grad_attn_in = product_back(grad_qkv, w_qkv)
    unused, attn_pull = jax.vjp(layer_norm, stream_zero, gain_attn)
    grad_zero_ln, grad_attn_gain = attn_pull(grad_attn_in)
    grad_stream_r = (grad_stream_one + grad_zero_ln).astype(BF)
    grad_w_embed = product_lead(embed_input, grad_stream_r)
    grad_embed_in = product_back(grad_stream_r, w_embed)
    grad_vector_two = pullback(length_plus, vector_two, grad_embed_in[:, D_S:])
    grad_ff_pre = pullback(jax.nn.silu, ff_preact, grad_embed_in[:, :D_S]).astype(BF)
    grad_ff_scalar = product_lead(ff_input, grad_ff_pre)
    grad_ff_input = product_back(grad_ff_pre, ff_scalar)
    grad_ff_update = pullback(vector_gate, ff_update, grad_vector_two).astype(BF)
    grad_ff_up = product_lead(ff_hidden_r, grad_ff_update)
    grad_ff_hidden = (
        product_back(grad_ff_update, ff_up)
        + pullback(length_plus, ff_hidden, grad_ff_input[:, D_S:])
    ).astype(BF)
    grad_ff_vec = product_lead(normed_vr, grad_ff_hidden)
    grad_normed_v = grad_vector_two + product_back(grad_ff_hidden, ff_vec)
    grad_normed_s = grad_embed_in[:, :D_S] + grad_ff_input[:, :D_S]
    unused, norm_pull = jax.vjp(layer_norm, scalar_one, gain_norm)
    grad_scalar_one, grad_norm_gain = norm_pull(grad_normed_s)
    grad_vector_one = pullback(vector_norm, vector_one, grad_normed_v)

    shard = lambda grad: grad.astype(BF).reshape((spaces, grad.shape[0] // spaces) + grad.shape[1:])
    gains = jnp.concatenate(
        [shard(grad_norm_gain), shard(grad_attn_gain), shard(grad_ffn_gain)], 1
    )
    gains = pad_to(pad_to(gains, 512, 1)[:, None, :], 16, 1)
    first_share = jnp.concatenate(
        [
            shard(grad_w_down),
            fold(shard(grad_w_up)),
            fold(shard(grad_w_qkv)),
            shard(grad_w_out),
            shard(grad_w_embed),
            fold(shard(grad_ff_scalar)),
            jnp.concatenate([shard(grad_ff_vec), shard(grad_ff_up)], 2),
            gains,
        ],
        1,
    )
    first_sum = lax.psum_scatter(first_share, "space", scatter_dimension=0, tiled=False)
    first_sum = lax.psum(first_sum, "dp").astype(F32)

    grad_a, grad_mix, grad_b, grad_p, grad_q, grad_vout = edge_backward(
        near_row, ev_col, ev_row, hidden, lx, dsilu, update,
        grad_scalar_one * (1.0 / NEIGH), grad_vector_one * (1.0 / NEIGH), wn_mix, vout, table_count,
    )
    grad_vedge = jnp.sum(grad_p[:, table_count], 0)[:H_V]
    grad_vec_edge = lax.psum(grad_vedge[None, :], ("dp", "space"))
    grad_a_r = grad_a.astype(BF)
    grad_p_r = grad_p[:, :table_count].astype(BF)
    grad_b_r = grad_b.astype(BF)
    grad_q_r = grad_q.astype(BF)
    grad_node_a = product_lead(table_s, grad_a_r)
    grad_node_b = product_lead(node_scalar, grad_b_r)
    grad_vec_a = product_lead(table_v, grad_p_r)
    grad_vec_b = product_lead(node_vector, grad_q_r)
    grad_table_scalar = product_back(grad_a_r, w_node[:, :D_S])
    grad_table_vector = product_back(grad_p_r, vec_source)
    grad_scalar = (
        grad_scalar_one + product_back(grad_b_r, w_node[:, D_S:]) + grad_table_scalar[:local_rows]
    )
    grad_vector = (
        grad_vector_one + product_back(grad_q_r, vec_target) + grad_table_vector[:, :local_rows]
    )
    back = jnp.concatenate(
        [grad_table_scalar[local_rows:]] + [grad_table_vector[c, local_rows:] for c in range(3)], 1
    )
    back = back.astype(BF).reshape(spaces, CAP, D_S + 3 * D_V)
    got = lax.all_to_all(back, "space", split_axis=0, concat_axis=0, tiled=True)
    got = got.reshape(extra_rows, D_S + 3 * D_V)
    got = jnp.where(sent_live[:, None], got, 0)
    added = lax.dot_general(pick, got, (((0,), (0,)), ((), ())), preferred_element_type=F32)
    grad_scalar = grad_scalar + added[:, :D_S]
    grad_vector = grad_vector + jnp.moveaxis(
        added[:, D_S:].reshape(local_rows, 3, D_V), 1, 0
    )

    columns = lambda grad: jnp.moveaxis(
        grad.reshape(grad.shape[0], spaces, grad.shape[1] // spaces), 1, 0
    )
    mix_block = columns(grad_mix.astype(BF))
    mix_width = D_S // spaces
    mix_rows = H_P * mix_width // 512
    second_share = jnp.concatenate(
        [
            fold(shard(grad_node_a)),
            fold(shard(grad_node_b)),
            mix_block.reshape(spaces, mix_rows, 512),
            shard(grad_vec_a)[:, :, :512],
            shard(grad_vec_b)[:, :, :512],
            shard(grad_vout)[:, :, :512],
            jnp.concatenate(
                [
                    shard(grad_vec_a)[:, :, 512:],
                    shard(grad_vec_b)[:, :, 512:],
                    shard(grad_vout)[:, :, 512:],
                    jnp.zeros((spaces, D_V // spaces, 128), BF),
                ],
                2,
            ),
        ],
        1,
    )
    second_sum = lax.psum_scatter(second_share, "space", scatter_dimension=0, tiled=False)
    second_sum = lax.psum(second_sum, "dp").astype(F32)

    def taker(rows_in):
        at = [0]

        def take(rows, cols, blocks=1):
            part = rows_in[at[0] : at[0] + rows * blocks]
            at[0] += rows * blocks
            return unfold(part, rows, cols) if blocks > 1 else part

        return take

    take = taker(first_sum)
    out_down = take(grad_w_down.shape[0] // spaces, 512)
    out_up = take(D_MODEL // spaces, 2048, 4)
    out_qkv = take(D_MODEL // spaces, 1536, 3)
    out_out = take(D_MODEL // spaces, 512)
    out_embed = take((D_S + D_V) // spaces, 512)
    out_ffs = take((D_S + D_V) // spaces, 1024, 2)
    both = take(D_V // spaces, 512)
    out_ffv, out_ffu = both[:, :D_V], both[:, D_V:]
    gain_row = take(16, 512)[0]
    cuts = [D_S // spaces, D_MODEL // spaces, D_MODEL // spaces]
    out_gn = gain_row[: cuts[0]]
    out_ga = gain_row[cuts[0] : cuts[0] + cuts[1]]
    out_gf = gain_row[cuts[0] + cuts[1] : sum(cuts)]
    take = taker(second_sum)
    node_a = take(D_S // spaces, 1024, 2)
    node_b = take(D_S // spaces, 1024, 2)
    mixed = take(mix_rows, 512).reshape(H_P, mix_width)
    vec_a = take(D_V // spaces, 512)
    vec_b = take(D_V // spaces, 512)
    vout_t = take(D_V // spaces, 512)
    tails = take(D_V // spaces, 512)
    out_vec_node = jnp.concatenate([vec_a, tails[:, :1], vec_b, tails[:, 128:129]], 1)
    out_vec_out = jnp.concatenate([vout_t, tails[:, 256:257]], 1).T
    return (
        stream_out,
        grad_scalar.astype(BF),
        grad_vector.astype(BF),
        jnp.concatenate([node_a, node_b], 1),
        mixed[H_V : H_V + D_E],
        mixed[:H_V],
        out_vec_node,
        grad_vec_edge,
        out_vec_out,
        out_gn,
        out_ffv,
        out_ffs,
        out_ffu,
        out_embed,
        out_ga,
        out_qkv,
        out_out,
        out_gf,
        out_up,
        out_down,
    )


def solution(mesh):
    rows = P(("dp", "space"), None)
    component = P(None, ("dp", "space"), None)
    return jax.shard_map(
        body,
        mesh=mesh,
        in_specs=(
            rows, component, rows, P(None, ("dp", "space")), rows,
            P(("dp", "space"), None, None), P("dp"), rows,
        ) + (P(),) * 17,
        out_specs=(
            rows, rows, component, P("space", None), P(None, "space"), P(None, "space"),
            P("space", None), P(), P(None, "space"), P("space"), P("space", None),
            P("space", None), P("space", None), P("space", None), P("space"), P("space", None),
            P("space", None), P("space"), P("space", None), P("space", None),
        ),
        check_vma=False,
    )
```

profile of v0, /device:TPU:0, one launch (start us, length us, event | category | flops | bytes accessed | tf_op | source)
XLA Modules:
  0.0 232.7 jit_solution(8444964648225515153)
XLA Ops:
  0.7 0.7 concatenate.17
  1.3 0.7 concatenate.18
  2.0 0.7 concatenate.16
  2.7 0.8 concatenate.19
  3.5 0.6 convert_element_type.20.ve_ref.gains_in
  4.1 1.0 reshape.103
  5.1 0.7 copy.46
  5.8 18.3 %prepare.1 = (f32[128,1024]{1,0:T(8,128)}, bf16[3,256,640]{2,1,0:T(8,128)(2,1)}, f32[3,128,640]{2,1,0:T(8,128)}, bf16[256,1024]{1,0:T(8,128)(2,1)}, bf16[3,256,2...) custom-call(bf16[128,1024]{1,0:T(8,128)(2,1)} %ns_hbm.3, ...), custom_call_target="tpu_custom_call" | custom-call | tf_op jit(solution)/shard_map/prepare/pallas_call | solution.py:1080
  24.1 35.3 %message.1 = (f32[128,1024]{1,0:T(8,128)}, f32[3,128,256]{2,1,0:T(8,128)}, bf16[30,3,128,640]{3,2,1,0:T(8,128)(2,1)}, bf16[30,128,640]{2,1,0:T(8,128)(2,1)}, bf1...) custom-call(s32[30,128]{1,0:T(8,128)} %bitcast.16, bf16[960,128]{1,0:T(8,128)(2,1)} %bitcast.15, ...), custom_call_target="tpu_custom_call" | custom-call | tf_op jit(solution)/shard_map/message/pallas_call | solution.py:305
  59.5 61.8 %middle.1 = (bf16[128,512]{1,0:T(8,128)(2,1)}, f32[128,1024]{1,0:T(8,128)}, f32[3,128,256]{2,1,0:T(8,128)}, f32[8,1024]{1,0:T(8,128)}, bf16[4,768,512]{2,1,0:T(8...) custom-call(bf16[128,1024]{1,0:T(8,128)(2,1)} %ns_hbm.3, ...), custom_call_target="tpu_custom_call" | custom-call | tf_op jit(solution)/shard_map/middle/pallas_call | solution.py:1206
  121.3 35.3 %scalar_backward.1 = (bf16[30,128,640]{2,1,0:T(8,128)(2,1)}, bf16[4,640,512]{2,1,0:T(8,128)(2,1)}, f32[4,64,128]{2,1,0:T(8,128)}, f32[128,1024]{1,0:T(8,128)}, b...) custom-call(s32[30,128]{1,0:T(8,128)} %bitcast.17, ...), custom_call_target="tpu_custom_call" | custom-call | tf_op jit(solution)/shard_map/scalar_backward/pallas_call | solution.py:1393
  156.6 66.6 %vector_backward.1 = (bf16[4,512,512]{2,1,0:T(8,128)(2,1)}, f32[3,128,256]{2,1,0:T(8,128)}, bf16[8,16,1792]{2,1,0:T(8,128)(2,1)}) custom-call(s32[30,128]{1,0:T(8,128)} %bitcast.18, f32[3,30,128]{2,1,0:T(8,128)} %bitcast.14, bf16[30,3,128,640]{3,2,1,0:T(8,128)(2,1)} %get-tuple-element.80.h_ref, bf16[30,128,640]{2,1,0:T(8,128)(2,1)} %get-tuple-element.89.ratio_ref, ...), custom_call_target="tpu_custom_call" | custom-call | tf_op jit(solution)/shard_map/vector_backward/pallas_call | solution.py:1663
  223.2 0.0 copy-start
  223.2 4.6 %finish.1 = (bf16[128,1024]{1,0:T(8,128)(2,1)}, bf16[3,128,256]{2,1,0:T(8,128)(2,1)}, f32[128,2048]{1,0:T(8,128)}, f32[32,128]{1,0:T(8,128)}, f32[513,128]{1,0:T...) custom-call(bf16[4,512,512]{2,1,0:T(8,128)(2,1)} %get-tuple-element., ...), custom_call_target="tpu_custom_call" | custom-call | tf_op jit(solution)/shard_map/finish/pallas_call | solution.py:1810
  227.8 1.2 slice_bitcast_fusion.2
  229.0 1.3 slice_bitcast_fusion
  230.3 1.7 copy.47
  232.0 0.0 copy-done
  232.0 0.7 copy.49
  (1 shorter events, 0.0 us)
Async XLA Ops:
  223.2 8.9 %copy-start = (bf16[128,512]{1,0:T(8,128)(2,1)S(1)}, bf16[128,512]{1,0:T(8,128)(2,1)}, u32[]{:S(2)}) copy-start(bf16[128,512]{1,0:T(8,128)(2,1)} %get-tuple-element.184) | copy-start | bytes 393220
where the time goes:
time: 233 us
  Pallas kernels  222 us (95%)
  local copies, waits for them, and re-layouts  9.46 us (4%)
    pallas_call x1, Pallas kernels, vector_backward(): pl.pallas_call(vector_backward_kernel, grid=(NEIGH // GROUP,), in_specs=[...  66.6 us
    pallas_call x1, Pallas kernels, middle(): pl.pallas_call(middle_kernel, out_shape=[jax.ShapeDtypeStruct(shape, kind...  61.8 us
    pallas_call x1, Pallas kernels, message(): pl.pallas_call(message_kernel, grid=(NEIGH // GROUP,), in_specs=[whole(ne...  35.3 us
    pallas_call x1, Pallas kernels, scalar_backward(): pl.pallas_call(scalar_backward_kernel, grid=(NEIGH // GROUP,), in_specs=[...  35.3 us
    pallas_call x1, Pallas kernels, prepare(): pl.pallas_call(prepare_kernel, out_shape=[jax.ShapeDtypeStruct(shape, kin...  18.3 us

commit v1 on v0

--- a/solution.py
+++ b/solution.py
@@ -469,7 +469,8 @@
 AT_AIN, AT_EMB, AT_FFIN, AT_FFH, AT_NV, FAC_NODE = 0, 512, 1792, 3072, 3840, 4608
 AT_GELU, AT_GUP, AT_FIN, AT_COT, AT_ATT, AT_GBR, FAC_FEED = 0, 2048, 4096, 4608, 5120, 5632, 6144
 AT_GQKV, AT_STREAM, AT_GPRE, AT_GFU, AT_GFH, FAC_BACK = 0, 1536, 2048, 3072, 3840, 4608
-ROWS_F, ROWS_M, ROWS_S, ROWS_T = 512, 768, 640, 128
+ROWS_F, ROWS_A, ROWS_N, ROWS_S, ROWS_B, ROWS_V = ALL_ROWS = (512, 256, 512, 256, 384, 128)
+ROWS_E = ROWS_F // 4
 
 def full_block(shape):
     return pl.BlockSpec(shape, lambda: (0,) * len(shape))
@@ -526,7 +527,7 @@
 
 def node_forward_kernel(
     ns_ref, nv_ref, as_ref, av_ref, ng_ref, fv_ref, fs_ref, fu_ref, we_ref, ag_ref, wq_ref,
-    s1_ref, v1_ref, ffh_ref, ffp_ref, ffu_ref, v2_ref, sz_ref, fac_ref, out_ref,
+    s1_ref, v1_ref, ffh_ref, ffp_ref, ffu_ref, v2_ref, sz_ref, fac_ref, out_ref, with_keys,
 ):
     nodes = ns_ref.shape[0]
     s1 = ns_ref[...].astype(F32) + as_ref[...]
@@ -563,22 +564,20 @@
     hat, unused = centre(sz)
     attn_in = (hat * ag_ref[...]).astype(BF)
     fac_ref[:, pl.ds(AT_AIN, D_MODEL)] = attn_in
-    q, k, v = [product(attn_in, wq_ref[:, pl.ds(n * D_MODEL, D_MODEL)]) for n in range(3)]
-    pack_heads(q, k, v, out_ref)
-
-
-def pack_heads(q, k, v, out_ref):
-    nodes = q.shape[0]
+    q, k = [product(attn_in, wq_ref[:, pl.ds(n * D_MODEL, D_MODEL)]) for n in range(2)]
     side = lower_half((nodes, 128))
     for pair in range(HEADS // 2):
         cols = slice(pair * 128, pair * 128 + 128)
-        qp, kp, vp = q[:, cols], k[:, cols], v[:, cols]
+        qp, kp = q[:, cols], k[:, cols]
         even = jnp.where(side, qp, swap_halves(kp))
         odd = jnp.where(side, swap_halves(qp), kp)
         for n, block in enumerate((even, odd)):
-            head = 2 * pair + n
-            out_ref[head, pl.ds(0, nodes), :] = block.astype(BF)
-            out_ref[head, pl.ds(nodes, nodes // 2), :] = pack_tall(vp, n == 1).astype(BF)
+            out_ref[2 * pair + n, pl.ds(0, nodes), :] = block.astype(BF)
+    with_keys()
+    v = product(attn_in, wq_ref[:, pl.ds(2 * D_MODEL, D_MODEL)])
+    for head in range(HEADS):
+        tile = v[:, head // 2 * 128 : head // 2 * 128 + 128]
+        out_ref[head, pl.ds(nodes, nodes // 2), :] = pack_tall(tile, head % 2 == 1).astype(BF)
 
 
 def split_heads(x_ref, nodes):
@@ -586,17 +585,21 @@
     both = x_ref[:, pl.ds(0, nodes), :].reshape(spaces * nodes, 128).astype(F32)
     queries = jnp.where(lower_half(both.shape), both, 0.0).astype(BF)
     keys = swap_halves(both).astype(BF)
-    values = jnp.concatenate(
+    return queries, keys
+
+
+def split_values(x_ref, nodes):
+    spaces = x_ref.shape[0]
+    return jnp.concatenate(
         [unpack_tall(x_ref[d, pl.ds(nodes, nodes // 2), :].astype(F32)) for d in range(spaces)], 0
     ).astype(BF)
-    return queries, keys, values
-
-
-def attend_kernel(x_ref, id_ref, probs_ref, att_ref, out_ref):
+
+
+def attend_kernel(x_ref, id_ref, probs_ref, att_ref, out_ref, with_probs):
     spaces = x_ref.shape[0]
     nodes = x_ref.shape[1] * 2 // 3
     count = spaces * nodes
-    queries, keys, values = split_heads(x_ref, nodes)
+    queries, keys = split_heads(x_ref, nodes)
     row_ids = id_ref[...]
     column_ids = jnp.transpose(jnp.broadcast_to(row_ids, (8, count)))[:, 0:1]
     block = 2 * nodes
@@ -607,23 +610,32 @@
         shifted = jnp.exp(scores - jnp.max(scores, axis=-1, keepdims=True))
         probs = (shifted / jnp.sum(shifted, axis=-1, keepdims=True)).astype(BF)
         probs_ref[pl.ds(first, block), :] = probs
-        att = product(probs, values)
+    with_probs()
+    values = split_values(x_ref, nodes)
+    for first in range(0, count, block):
+        att = product(probs_ref[pl.ds(first, block), :], values)
         att_ref[pl.ds(first, block), :] = att
         for n in range(block // nodes):
             tile = att[n * nodes : (n + 1) * nodes]
             out_ref[first // nodes + n] = pack_tall(tile, False).astype(BF)
 
 
-def attend_backward_kernel(x_ref, probs_ref, att_ref, g_ref, out_ref, gs_scr):
+def attend_backward_kernel(x_ref, probs_ref, att_ref, g_ref, out_ref, gs_scr, with_values):
     spaces = x_ref.shape[0]
     nodes = x_ref.shape[1] * 2 // 3
     count = spaces * nodes
-    queries, keys, values = split_heads(x_ref, nodes)
+    queries, keys = split_heads(x_ref, nodes)
+    values = split_values(x_ref, nodes)
     grad = jnp.concatenate(
         [unpack_tall(g_ref[d].astype(F32)) for d in range(spaces)], 0
     )
     dots = jnp.sum(grad * att_ref[...], axis=-1, keepdims=True)
     grad = grad.astype(BF)
+    grad_values = jnp.transpose(lead_product(grad, probs_ref[...]))
+    for d in range(spaces):
+        tile = grad_values[d * nodes : (d + 1) * nodes]
+        out_ref[d, pl.ds(nodes, nodes // 2), :] = pack_tall(tile, False).astype(BF)
+    with_values()
     block = 2 * nodes
     scale = HEAD_DIM ** (-0.5)
     grad_queries = []
@@ -635,14 +647,12 @@
         grad_queries.append(product(grad_scores, keys))
     grad_queries = jnp.concatenate(grad_queries, 0) * scale
     grad_keys = jnp.transpose(lead_product(queries, gs_scr[...])) * scale
-    grad_values = jnp.transpose(lead_product(grad, probs_ref[...]))
     side = lower_half((nodes, 128))
     for d in range(spaces):
         rows = slice(d * nodes, (d + 1) * nodes)
         out_ref[d, pl.ds(0, nodes), :] = jnp.where(
             side, grad_queries[rows], swap_halves(grad_keys[rows])
         ).astype(BF)
-        out_ref[d, pl.ds(nodes, nodes // 2), :] = pack_tall(grad_values[rows], False).astype(BF)
 
 
 def merge_heads(block_ref, first, half):
@@ -656,7 +666,7 @@
 
 def feed_kernel(
     att_ref, sz_ref, wo_ref, fg_ref, wu_ref, wd_ref, cot_ref,
-    out_ref, gatt_ref, gs1_ref, ggain_ref, fac_ref,
+    out_ref, gatt_ref, gs1_ref, ggain_ref, fac_ref, with_up,
 ):
     nodes = sz_ref.shape[0]
     att = merge_heads(att_ref, 0, nodes // 2).astype(BF)
@@ -677,6 +687,7 @@
         fac_ref[:, pl.ds(AT_GUP + start, 512)] = (
             product_back(cot, wd_ref[cols, :]) * slope
         ).astype(BF)
+    with_up()
     out_ref[...] = (
         stream_one + product(fac_ref[:, pl.ds(AT_GELU, ffn)], wd_ref[...])
     ).astype(BF)
@@ -725,9 +736,7 @@
             pack_ref[z, pl.ds(256 + n * 64, 64), :] = block[z * 64 : (z + 1) * 64]
 
 
-def node_grads_kernel(
-    node_ref, node_other, back_ref, back_other, feed_ref, feed_other, pack_ref, tall_scr, low_scr
-):
+def attention_grads(node_ref, node_other, back_ref, back_other, feed_ref, feed_other, pack_ref):
     quads = pack_ref.shape[0]
     core = lax.rem(lax.axis_index("space"), 2)
     left = core_columns(both_rows(node_ref, node_other, AT_AIN, D_MODEL), core)
@@ -744,6 +753,11 @@
         block = lead_product(one, two).astype(BF)
         for z in range(quads):
             pack_ref[z, pl.ds(n * 64, 64), :] = block[z * 64 : (z + 1) * 64]
+
+
+def node_grads(node_ref, node_other, back_ref, back_other, pack_ref, tall_scr, low_scr):
+    quads = pack_ref.shape[0]
+    core = lax.rem(lax.axis_index("space"), 2)
     emb = both_rows(node_ref, node_other, AT_EMB, D_S + D_V)
     ffin = both_rows(node_ref, node_other, AT_FFIN, D_S + D_V)
     rights = [(emb, back_ref, back_other, AT_STREAM)]
@@ -752,7 +766,7 @@
         tall_scr[...] = lead_product(one, both_rows(own, other, start, 512)).astype(BF)
         for z in range(quads):
             rows = pl.ds(pl.multiple_of((2 * z + core) * 160, 32), 160)
-            pack_ref[z, pl.ds(256 + n * 160, 160), :] = tall_scr[rows, :]
+            pack_ref[z, pl.ds(n * 160, 160), :] = tall_scr[rows, :]
     vec = up = None
     for c in range(3):
         one = lead_product(
@@ -768,13 +782,13 @@
     low_scr[...] = jnp.concatenate([vec, up], 1).astype(BF)
     for z in range(quads):
         rows = pl.ds(pl.multiple_of((2 * z + core) * 32, 32), 32)
-        pack_ref[z, pl.ds(736, 32), :] = low_scr[rows, :]
+        pack_ref[z, pl.ds(480, 32), :] = low_scr[rows, :]
 
 
 def node_backward_kernel(
     gq_ref, gs1_ref, s1_ref, v1_ref, ffh_ref, ffp_ref, ffu_ref, v2_ref,
     sz_ref, ng_ref, fv_ref, fs_ref, fu_ref, we_ref, ag_ref, wq_ref, fgain_ref,
-    gsone_ref, gvone_ref, gains_ref, back_ref,
+    gsone_ref, gvone_ref, gains_ref, back_ref, with_qkv,
 ):
     nodes = gs1_ref.shape[0]
     shards = gq_ref.shape[0]
@@ -789,6 +803,7 @@
     grads.append(merge_heads(gq_ref, nodes, nodes // 2).astype(BF))
     for n in range(3):
         back_ref[:, pl.ds(AT_GQKV + n * D_MODEL, D_MODEL)] = grads[n]
+    with_qkv()
     grad_in = product_back(back_ref[:, pl.ds(AT_GQKV, 3 * D_MODEL)], wq_ref[...])
     hat, inverse = centre(sz_ref[...])
     grad_attn_gain = jnp.sum(grad_in * hat, axis=0, keepdims=True)
@@ -843,6 +858,8 @@
         gains_ref[1:2, pl.ds(p * 128, 128)] = both[0:1]
 
 
+BACKWARD_LIMIT = 62 * 1024 * 1024
+
 def place():
     dp, space = lax.axis_index("dp"), lax.axis_index("space")
     return {"x": lax.rem(dp, 2), "y": dp // 2, "z": space // 2, "core": lax.rem(space, 2)}
@@ -907,7 +924,7 @@
     quarter = share_ref.shape[1] // 4
     starts = (at["x"] * quarter, (2 + at["y"]) * quarter)
     return [
-        pltpu.make_async_copy(rows_at(share_ref, start, quarter), own_ref.at[n], sems.at[n])
+        pltpu.make_async_copy(rows_at(share_ref, start, quarter), own_ref.at[n], sems[n])
         for n, start in enumerate(starts)
     ]
 
@@ -963,6 +980,35 @@
     for n in range(3):
         total = total + got_ref[n].astype(F32)
     return total.astype(BF)
+
+
+class Share:
+    def __init__(self, wires, packed, own, refs, loads=()):
+        self.packed, self.own, self.loads = packed, own, list(loads)
+        self.got, self.sum, self.got2, self.part, self.gotz = refs
+        self.copies = first_cut(wires, packed, self.got)
+        self.copies2 = second_cut(wires, self.sum, self.got2)
+        self.copiesz = z_send(wires, self.part, self.gotz)
+
+    def start(self):
+        start_all(self.loads + self.copies)
+
+    def cut(self):
+        wait_all(self.loads + self.copies)
+        if self.own is None:
+            first_add_whole(self.packed, self.got, self.sum)
+        else:
+            first_add(self.own, self.got, self.sum)
+        start_all(self.copies2)
+
+    def spread(self):
+        wait_all(self.copies2)
+        second_add(self.sum, self.got2, self.part)
+        start_all(self.copiesz)
+
+    def total(self):
+        wait_all(self.copiesz)
+        return z_add(self.part[place()["z"]], self.gotz)
 
 
 def start_all(copies):
@@ -1101,7 +1147,7 @@
 
 def middle_kernel(
     ns_ref, nv_ref, as_ref, av_ref, gains_in, fv_ref, fs_ref, fu_ref, we_ref, wq_ref, id_ref, cot_ref, wo_hbm, wu_hbm, wd_hbm, ts_hbm, ns_hbm,
-    out_ref, gsone_ref, gvone_ref, gains_ref, m_ref, f_ref, tso_hbm, nso_hbm,
+    out_ref, gsone_ref, gvone_ref, gains_ref, a_ref, m_ref, e_ref, tso_hbm, nso_hbm,
     s1, v1, ffh, ffp, ffu, v2, sz, fac_node, fac_node_o, heads_out, heads_in,
     probs, att, att_out, att_in, wo_ref, wu_ref, wd_ref, gatt, gatt_in, gs1, fgain,
     fac_feed, fac_feed_o, gs_scr, ghead, ghead_in, fac_back, fac_back_o,
@@ -1117,9 +1163,10 @@
     wires = Wires(send_sem, recv_sem)
     ring = [peer("group", shift) for shift in range(1, spaces)]
 
-    def exchange(source, target):
+    def exchange(source, target, start=0, count=None):
+        rows = pl.ds(start, source.shape[1] if count is None else count)
         return [
-            wires.copy(source.at[lax.rem(me + n + 1, spaces)], target.at[me], ring[n])
+            wires.copy(source.at[lax.rem(me + n + 1, spaces), rows], target.at[me, rows], ring[n])
             for n in range(spaces - 1)
         ]
 
@@ -1137,48 +1184,67 @@
     swaps = start_all(
         [wires.copy(ts_hbm, tso_hbm, peer("core")), wires.copy(ns_hbm, nso_hbm, peer("core"))]
     )
+    nodes = ns_ref.shape[0]
+    key_copies = exchange(heads_out, heads_in, 0, nodes)
+    value_copies = exchange(heads_out, heads_in, nodes, nodes // 2)
+    grad_key_copies = exchange(ghead, ghead_in, 0, nodes)
+    grad_value_copies = exchange(ghead, ghead_in, nodes, nodes // 2)
+    start_later = lambda copies: functools.partial(start_all, copies)
     node_forward_kernel(
         ns_ref, nv_ref, as_ref, av_ref, ng_ref, fv_ref, fs_ref, fu_ref, we_ref, ag_ref, wq_ref,
-        s1, v1, ffh, ffp, ffu, v2, sz, fac_node, heads_out,
-    )
-    copies = start_all(exchange(heads_out, heads_in))
+        s1, v1, ffh, ffp, ffu, v2, sz, fac_node, heads_out, start_later(key_copies),
+    )
+    start_all(value_copies)
     swaps += start_all([wires.copy(fac_node, fac_node_o, peer("core"))])
     keep(heads_out, heads_in)
-    wait_all(copies)
-    attend_kernel(heads_in, id_ref, probs, att, att_out)
+    wait_all(key_copies)
+    attend_kernel(heads_in, id_ref, probs, att, att_out, functools.partial(wait_all, value_copies))
     copies = start_all(exchange(att_out, att_in))
     keep(att_out, att_in)
     wait_all(loads)
     wait_all(copies)
+    up_cols, rest_cols = pl.ds(0, AT_ATT), pl.ds(AT_ATT, FAC_FEED - AT_ATT)
+    feed_swap = wires.copy(fac_feed.at[:, up_cols], fac_feed_o.at[:, up_cols], peer("core"))
     feed_kernel(
-        att_in, sz, wo_ref, fg_ref, wu_ref, wd_ref, cot_ref, out_ref, gatt, gs1, fgain, fac_feed
+        att_in, sz, wo_ref, fg_ref, wu_ref, wd_ref, cot_ref, out_ref, gatt, gs1, fgain, fac_feed,
+        feed_swap.start,
     )
     copies = start_all(exchange(gatt, gatt_in))
-    feed_swap = start_all([wires.copy(fac_feed, fac_feed_o, peer("core"))])
+    swaps += start_all(
+        [wires.copy(fac_feed.at[:, rest_cols], fac_feed_o.at[:, rest_cols], peer("core"))]
+    )
     keep(gatt, gatt_in)
-    wait_all(copies)
-    attend_backward_kernel(heads_in, probs, att, gatt_in, ghead, gs_scr)
-    copies = start_all(exchange(ghead, ghead_in))
-    keep(ghead, ghead_in)
-    wait_all(feed_swap)
+    feed_swap.wait()
     feed_grads_kernel(fac_feed, fac_feed_o, first)
     cuts = start_all(first_cut(wires, first, first_got))
     wait_all(copies)
+    attend_backward_kernel(
+        heads_in, probs, att, gatt_in, ghead, gs_scr, start_later(grad_value_copies)
+    )
+    copies = start_all(grad_key_copies) + grad_value_copies
+    keep(ghead, ghead_in)
+    wait_all(cuts)
+    first_add_whole(first, first_got, first_sum)
+    cuts = start_all(second_cut(wires, first_sum, first_got2))
+    wait_all(copies)
+    qkv_cols, other_cols = pl.ds(0, AT_STREAM), pl.ds(AT_STREAM, FAC_BACK - AT_STREAM)
+    qkv_swap = wires.copy(fac_back.at[:, qkv_cols], fac_back_o.at[:, qkv_cols], peer("core"))
+
     node_backward_kernel(
         ghead_in, gs1, s1, v1, ffh, ffp, ffu, v2, sz,
         ng_ref, fv_ref, fs_ref, fu_ref, we_ref, ag_ref, wq_ref, fgain,
-        gsone_ref, gvone_ref, gains_ref, fac_back,
-    )
-    swaps += start_all([wires.copy(fac_back, fac_back_o, peer("core"))])
+        gsone_ref, gvone_ref, gains_ref, fac_back, qkv_swap.start,
+    )
+    swap = start_all(
+        [wires.copy(fac_back.at[:, other_cols], fac_back_o.at[:, other_cols], peer("core"))]
+    )
+    qkv_swap.wait()
+    wait_all(swaps)
+    attention_grads(fac_node, fac_node_o, fac_back, fac_back_o, fac_feed, fac_feed_o, a_ref)
     wait_all(cuts)
-    first_add_whole(first, first_got, first_sum)
-    cuts = start_all(second_cut(wires, first_sum, first_got2))
-    wait_all(swaps)
-    node_grads_kernel(
-        fac_node, fac_node_o, fac_back, fac_back_o, fac_feed, fac_feed_o, m_ref, tall_scr, low_scr
-    )
-    wait_all(cuts)
-    second_add(first_sum, first_got2, f_ref)
+    second_add(first_sum, first_got2, e_ref)
+    wait_all(swap)
+    node_grads(fac_node, fac_node_o, fac_back, fac_back_o, m_ref, tall_scr, low_scr)
 
 
 def middle(vmem_operands, hbm_operands, table_s, node_scalar, quads):
@@ -1197,17 +1263,18 @@
         ((nodes, D_S), F32),
         ((3, nodes, D_V), F32),
         ((8, D_S), F32),
-        ((quads, ROWS_M, 512), BF),
-        ((quads, ROWS_F // 4, 512), BF),
+        ((quads, ROWS_A, 512), BF),
+        ((quads, ROWS_N, 512), BF),
+        ((quads, ROWS_E, 512), BF),
         (table_s.shape, BF),
         (node_scalar.shape, BF),
     ]
-    wires = 4 * (spaces - 1) + 9
+    wires = 6 * (spaces - 1) + 12
     return pl.pallas_call(
         middle_kernel,
         out_shape=[jax.ShapeDtypeStruct(shape, kind) for shape, kind in outs],
         in_specs=[vmem] * len(vmem_operands) + [hbm] * (len(hbm_operands) + 2),
-        out_specs=[vmem] * 6 + [hbm] * 2,
+        out_specs=[vmem] * 7 + [hbm] * 2,
         scratch_shapes=[
             wide(nodes, D_S), wide(3, nodes, D_V), wide(3, nodes, D_V), wide(nodes, D_S),
             wide(3, nodes, D_V), wide(3, nodes, D_V), wide(nodes, D_MODEL),
@@ -1246,91 +1313,183 @@
     rows_scr[pl.ds(0, ref.shape[0]), :] = ref[...].astype(F32)
 
 
-def scalar_backward_kernel(
-    near_ref, lx_ref, ds_ref, gsone_ref, wn_ref, ts_hbm, ns_hbm, wnode_hbm, tso_hbm, nso_hbm,
-    m_ref, f_ref,
-    ratio_ref, pack_ref, rest_ref, gscal_ref, back_ref, m2_ref, ffin_ref,
-    ga_ref, gw_ref, gb_ref, pre_scr, grads_scr, grads_got, mix_scr, mix_got, rest_scr, rest_got,
-    m_own, m_got, m_sum, m_got2, f_own, f_got, ts_ref, ns_ref, wnode_ref, tso_ref, nso_ref,
-    send_sem, recv_sem, load_sem, near_scr,
+def backward_kernel(
+    near_ref, ev_ref, lx_ref, ds_ref, h_ref, z_ref, gsone_ref, wn_ref, gvone_ref, vo_ref, tv_ref,
+    nv_ref, vs_ref, vt_ref, gains_ref,
+    ts_hbm, ns_hbm, wnode_hbm, tso_hbm, nso_hbm, e_hbm, a_hbm, n_hbm,
+    gscal_ref, gvec_ref, plane_hbm, got_hbm,
+    near_scr, ev_scr, ga_ref, gw_ref, gb_ref, pre_scr, gp_ref, gq_ref, gvo_ref, up_scr,
+    gh_scr, ts_ref, ns_ref, wnode_ref, tso_ref, nso_ref,
+    grads_scr, grads_got, mix_scr, mix_got, rest_scr, rest_got, e_own, e_got, a_own, n_own,
+    s_scr, b_scr, v_got, backs_scr, backv_scr, fin_scr,
+    send_sem, recv_sem, load_sem, *share_refs,
 ):
     nodes = gsone_ref.shape[0]
     table = ts_ref.shape[0]
     rows = GROUP * nodes
-    quads = pack_ref.shape[0]
+    spaces = lax.axis_size("space")
+    quads = spaces // 2
     step = pl.program_id(0)
-    last = pl.num_programs(0) - 1
+    half = NEIGH // GROUP
+    last = 2 * half - 1
+    first_slot = lax.rem(step, half) * GROUP
+    at = place()
+    core = at["core"]
+    me = lax.axis_index("space")
+    mine = 2 * at["x"] + at["y"]
+    ring = [peer("group", shift) for shift in range(1, spaces)]
+    plane = [peer("x"), peer("y"), peer("diagonal")]
+
     wires = Wires(send_sem, recv_sem)
-    f_copies = z_send(wires, f_ref, f_got)
-    m_copies = first_cut(wires, m_ref, m_got)
-    pairs = (
-        (ts_hbm, ts_ref), (ns_hbm, ns_ref), (wnode_hbm, wnode_ref), (tso_hbm, tso_ref),
-        (nso_hbm, nso_ref), (f_ref.at[place()["z"]], f_own),
-    )
-    loads = [
-        pltpu.make_async_copy(source, target, load_sem.at[2 + n])
-        for n, (source, target) in enumerate(pairs)
-    ]
-    m_loads = own_quarters(m_ref, m_own, load_sem)
-    m_copies2 = second_cut(wires, m_sum, m_got2)
+    own_copy = lambda n, source, target: pltpu.make_async_copy(source, target, load_sem.at[n])
+    quarters = lambda share_ref, own_ref, n: own_quarters(
+        share_ref, own_ref, [load_sem.at[n], load_sem.at[n + 1]]
+    )
+    refs = [share_refs[n : n + 5] for n in range(0, len(share_refs), 5)]
+    e_copiesz = z_send(wires, e_hbm, e_got)
+    share_a = Share(wires, a_hbm, a_own, refs[0], quarters(a_hbm, a_own, 9))
+    share_n = Share(wires, n_hbm, n_own, refs[1], quarters(n_hbm, n_own, 11))
+    share_s = Share(wires, s_scr, None, refs[2])
+    share_b = Share(wires, b_scr, None, refs[3])
+    v_scr = s_scr.at[:, pl.ds(0, ROWS_V), :]
+    share_v = Share(wires, v_scr, None, refs[4])
     pair_copies = [
         wires.copy(source, target, peer("core"))
         for source, target in ((grads_scr, grads_got), (mix_scr, mix_got), (rest_scr, rest_got))
     ]
+    v_pair = n_own
+    v_copies = [wires.copy(v_pair.at[1 - core], v_got, peer("core"))]
+    bounds = [0]
+    for count in ALL_ROWS:
+        bounds.append(bounds[-1] + count // 4)
+    rows_e, rows_a, rows_n, rows_s, rows_b, rows_v = [
+        pl.ds(lo, hi - lo) for lo, hi in zip(bounds, bounds[1:])
+    ]
+    batches = [(bounds[0], bounds[3]), (bounds[3], bounds[4]), (bounds[4], bounds[5])]
+    rounds = [
+        [
+            wires.copy(fin_scr.at[pl.ds(lo, hi - lo), :], plane_hbm.at[mine, pl.ds(lo, hi - lo), :], to)
+            for to in plane[:2]
+        ]
+        for lo, hi in batches
+    ]
+    relays = []
+    over_x, over_y = 2 * (1 - at["x"]) + at["y"], 2 * at["x"] + 1 - at["y"]
+    for lo, hi in batches:
+        middle_row = (lo + hi) // 2
+        upper, lower = pl.ds(lo, middle_row - lo), pl.ds(middle_row, hi - middle_row)
+        relays.append(
+            [
+                wires.copy(plane_hbm.at[over_x, upper, :], plane_hbm.at[over_x, upper, :], plane[1]),
+                wires.copy(plane_hbm.at[over_y, lower, :], plane_hbm.at[over_y, lower, :], plane[0]),
+            ]
+        )
+    last_round = [
+        wires.copy(fin_scr.at[rows_v, :], plane_hbm.at[mine, rows_v, :], to) for to in plane
+    ]
+    back_scalar, back_vector = pl.ds(0, D_S), pl.ds(D_S, 3 * D_V)
+    scalar_copies = [
+        wires.copy(
+            backs_scr.at[lax.rem(me + n + 1, spaces)], got_hbm.at[me, :, back_scalar], ring[n]
+        )
+        for n in range(spaces - 1)
+    ]
+    vector_copies = [
+        wires.copy(
+            backv_scr.at[lax.rem(me + n + 1, spaces)], got_hbm.at[me, :, back_vector], ring[n]
+        )
+        for n in range(spaces - 1)
+    ]
+    e_load = own_copy(0, e_hbm.at[at["z"]], e_own)
+    loads = [
+        own_copy(1 + n, source, target)
+        for n, (source, target) in enumerate(
+            (
+                (ts_hbm, ts_ref), (ns_hbm, ns_ref), (wnode_hbm.at[:, pl.ds(0, D_S)], wnode_ref),
+                (tso_hbm, tso_ref),
+                (nso_hbm, nso_ref),
+            )
+        )
+    ]
+    own_scalar = own_copy(6, backs_scr.at[me], got_hbm.at[me, :, back_scalar])
+    own_vector = own_copy(7, backv_scr.at[me], got_hbm.at[me, :, back_vector])
+    own_plane = own_copy(8, fin_scr, plane_hbm.at[mine])
+    target_load = own_copy(13, wnode_hbm.at[:, pl.ds(D_S, D_S)], wnode_ref)
+
+    def early_total():
+        e_load.wait()
+        wait_all(e_copiesz)
+        fin_scr[rows_e, :] = z_add(e_own[...], e_got)
+
+    def middle_total():
+        fin_scr[rows_a, :] = share_a.total()
+        fin_scr[rows_n, :] = share_n.total()
+        start_all(rounds[0])
+
+    def source_total():
+        fin_scr[rows_s, :] = share_s.total()
+        start_all(rounds[1])
+
+    def relay(n):
+        wait_all(rounds[n])
+        start_all(relays[n])
+
+    schedule = {
+        (4, 0): [share_a.cut],
+        (7, 0): [share_a.spread],
+        (7, 1): [share_n.spread],
+        (8, 1): [share_s.cut],
+        (9, 1): [early_total],
+        (10, 0): [share_b.cut],
+        (10, 1): [share_s.spread, middle_total],
+        (11, 1): [share_b.spread, source_total],
+    }
+
+    def carry_on(part):
+        for (at_step, at_part), actions in schedule.items():
+            if at_part == part:
+
+                @pl.when(step == at_step)
+                def _():
+                    for action in actions:
+                        action()
 
     @pl.when(step == 0)
     def _():
-        greet([peer("x"), peer("y"), peer("core")] + [peer("z", shift) for shift in (1, 2, 3)])
-        start_all(m_copies)
-        start_all(f_copies)
-        start_all(m_loads)
-        start_all(loads)
+        greet(ring + plane)
+        share_a.start()
+        share_n.start()
+        start_all(e_copiesz)
+        start_all([e_load] + loads)
         keep_rows(near_ref, near_scr)
-        for ref in (ga_ref, gw_ref, gb_ref):
+        for c in range(3):
+            keep_rows(ev_ref.at[c], ev_scr.at[c])
+        for ref in (ga_ref, gw_ref, gb_ref, gp_ref, gq_ref, gvo_ref):
             ref[...] = jnp.zeros_like(ref)
 
-    @pl.when(step == 4)
+    carry_on(0)
+
+    @pl.when(step < half)
     def _():
-        wait_all(m_loads)
-        wait_all(m_copies)
-        first_add(m_own, m_got, m_sum)
-        start_all(m_copies2)
-
-    for start in range(0, D_S, 256):
-        cols = pl.ds(start, 256)
-        for first in range(0, nodes, ROW_TILE):
-            part = pl.ds(first, ROW_TILE)
-            share = gsone_ref[part, cols] * (1.0 / NEIGH)
-            acc = None
-            for k in range(GROUP):
-                g = (ds_ref[k, part, cols].astype(F32) * share).astype(BF)
-                pre_scr[pl.ds(k * nodes + first, ROW_TILE), cols] = g
-                g = g.astype(F32)
-                acc = g if acc is None else acc + g
-            gb_ref[part, cols] += acc
-    one_hot = one_hot_rows(near_scr, step * GROUP, table, nodes)
-    grad_pre = pre_scr[...]
-    ga_ref[...] += product(one_hot, grad_pre)
-    lx = lx_ref[...].reshape(rows, H_P)
-    gw_ref[...] += lead_product(lx, grad_pre)
-    for start, width in LANE_BLOCKS:
-        cols = pl.ds(start, width)
-        grad_length = product_back(grad_pre, wn_ref[cols, :])
-        for first in range(0, nodes, ROW_TILE):
-            part = pl.ds(first, ROW_TILE)
-            for k in range(GROUP):
-                at = k * nodes + first
-                ratio = grad_length[at : at + ROW_TILE] * pl.reciprocal(
-                    lx_ref[k, part, cols].astype(F32), approx=True
-                )
-                if start == 512:
-                    lane = lax.broadcasted_iota(jnp.int32, (ROW_TILE, width), 1)
-                    ratio = jnp.where(lane == 0, ratio, 0.0)
-                ratio_ref[k, part, cols] = ratio.astype(BF)
-
-    @pl.when(step == last)
+        for start in range(0, D_S, 256):
+            cols = pl.ds(start, 256)
+            for first in range(0, nodes, ROW_TILE):
+                part = pl.ds(first, ROW_TILE)
+                share = gsone_ref[part, cols] * (1.0 / NEIGH)
+                acc = None
+                for k in range(GROUP):
+                    g = (ds_ref[k, part, cols].astype(F32) * share).astype(BF)
+                    pre_scr[step, pl.ds(k * nodes + first, ROW_TILE), cols] = g
+                    g = g.astype(F32)
+                    acc = g if acc is None else acc + g
+                gb_ref[part, cols] += acc
+        one_hot = one_hot_rows(near_scr, first_slot, table, nodes)
+        grad_pre = pre_scr[step]
+        ga_ref[...] += product(one_hot, grad_pre)
+        lx = lx_ref[...].reshape(rows, H_P)
+        gw_ref[...] += lead_product(lx, grad_pre)
+    @pl.when(step == half - 1)
     def _():
-        core = place()["core"]
         grads_scr[pl.ds(0, table), :] = ga_ref[...].astype(BF)
         grads_scr[pl.ds(table, nodes), :] = gb_ref[...].astype(BF)
         for z in range(quads):
@@ -1341,242 +1500,97 @@
         start_all(pair_copies)
         wait_all(loads)
         ga = grads_scr[pl.ds(0, table), :]
-        gb = grads_scr[pl.ds(table, nodes), :]
-        projected = product_back(ga, wnode_ref[:, pl.ds(0, D_S)])
-        gscal_ref[...] = (
-            gsone_ref[...] + product_back(gb, wnode_ref[:, pl.ds(D_S, D_S)]) + projected[:nodes]
-        )
-        back_ref[...] = projected[nodes:].astype(BF)
+        projected = product_back(ga, wnode_ref[...])
+        target_load.start()
+        gscal_ref[...] = gsone_ref[...] + projected[:nodes]
+        for d in range(spaces):
+            backs_scr[d] = projected[nodes + d * CAP : nodes + (d + 1) * CAP].astype(BF)
+        start_all(scalar_copies)
+        own_scalar.start()
+
+    @pl.when(step == half)
+    def _():
         wait_all(pair_copies)
-        gao = grads_got[pl.ds(0, table), :]
-        gbo = grads_got[pl.ds(table, nodes), :]
-        for z in range(quads):
-            own = pl.ds(pl.multiple_of((2 * z + core) * 128, 128), 128)
-            for half, (left, right, lefto, righto) in enumerate(
-                ((ts_ref, ga, tso_ref, gao), (ns_ref, gb, nso_ref, gbo))
-            ):
+        grad_rows = pl.ds(0, table), pl.ds(table, nodes)
+        for side, (left, lefto, pack) in enumerate(
+            ((ts_ref, tso_ref, s_scr), (ns_ref, nso_ref, b_scr))
+        ):
+            right, righto = grads_scr[grad_rows[side], :], grads_got[grad_rows[side], :]
+            for z in range(quads):
+                own = pl.ds(pl.multiple_of((2 * z + core) * 128, 128), 128)
                 block = lead_product(left[:, own], right) + lead_product(lefto[:, own], righto)
                 block = block.astype(BF)
                 for n in range(2):
-                    pack_ref[z, pl.ds((2 * half + n) * 128, 128), :] = block[
-                        :, n * 512 : (n + 1) * 512
-                    ]
+                    pack[z, pl.ds(n * 128, 128), :] = block[:, n * 512 : (n + 1) * 512]
+            if side == 0:
+                share_n.cut()
+                share_s.start()
+        for z in range(quads):
+            own = pl.ds(pl.multiple_of((2 * z + core) * 128, 128), 128)
             for r in range(4):
                 lanes = pl.ds(r * 128, 128)
-                pack_ref[z, pl.ds(512, 128), lanes] = (
+                b_scr[z, pl.ds(256, 128), lanes] = (
                     gw_ref[pl.ds(r * 128, 128), own] + mix_got[z, :, lanes].astype(F32)
                 ).astype(BF)
-            rest_ref[z] = gw_ref[pl.ds(512, 64), own] + rest_got[z].astype(F32)
-        wait_all(m_copies2)
-        second_add(m_sum, m_got2, m2_ref)
-        wait_all(f_copies)
-        ffin_ref[...] = z_add(f_own[...], f_got)
-
-
-def scalar_backward(near, lx, dsilu, gsone, wn, ts, ns, w_node, ts_other, ns_other, m, f):
-    nodes = gsone.shape[0]
-    table = ts.shape[0]
-    quads = m.shape[0]
-    rows = GROUP * nodes
-    once = pl.Buffered(1)
-    whole = lambda shape: pl.BlockSpec(shape, lambda g: (0,) * len(shape), pipeline_mode=once)
-    slots = lambda *shape: pl.BlockSpec((GROUP,) + shape, lambda g: (g,) + (0,) * len(shape))
-    steps = lambda *shape: pl.BlockSpec((1,) + shape, lambda g: (g,) + (0,) * len(shape))
-    outs = [
-        ((quads, ROWS_S, 512), BF),
-        ((quads, 64, 128), F32),
-        ((nodes, D_S), F32),
-        ((table - nodes, D_S), BF),
-        ((quads, ROWS_M // 4, 512), BF),
-        ((ROWS_F // 4, 512), BF),
-    ]
-    return pl.pallas_call(
-        scalar_backward_kernel,
-        grid=(NEIGH // GROUP,),
-        in_specs=[whole(near.shape), slots(nodes, H_P), slots(nodes, D_S)]
-        + [whole(one.shape) for one in (gsone, wn)]
-        + [pl.BlockSpec(memory_space=pl.ANY)] * 7,
-        out_specs=[slots(nodes, H_P)] + [whole(shape) for shape, kind in outs],
-        out_shape=[jax.ShapeDtypeStruct((NEIGH, nodes, H_P), BF)]
-        + [jax.ShapeDtypeStruct(shape, kind) for shape, kind in outs],
-        scratch_shapes=[
-            pltpu.VMEM((table, D_S), F32),
-            pltpu.VMEM((H_P, D_S), F32),
-            pltpu.VMEM((nodes, D_S), F32),
-            pltpu.VMEM((rows, D_S), BF),
-            pltpu.VMEM((table + nodes, D_S), BF),
-            pltpu.VMEM((table + nodes, D_S), BF),
-            pltpu.VMEM((quads, 128, 512), BF),
-            pltpu.VMEM((quads, 128, 512), BF),
-            pltpu.VMEM((quads, 64, 128), BF),
-            pltpu.VMEM((quads, 64, 128), BF),
-            pltpu.VMEM((2, quads, ROWS_M // 4, 512), BF),
-            pltpu.VMEM((2, quads, ROWS_M // 4, 512), BF),
-            pltpu.VMEM((2, quads, ROWS_M // 4, 512), BF),
-            pltpu.VMEM((2, quads, ROWS_M // 8, 512), BF),
-            pltpu.VMEM((ROWS_F // 4, 512), BF),
-            pltpu.VMEM((3, ROWS_F // 4, 512), BF),
-        ]
-        + [pltpu.VMEM(one.shape, BF) for one in (ts, ns, w_node, ts_other, ns_other)]
-        + [
-            pltpu.SemaphoreType.DMA((10,)),
-            pltpu.SemaphoreType.DMA((10,)),
-            pltpu.SemaphoreType.DMA((8,)),
-            pltpu.VMEM((32, 128), F32),
-        ],
-        compiler_params=pltpu.CompilerParams(
-            collective_id=1, has_side_effects=True, vmem_limit_bytes=VMEM_LIMIT
-        ),
-        name="scalar_backward",
-    )(near, lx, dsilu, gsone, wn, ts, ns, w_node, ts_other, ns_other, m, f)
-
-
-def vector_backward_kernel(
-    near_ref, ev_ref, h_ref, ratio_ref, z_ref, gvone_ref, vo_ref, tv_ref,
-    nv_ref, vs_ref, vt_ref, rest_ref, gains_ref, s_ref, m_ref, f_ref, backs_ref,
-    plane_ref, gvec_ref, got_ref, gp_ref, gq_ref, gvo_ref, up_scr, gh_scr,
-    s_own, s_got, s_sum, s_got2, s_part, s_gotz, m_own, m_gotz, t_scr, t_got, t_half, t_got1, t_sum, t_got2,
-    t_part, t_gotz, back_scr, fin_scr, own_sem, send_sem, recv_sem, load_sem, near_scr, ev_scr,
-):
-    nodes = gvone_ref.shape[1]
-    table = tv_ref.shape[1]
-    rows = GROUP * nodes
-    spaces = lax.axis_size("space")
-    quads = spaces // 2
-    step = pl.program_id(0)
-    last = pl.num_programs(0) - 1
-    at = place()
-    me = lax.axis_index("space")
-    mine = 2 * at["x"] + at["y"]
-    wires = Wires(send_sem, recv_sem)
-    early, late = ROWS_F // 4 + ROWS_M // 4, ROWS_S // 4 + ROWS_T // 4
-    ring = [peer("group", shift) for shift in range(1, spaces)]
-    plane = [peer("x"), peer("y"), peer("diagonal")]
-    s_copies = first_cut(wires, s_ref, s_got)
-    s_copies2 = second_cut(wires, s_sum, s_got2)
-    s_copiesz = z_send(wires, s_part, s_gotz)
-    m_copiesz = z_send(wires, m_ref, m_gotz)
-    early_rows, late_rows = pl.ds(0, early), pl.ds(early, late)
-    early_copies = [
-        wires.copy(fin_scr.at[early_rows, :], plane_ref.at[mine, early_rows, :], to) for to in plane
-    ]
-    late_copies = [
-        wires.copy(fin_scr.at[late_rows, :], plane_ref.at[mine, late_rows, :], to) for to in plane
-    ]
-    back_scalar, back_vector = pl.ds(0, D_S), pl.ds(D_S, 3 * D_V)
-    scalar_copies = [
-        wires.copy(
-            backs_ref.at[pl.ds(lax.rem(me + n + 1, spaces) * CAP, CAP), :],
-            got_ref.at[me, :, back_scalar],
-            ring[n],
-        )
-        for n in range(spaces - 1)
-    ]
-    back_copies = [
-        wires.copy(
-            back_scr.at[lax.rem(me + n + 1, spaces)], got_ref.at[me, :, back_vector], ring[n]
-        )
-        for n in range(spaces - 1)
-    ]
-    s_loads = own_quarters(s_ref, s_own, load_sem)
-    m_load = pltpu.make_async_copy(m_ref.at[at["z"]], m_own, load_sem.at[2])
-    f_load = pltpu.make_async_copy(f_ref, fin_scr.at[pl.ds(0, ROWS_F // 4), :], load_sem.at[3])
-    own_scalar = pltpu.make_async_copy(
-        backs_ref.at[pl.ds(me * CAP, CAP), :], got_ref.at[me, :, back_scalar], load_sem.at[4]
-    )
-    t_pair = [wires.copy(t_scr.at[:, 1 - at["core"]], t_got, peer("core"))]
-    t_copies = first_cut(wires, t_half, t_got1)
-    t_copies2 = second_cut(wires, t_sum, t_got2)
-    t_copiesz = z_send(wires, t_part, t_gotz)
-
-    @pl.when(step == 0)
+        share_b.start()
+        target_load.wait()
+        gscal_ref[...] += product_back(grads_scr[pl.ds(table, nodes), :], wnode_ref[...])
+
+    @pl.when(step >= half)
     def _():
-        greet(ring + plane)
-        start_all(s_copies)
-        start_all(m_copiesz)
-        start_all(s_loads + [m_load, f_load, own_scalar])
-        keep_rows(near_ref, near_scr)
-        for c in range(3):
-            keep_rows(ev_ref.at[c], ev_scr.at[c])
-        for ref in (gp_ref, gq_ref, gvo_ref):
-            ref[...] = jnp.zeros_like(ref)
-
-    @pl.when(step == 3)
-    def _():
-        wait_all(s_loads)
-        wait_all(s_copies)
-        first_add(s_own, s_got, s_sum)
-        start_all(s_copies2)
-        start_all(scalar_copies)
-
-    @pl.when(step == 4)
-    def _():
-        wait_all([m_load, f_load])
-        wait_all(m_copiesz)
-        fin_scr[pl.ds(ROWS_F // 4, ROWS_M // 4), :] = z_add(m_own[...], m_gotz)
-        start_all(early_copies)
-
-    @pl.when(step == last)
-    def _():
-        wait_all(s_copies2)
-        second_add(s_sum, s_got2, s_part)
-        start_all(s_copiesz)
-
-    for first in range(0, nodes, ROW_TILE):
-        part = pl.ds(first, ROW_TILE)
-        share = [gvone_ref[c, part, :] * (1.0 / NEIGH) for c in range(3)]
-        for k in range(GROUP):
-            z = [z_ref[k, c, part, :].astype(F32) for c in range(3)]
-            power = power_of(z) + 1.0
-            inverse = lax.rsqrt(power)
-            s = sigmoid(power * inverse)
-            dot = z[0] * share[0] + z[1] * share[1] + z[2] * share[2]
-            factor = dot * inverse * (s * (1.0 - s))
-            for c in range(3):
-                up_scr[c, pl.ds(k * nodes + first, ROW_TILE), :] = (
-                    share[c] * s + z[c] * factor
-                ).astype(BF)
-    for start, width in LANE_BLOCKS:
-        cols = pl.ds(start, width)
-        grad_direct = [product_back(up_scr[c], vo_ref[cols, :]) for c in range(3)]
         for first in range(0, nodes, ROW_TILE):
             part = pl.ds(first, ROW_TILE)
-            acc = [None] * 3
+            share = [gvone_ref[c, part, :] * (1.0 / NEIGH) for c in range(3)]
             for k in range(GROUP):
-                row = k * nodes + first
-                ratio = ratio_ref[k, part, cols].astype(F32)
+                z = [z_ref[k, c, part, :].astype(F32) for c in range(3)]
+                power = power_of(z) + 1.0
+                inverse = lax.rsqrt(power)
+                s = sigmoid(power * inverse)
+                dot = z[0] * share[0] + z[1] * share[1] + z[2] * share[2]
+                factor = dot * inverse * (s * (1.0 - s))
                 for c in range(3):
-                    g = grad_direct[c][row : row + ROW_TILE] + ratio * h_ref[
-                        k, c, part, cols
-                    ].astype(F32)
-                    gh_scr[c, pl.ds(row, ROW_TILE), cols] = g.astype(BF)
-                    acc[c] = g if acc[c] is None else acc[c] + g
-            for c in range(3):
-                gq_ref[c, part, cols] += acc[c]
-    one_hot = one_hot_rows(near_scr, step * GROUP, table, nodes)
-    for c in range(3):
-        evr = jnp.broadcast_to(slot_rows(ev_scr.at[c], step * GROUP, nodes), (16, rows))
-        lead = jnp.concatenate([one_hot, evr.astype(BF)], axis=0)
-        gp_ref[c] += product(lead, gh_scr[c])
-        gvo_ref[...] += lead_product(up_scr[c], h_ref[:, c, :, :].reshape(rows, H_P))
+                    up_scr[c, pl.ds(k * nodes + first, ROW_TILE), :] = (
+                        share[c] * s + z[c] * factor
+                    ).astype(BF)
+        for start, width in LANE_BLOCKS:
+            cols = pl.ds(start, width)
+            grad_length = product_back(pre_scr[step - half], wn_ref[cols, :])
+            grad_direct = [product_back(up_scr[c], vo_ref[cols, :]) for c in range(3)]
+            for first in range(0, nodes, ROW_TILE):
+                part = pl.ds(first, ROW_TILE)
+                acc = [None] * 3
+                for k in range(GROUP):
+                    row = k * nodes + first
+                    ratio = grad_length[row : row + ROW_TILE] * pl.reciprocal(
+                        lx_ref[k, part, cols].astype(F32), approx=True
+                    )
+                    if start == 512:
+                        lane = lax.broadcasted_iota(jnp.int32, (ROW_TILE, width), 1)
+                        ratio = jnp.where(lane == 0, ratio, 0.0)
+                    for c in range(3):
+                        g = grad_direct[c][row : row + ROW_TILE] + ratio * h_ref[
+                            k, c, part, cols
+                        ].astype(F32)
+                        gh_scr[c, pl.ds(row, ROW_TILE), cols] = g.astype(BF)
+                        acc[c] = g if acc[c] is None else acc[c] + g
+                for c in range(3):
+                    gq_ref[c, part, cols] += acc[c]
+    carry_on(1)
+
+    @pl.when(step >= half)
+    def _():
+        one_hot = one_hot_rows(near_scr, first_slot, table, nodes)
+        for c in range(3):
+            evr = jnp.broadcast_to(slot_rows(ev_scr.at[c], first_slot, nodes), (16, rows))
+            lead = jnp.concatenate([one_hot, evr.astype(BF)], axis=0)
+            gp_ref[c] += product(lead, gh_scr[c])
+            gvo_ref[...] += lead_product(up_scr[c], h_ref[:, c, :, :].reshape(rows, H_P))
 
     @pl.when(step == last)
     def _():
         tall = D_V // spaces
         gp = [gp_ref[c, pl.ds(0, table), :].astype(BF) for c in range(3)]
         gq = [gq_ref[c].astype(BF) for c in range(3)]
-        for c in range(3):
-            projected = product(gp[c], vs_ref[...])
-            gvec_ref[c] = gvone_ref[c] + product(gq[c], vt_ref[...]) + projected[:nodes]
-            for d in range(spaces):
-                back_scr[d, :, pl.ds(c * D_V, D_V)] = projected[
-                    nodes + d * CAP : nodes + (d + 1) * CAP
-                ].astype(BF)
-        start_all(back_copies)
-        own = pltpu.make_async_copy(
-            back_scr.at[me], got_ref.at[me, :, back_vector], load_sem.at[5]
-        )
-        own.start()
         grads = []
         for lead_ref, right in ((tv_ref, gp), (nv_ref, gq)):
             total = None
@@ -1589,7 +1603,7 @@
         tails = jnp.zeros((D_V, 128), F32)
         for n, grad in enumerate(grads):
             for p in range(spaces):
-                t_scr[p // 2, p % 2, pl.ds(n * tall, tall), :] = grad[
+                v_pair[p % 2, p // 2, pl.ds(n * tall, tall), :] = grad[
                     p * tall : (p + 1) * tall, :512
                 ].astype(BF)
             tails = tails + jnp.where(
@@ -1601,9 +1615,11 @@
         row = lax.broadcasted_iota(jnp.int32, (tall, 128), 0)
         below = pl.ds(3 * tall, tall)
         for p in range(spaces):
-            rest = jnp.where(at["core"] == p % 2, rest_ref[p // 2], 0.0)
-            t_scr[p // 2, p % 2, below, pl.ds(0, 128)] = tails[p * tall : (p + 1) * tall]
-            t_scr[p // 2, p % 2, below, pl.ds(128, 128)] = rest[16 : 16 + tall].astype(BF)
+            own = pl.ds(p * 128, 128)
+            rest = gw_ref[pl.ds(512, 64), own] + rest_got[p // 2].astype(F32)
+            rest = jnp.where(core == p % 2, rest, 0.0)
+            v_pair[p % 2, p // 2, below, pl.ds(0, 128)] = tails[p * tall : (p + 1) * tall]
+            v_pair[p % 2, p // 2, below, pl.ds(128, 128)] = rest[16 : 16 + tall].astype(BF)
             extra = jnp.where(row == 0, jnp.broadcast_to(rest[0:1], (tall, 128)), 0.0)
             for n in range(5):
                 piece = jnp.broadcast_to(vedge[0:1, n * 128 : (n + 1) * 128], (tall, 128))
@@ -1613,119 +1629,127 @@
                     gains_ref[n : n + 1, p * 128 : (p + 1) * 128], (tall, 128)
                 )
                 extra = jnp.where(row == 6 + n, piece, extra)
-            t_scr[p // 2, p % 2, below, pl.ds(256, 128)] = extra.astype(BF)
-            t_scr[p // 2, p % 2, below, pl.ds(384, 128)] = jnp.zeros((tall, 128), BF)
-        start_all(t_pair)
-        wait_all(t_pair)
-        t_half[...] = (t_scr[:, at["core"]].astype(F32) + t_got[...].astype(F32)).astype(BF)
-        start_all(t_copies)
-        wait_all(t_copies)
-        first_add_whole(t_half, t_got1, t_sum)
-        start_all(t_copies2)
-        wait_all(t_copies2)
-        second_add(t_sum, t_got2, t_part)
-        start_all(t_copiesz)
-        wait_all(s_copiesz)
-        fin_scr[pl.ds(early, ROWS_S // 4), :] = z_add(s_part[at["z"]], s_gotz)
-        wait_all(t_copiesz)
-        fin_scr[pl.ds(early + ROWS_S // 4, ROWS_T // 4), :] = z_add(t_part[at["z"]], t_gotz)
-        start_all(late_copies)
-        own.wait()
+            v_pair[p % 2, p // 2, below, pl.ds(256, 128)] = extra.astype(BF)
+            v_pair[p % 2, p // 2, below, pl.ds(384, 128)] = jnp.zeros((tall, 128), BF)
+        start_all(v_copies)
+        for c in range(3):
+            projected = product(gp[c], vs_ref[...])
+            gvec_ref[c] = gvone_ref[c] + product(gq[c], vt_ref[...]) + projected[:nodes]
+            for d in range(spaces):
+                backv_scr[d, :, pl.ds(c * D_V, D_V)] = projected[
+                    nodes + d * CAP : nodes + (d + 1) * CAP
+                ].astype(BF)
+        relay(0)
+        start_all(vector_copies)
+        own_vector.start()
+        wait_all(v_copies)
+        v_scr[...] = (v_pair[core].astype(F32) + v_got[...].astype(F32)).astype(BF)
+        share_v.start()
+        share_v.cut()
+        fin_scr[rows_b, :] = share_b.total()
+        start_all(rounds[2])
+        share_v.spread()
+        relay(1)
+        relay(2)
+        fin_scr[rows_v, :] = share_v.total()
+        start_all(last_round)
+        own_plane.start()
+        for copies in relays:
+            wait_all(copies)
+        wait_all(scalar_copies)
+        wait_all(vector_copies)
         own_scalar.wait()
-        wait_all(scalar_copies)
-        own_plane = pltpu.make_async_copy(fin_scr, plane_ref.at[mine], own_sem)
-        own_plane.start()
+        own_vector.wait()
         own_plane.wait()
-        wait_all(back_copies)
-        wait_all(early_copies)
-        wait_all(late_copies)
-
-
-def vector_backward(
-    near, ev, hidden, ratio, update, gvone, vout, tv, nv, vs, vt, rest, gains,
-    s, m, f, back,
-):
-    nodes = gvone.shape[1]
-    table = tv.shape[1]
-    quads = s.shape[0]
+        wait_all(last_round)
+
+
+def backward(blocked, whole_operands, hbm_operands):
+    near, ev, lx, dsilu, hidden, update = blocked
+    ts, ns, w_node = hbm_operands[:3]
+    nodes = ns.shape[0]
+    table = ts.shape[0]
+    quads = hbm_operands[-1].shape[0]
     spaces = 2 * quads
     rows = GROUP * nodes
+    half = NEIGH // GROUP
     once = pl.Buffered(1)
     whole = lambda shape: pl.BlockSpec(shape, lambda g: (0,) * len(shape), pipeline_mode=once)
-    slots = lambda *shape: pl.BlockSpec((GROUP,) + shape, lambda g: (g,) + (0,) * len(shape))
-    steps = lambda *shape: pl.BlockSpec((1,) + shape, lambda g: (g,) + (0,) * len(shape))
+    early = lambda *shape: pl.BlockSpec(
+        (GROUP,) + shape, lambda g: (jnp.minimum(g, half - 1),) + (0,) * len(shape)
+    )
+    late = lambda *shape: pl.BlockSpec(
+        (GROUP,) + shape, lambda g: (jnp.maximum(g - half, 0),) + (0,) * len(shape)
+    )
+    both = lambda *shape: pl.BlockSpec(
+        (GROUP,) + shape, lambda g: (lax.rem(g, half),) + (0,) * len(shape)
+    )
+    hbm = pl.BlockSpec(memory_space=pl.ANY)
     outs = [
-        ((4, (ROWS_F + ROWS_M + ROWS_S + ROWS_T) // 4, 512), BF),
+        ((nodes, D_S), F32),
         ((3, nodes, D_V), F32),
+        ((4, sum(ALL_ROWS) // 4, 512), BF),
         ((spaces, CAP, D_S + 3 * D_V), BF),
     ]
     bits = lambda *shape: pltpu.VMEM(shape, BF)
+    wide = lambda *shape: pltpu.VMEM(shape, F32)
+    grads = (table + nodes, D_S)
+    pieces = lambda count: [
+        bits(2, quads, count // 4, 512), bits(2, quads, count // 4, 512),
+        bits(2, quads, count // 8, 512), bits(quads, count // 4, 512), bits(3, count // 4, 512),
+    ]
+    wires = 57 + 2 * (spaces - 1)
     return pl.pallas_call(
-        vector_backward_kernel,
-        grid=(NEIGH // GROUP,),
+        backward_kernel,
+        grid=(2 * half,),
         in_specs=[
             whole(near.shape),
             whole(ev.shape),
-            slots(3, nodes, H_P),
-            slots(nodes, H_P),
-            slots(3, nodes, D_V),
+            both(nodes, H_P),
+            early(nodes, D_S),
+            late(3, nodes, H_P),
+            late(3, nodes, D_V),
         ]
-        + [whole(one.shape) for one in (gvone, vout, tv, nv, vs, vt, rest, gains)]
-        + [pl.BlockSpec(memory_space=pl.ANY)] * 4,
-        out_specs=[
-            pl.BlockSpec(memory_space=pl.ANY),
-            whole(outs[1][0]),
-            pl.BlockSpec(memory_space=pl.ANY),
-        ],
+        + [whole(one.shape) for one in whole_operands]
+        + [hbm] * len(hbm_operands),
+        out_specs=[whole(outs[0][0]), whole(outs[1][0]), hbm, hbm],
         out_shape=[jax.ShapeDtypeStruct(shape, kind) for shape, kind in outs],
         scratch_shapes=[
-            pltpu.VMEM((3, table + 16, H_P), F32),
-            pltpu.VMEM((3, nodes, H_P), F32),
-            pltpu.VMEM((D_V, H_P), F32),
-            bits(3, rows, D_V),
+            wide(32, 128), wide(3, 32, 128),
+            wide(table, D_S), wide(H_P, D_S), wide(nodes, D_S), bits(half, rows, D_S),
+            wide(3, table + 16, H_P), wide(3, nodes, H_P), wide(D_V, H_P), bits(3, rows, D_V),
             bits(3, rows, H_P),
-            bits(2, quads, ROWS_S // 4, 512),
-            bits(2, quads, ROWS_S // 4, 512),
-            bits(2, quads, ROWS_S // 4, 512),
-            bits(2, quads, ROWS_S // 8, 512),
-            bits(quads, ROWS_S // 4, 512),
-            bits(3, ROWS_S // 4, 512),
-            bits(ROWS_M // 4, 512),
-            bits(3, ROWS_M // 4, 512),
-            bits(quads, 2, ROWS_T, 512),
-            bits(quads, ROWS_T, 512),
-            bits(quads, ROWS_T, 512),
-            bits(2, quads, ROWS_T // 4, 512),
-            bits(2, quads, ROWS_T // 4, 512),
-            bits(2, quads, ROWS_T // 8, 512),
-            bits(quads, ROWS_T // 4, 512),
-            bits(3, ROWS_T // 4, 512),
-            bits(spaces, CAP, 3 * D_V),
-            bits((ROWS_F + ROWS_M + ROWS_S + ROWS_T) // 4, 512),
-            pltpu.SemaphoreType.DMA,
-            pltpu.SemaphoreType.DMA((38,)),
-            pltpu.SemaphoreType.DMA((38,)),
-            pltpu.SemaphoreType.DMA((6,)),
-            pltpu.VMEM((32, 128), F32),
-            pltpu.VMEM((3, 32, 128), F32),
-        ],
+        ]
+        + [
+            bits(*(one.shape if one is not w_node else (D_S, D_S))) for one in hbm_operands[:5]
+        ]
+        + [
+            bits(*grads), bits(*grads), bits(quads, 128, 512), bits(quads, 128, 512),
+            bits(quads, 64, 128), bits(quads, 64, 128), bits(ROWS_E, 512), bits(3, ROWS_E, 512),
+            bits(2, quads, ROWS_A // 4, 512), bits(2, quads, ROWS_N // 4, 512),
+            bits(quads, ROWS_S, 512), bits(quads, ROWS_B, 512),
+            bits(quads, ROWS_V, 512),
+            bits(spaces, CAP, D_S), bits(spaces, CAP, 3 * D_V), bits(sum(ALL_ROWS) // 4, 512),
+            pltpu.SemaphoreType.DMA((wires,)),
+            pltpu.SemaphoreType.DMA((wires,)),
+            pltpu.SemaphoreType.DMA((14,)),
+        ]
+        + sum([pieces(count) for count in ALL_ROWS[1:]], []),
         compiler_params=pltpu.CompilerParams(
-            collective_id=2, has_side_effects=True, vmem_limit_bytes=VMEM_LIMIT
+            collective_id=1, has_side_effects=True, vmem_limit_bytes=BACKWARD_LIMIT
         ),
-        name="vector_backward",
-    )(
-        near, ev, hidden, ratio, update, gvone, vout, tv, nv, vs, vt, rest, gains,
-        s, m, f, back,
-    )
+        name="backward",
+    )(*blocked, *whole_operands, *hbm_operands)
 
 
 def finish_kernel(
-    plane_ref, got_ref, sent_ref, gscal_ref, gvec_ref,
+    plane_ref, got_ref, sent_ref, gscal_ref, gvec_ref, stream_ref,
     gs_ref, gv_ref, node_ref, edge_ref, norms_ref, vnode_ref, vedge_ref, vout_ref, ffv_ref, ffs_ref,
-    ffu_ref, embed_ref, qkv_ref, out_ref, up_ref, down_ref, gains_ref, row_scr, sent_scr,
+    ffu_ref, embed_ref, qkv_ref, out_ref, up_ref, down_ref, ngain_ref, again_ref, fgain_ref,
+    stream_out_ref, row_scr, sent_scr,
 ):
     base = 0
-    for rows in (ROWS_F, ROWS_M, ROWS_S, ROWS_T):
+    for rows in ALL_ROWS:
         eighth = rows // 8
         for half, order in enumerate(((0, 1, 2, 3), (0, 2, 1, 3))):
             for n, q in enumerate(order):
@@ -1741,20 +1765,21 @@
     down_ref[...] = take(at, 256)
     for n in range(4):
         up_ref[:, pl.ds(n * 512, 512)] = take(at + 256 + n * 64, 64)
-    at = ROWS_F
+    at += ROWS_F
     for n in range(3):
         qkv_ref[:, pl.ds(n * 512, 512)] = take(at + n * 64, 64)
     out_ref[...] = take(at + 192, 64)
-    embed_ref[...] = take(at + 256, 160)
+    at += ROWS_A
+    embed_ref[...] = take(at, 160)
     for n in range(2):
-        ffs_ref[:, pl.ds(n * 512, 512)] = take(at + 416 + n * 160, 160)
-    ffv_ref[...] = take(at + 736, 32, 0, 256)
-    ffu_ref[...] = take(at + 736, 32, 256, 256)
-    at += ROWS_M
+        ffs_ref[:, pl.ds(n * 512, 512)] = take(at + 160 + n * 160, 160)
+    ffv_ref[...] = take(at + 480, 32, 0, 256)
+    ffu_ref[...] = take(at + 480, 32, 256, 256)
+    at += ROWS_N
     for n in range(4):
         node_ref[:, pl.ds(n * 512, 512)] = take(at + n * 128, 128)
         norms_ref[pl.ds(n * 128, 128), :] = take(at + 512, 128, n * 128, 128)
-    at += ROWS_S
+    at += ROWS_S + ROWS_B
     tails = take(at + 96, 32, 0, 128)
     edge_ref[...] = take(at + 96, 32, 128, 128)
     extra = take(at + 96, 32, 256, 128)
@@ -1762,7 +1787,9 @@
     for n in range(5):
         width = min(128, H_V - n * 128)
         vedge_ref[:, pl.ds(n * 128, width)] = extra[1 + n : 2 + n, :width]
-    gains_ref[...] = extra[0:8]
+    ngain_ref[...] = extra[6]
+    again_ref[...] = extra[7, :64]
+    fgain_ref[...] = extra[7, 64:]
     vnode_ref[:, pl.ds(0, 512)] = take(at, 32)
     wide = jnp.concatenate([take(at + 32, 32), jnp.zeros((32, 128), F32)], 1)
     lane = lax.broadcasted_iota(jnp.int32, (32, 640), 1)
@@ -1770,10 +1797,9 @@
     wide = jnp.where(lane == 0, tails[:, 0:1], wide)
     wide = jnp.where(lane == 513, tails[:, 1:2], wide)
     vnode_ref[:, pl.ds(512, 514)] = wide[:, :514]
-    flat = jnp.concatenate([take(at + 64, 32), jnp.zeros((96, 512), F32)], 0)
-    vout_ref[pl.ds(0, 512), :] = jnp.transpose(flat)[:, :32]
-    flat = jnp.concatenate([tails, jnp.zeros((96, 128), F32)], 0)
-    vout_ref[pl.ds(512, 1), :] = jnp.transpose(flat)[2:3, :32]
+    vout_ref[:, pl.ds(0, 512)] = take(at + 64, 32)
+    vout_ref[:, pl.ds(512, 1)] = tails[:, 2:3]
+    stream_out_ref[...] = stream_ref[...]
     nodes = gscal_ref.shape[0]
     slots = got_ref.shape[0] * got_ref.shape[1]
     got = got_ref[...].reshape(slots, D_S + 3 * D_V)
@@ -1786,7 +1812,7 @@
         ).astype(BF)
 
 
-def finish(plane, got, sent, gscal, gvec):
+def finish(plane, got, sent, gscal, gvec, stream):
     nodes = gscal.shape[0]
     outs = [
         ((nodes, D_S), BF),
@@ -1796,7 +1822,7 @@
         ((513, 128), F32),
         ((32, 1026), F32),
         ((1, 513), F32),
-        ((513, 32), F32),
+        ((32, 513), F32),
         ((32, 256), F32),
         ((160, 1024), F32),
         ((32, 256), F32),
@@ -1805,18 +1831,21 @@
         ((64, 512), F32),
         ((64, 2048), F32),
         ((256, 512), F32),
-        ((8, 128), F32),
+        ((128,), F32),
+        ((64,), F32),
+        ((64,), F32),
+        (stream.shape, BF),
     ]
     return pl.pallas_call(
         finish_kernel,
         out_shape=[jax.ShapeDtypeStruct(shape, kind) for shape, kind in outs],
         scratch_shapes=[
-            pltpu.VMEM((ROWS_F + ROWS_M + ROWS_S + ROWS_T, 512), BF),
+            pltpu.VMEM((sum(ALL_ROWS), 512), BF),
             pltpu.VMEM((8, 128), F32),
         ],
         compiler_params=pltpu.CompilerParams(vmem_limit_bytes=VMEM_LIMIT),
         name="finish",
-    )(plane, got, sent, gscal, gvec)
+    )(plane, got, sent, gscal, gvec, stream)
 
 
 def pad_to(values, size, axis):
@@ -1867,29 +1896,31 @@
         agg_s, agg_v, hidden, lx, dsilu, update = message(
             near, edge_scalar.T, ev, mix, b_target, p_source, q_target, gain_row, vout
         )
-        stream_out, gsone, gvone, gains, middle_share, first_share, table_o, node_o = middle(
+        (
+            stream_out, gsone, gvone, gains, attention_share, node_share, early_share, table_o, node_o,
+        ) = middle(
             (
                 node_scalar, node_vector, agg_s, agg_v, gain_row, ff_vec, ff_scalar, ff_up,
                 w_embed, w_qkv, complex_id[None], cotangent,
             ),
             (w_out, w_up, w_down), table_s, node_scalar, quads,
         )
-        ratio, second_share, rest, gscal, back_s, middle_part, first_part = scalar_backward(
-            near, lx, dsilu, gsone, wn_mix, table_s, node_scalar, w_node, table_o, node_o,
-            middle_share, first_share,
-        )
-        plane, gvec, got = vector_backward(
-            near, ev, hidden, ratio, update, gvone, vout, table_v, node_vector,
-            vec_source, vec_target, rest, gains, second_share, middle_part, first_part, back_s,
+        gscal, gvec, plane, got = backward(
+            (near, ev, lx, dsilu, hidden, update),
+            (
+                gsone, wn_mix, gvone, vout, table_v, node_vector, vec_source, vec_target, gains,
+            ),
+            (table_s, node_scalar, w_node, table_o, node_o, early_share, attention_share, node_share),
         )
         (
             grad_scalar, grad_vector, out_node, out_edge, out_norms, out_vnode, out_vedge, out_vout,
-            out_ffv, out_ffs, out_ffu, out_embed, out_qkv, out_out, out_up, out_down, rows,
-        ) = finish(plane, got, sent, gscal, gvec)
+            out_ffv, out_ffs, out_ffu, out_embed, out_qkv, out_out, out_up, out_down, out_ng, out_ag,
+            out_fg, stream_out,
+        ) = finish(plane, got, sent, gscal, gvec, stream_out)
         return (
             stream_out, grad_scalar, grad_vector, out_node, out_edge, out_norms, out_vnode,
-            out_vedge, out_vout, rows[6], out_ffv, out_ffs, out_ffu, out_embed, rows[7, :64],
-            out_qkv, out_out, rows[7, 64:], out_up, out_down,
+            out_vedge, out_vout.T, out_ng, out_ffv, out_ffs, out_ffu, out_embed, out_ag,
+            out_qkv, out_out, out_fg, out_up, out_down,
         )
 
     sent_index = send_rows[0].reshape(-1)

time: 233 us -> 218 us (0.936)
  Pallas kernels: 222 us -> 211 us
  local copies, waits for them, and re-layouts: 9.46 us -> 4.53 us
    pallas_call x2 -> x1, Pallas kernels: 102 us -> 95.7 us  [backward(): pl.pallas_call(backward_kernel, grid=(2 * half,), in_specs=[whole(near.sh...]
    pallas_call x1, Pallas kernels: 61.8 us -> 57.2 us  [middle(): pl.pallas_call(middle_kernel, out_shape=[jax.ShapeDtypeStruct(shape, kind...]
    squeeze x2 -> x0, local copies, waits for them, and re-layouts: 2.54 us -> none  [the longest x1 1.34 us: body(): rows[7, 64:]]
    unnamed x4 -> x0, local copies, waits for them, and re-layouts: 2.39 us -> none
where the time goes in v1:
time: 218 us; the launch traced here: 217 us
  Pallas kernels  211 us (97%)
  local copies, waits for them, and re-layouts  4.53 us (2%)
    pallas_call x1, Pallas kernels, backward(): pl.pallas_call(backward_kernel, grid=(2 * half,), in_specs=[whole(near.sh...  95.7 us
    pallas_call x1, Pallas kernels, middle(): pl.pallas_call(middle_kernel, out_shape=[jax.ShapeDtypeStruct(shape, kind...  57.2 us
    pallas_call x1, Pallas kernels, message(): pl.pallas_call(message_kernel, grid=(NEIGH // GROUP,), in_specs=[whole(ne...  35.6 us
    pallas_call x1, Pallas kernels, prepare(): pl.pallas_call(prepare_kernel, out_shape=[jax.ShapeDtypeStruct(shape, kin...  18.2 us
    pallas_call x1, Pallas kernels, finish(): pl.pallas_call(finish_kernel, out_shape=[jax.ShapeDtypeStruct(shape, kind...  4.54 us

profile of v1, /device:TPU:0, one launch (start us, length us, event | category | flops | bytes accessed | tf_op | source)
XLA Modules:
  0.0 217.2 jit_solution(10338025785112210317)
XLA Ops:
  0.7 0.7 concatenate.17
  1.3 0.7 concatenate.18
  2.0 0.7 concatenate.16
  2.7 0.8 concatenate.19
  3.5 0.6 convert_element_type.20.ve_ref.gains_in
  4.1 1.0 reshape.103
  5.1 0.7 copy.45
  5.8 18.2 %prepare.1 = (f32[128,1024]{1,0:T(8,128)}, bf16[3,256,640]{2,1,0:T(8,128)(2,1)}, f32[3,128,640]{2,1,0:T(8,128)}, bf16[256,1024]{1,0:T(8,128)(2,1)}, bf16[3,256,2...) custom-call(bf16[128,1024]{1,0:T(8,128)(2,1)} %ns_hbm.3, ...), custom_call_target="tpu_custom_call" | custom-call | tf_op jit(solution)/shard_map/prepare/pallas_call | solution.py:1126
  24.0 35.6 %message.1 = (f32[128,1024]{1,0:T(8,128)}, f32[3,128,256]{2,1,0:T(8,128)}, bf16[30,3,128,640]{3,2,1,0:T(8,128)(2,1)}, bf16[30,128,640]{2,1,0:T(8,128)(2,1)}, bf1...) custom-call(s32[30,128]{1,0:T(8,128)} %bitcast.11, bf16[960,128]{1,0:T(8,128)(2,1)} %bitcast.10, ...), custom_call_target="tpu_custom_call" | custom-call | tf_op jit(solution)/shard_map/message/pallas_call | solution.py:305
  59.5 57.2 %middle.1 = (bf16[128,512]{1,0:T(8,128)(2,1)}, f32[128,1024]{1,0:T(8,128)}, f32[3,128,256]{2,1,0:T(8,128)}, f32[8,1024]{1,0:T(8,128)}, bf16[4,256,512]{2,1,0:T(8...) custom-call(bf16[128,1024]{1,0:T(8,128)(2,1)} %ns_hbm.3, ...), custom_call_target="tpu_custom_call" | custom-call | tf_op jit(solution)/shard_map/middle/pallas_call | solution.py:1273
  116.8 95.7 %backward.1 = (f32[128,1024]{1,0:T(8,128)}, f32[3,128,256]{2,1,0:T(8,128)}, bf16[4,512,512]{2,1,0:T(8,128)(2,1)}, bf16[8,16,1792]{2,1,0:T(8,128)(2,1)}) custom-call(s32[30,128]{1,0:T(8,128)} %bitcast.12, f32[3,30,128]{2,1,0:T(8,128)} %bitcast.9, bf16[30,128,640]{2,1,0:T(8,128)(2,1)} %get-tuple-element.74.lx_ref, ...), custom_call_target="tpu_custom_call" | custom-call | tf_op jit(solution)/shard_map/backward/pallas_call | solution.py:1702
  212.5 4.5 %finish.1 = (bf16[128,1024]{1,0:T(8,128)(2,1)}, bf16[3,128,256]{2,1,0:T(8,128)(2,1)}, f32[128,2048]{1,0:T(8,128)}, f32[32,128]{1,0:T(8,128)}, f32[513,128]{1,0:T...) custom-call(bf16[4,512,512]{2,1,0:T(8,128)(2,1)} %get-tuple-element., ...), custom_call_target="tpu_custom_call" | custom-call | tf_op jit(solution)/shard_map/finish/pallas_call | solution.py:1839
  (1 shorter events, 0.0 us)

commit v2 on v1

--- a/solution.py
+++ b/solution.py
@@ -196,12 +196,34 @@
 
 
 def message_kernel(
-    near_ref, es_ref, ev_ref, a_ref, b_ref, p_ref, q_ref, ve_ref, vo_ref,
-    aggs_ref, aggv_ref, h_ref, lx_ref, ds_ref, z_ref, x_scr, turn_scr,
+    near_ref, es_ref, ev_ref, ve_ref, ns_ref, nv_ref, sent_ref, vn_ref, we_ref, vout_ref, norms_ref,
+    wnode_hbm,
+    aggs_ref, aggv_ref, h_ref, lx_ref, ds_ref, z_ref, ts_hbm, tv_hbm, vs_hbm, vt_hbm, vo_hbm, wn_hbm,
+    x_scr, turn_scr, b_ref, p_ref, q_ref, ts_ref, tv_ref, vs_ref, vt_ref, vo_ref, a_ref, wn_ref,
+    pt_ref, wnode, row_scr, vt_scr, out_scr, in_scr, send_sem, recv_sem, load_sem, keep_sem,
 ):
     nodes = b_ref.shape[0]
     table = p_ref.shape[1]
     rows = GROUP * nodes
+    keeps = [
+        pltpu.make_async_copy(source, target, keep_sem.at[n])
+        for n, (source, target) in enumerate(
+            (
+                (ts_ref, ts_hbm), (tv_ref, tv_hbm), (vs_ref, vs_hbm), (vt_ref, vt_hbm),
+                (vo_ref, vo_hbm), (wn_ref, wn_hbm),
+            )
+        )
+    ]
+
+    @pl.when(pl.program_id(0) == 0)
+    def _():
+        prepare_kernel(
+            ns_ref, nv_ref, sent_ref, vn_ref, we_ref, vout_ref, norms_ref, wnode_hbm,
+            b_ref, p_ref, q_ref, ts_ref, tv_ref, vs_ref, vt_ref, vo_ref, a_ref, wn_ref, pt_ref,
+            wnode, row_scr, vt_scr, out_scr, in_scr, send_sem, recv_sem, load_sem,
+        )
+        start_all(keeps)
+
     first_slot = pl.program_id(0) * GROUP
 
     @pl.when(pl.program_id(0) == 0)
@@ -234,7 +256,15 @@
     one_hot = x_scr[:, :table]
     for start, width in LANE_BLOCKS:
         cols = pl.ds(start, width)
-        gathered = [product(one_hot, p_ref[c, :, cols]) for c in range(3)]
+        if start == 512:
+            lane = lax.broadcasted_iota(jnp.int32, (rows, width), 1)
+            three = product(one_hot, pt_ref[...])
+            gathered = [
+                jnp.where(lane == 0, three if c == 0 else pltpu.roll(three, width - c, 1), 0.0)
+                for c in range(3)
+            ]
+        else:
+            gathered = [product(one_hot, p_ref[c, :, cols]) for c in range(3)]
         for k in range(GROUP):
             for first in range(0, nodes, ROW_TILE):
                 at = k * nodes + first
@@ -279,14 +309,20 @@
                 acc = y if acc is None else acc + y
             aggs_ref[part, cols] += acc * (1.0 / NEIGH)
     ups = [
-        product(h_ref[:, c, :, :].reshape(rows, H_P), vo_ref[...]) for c in range(3)
+        product(h_ref[:, c, :, pl.ds(0, 512)].reshape(rows, 512), vo_ref[pl.ds(0, 512), :])
+        for c in range(3)
     ]
+    last_row = vo_ref[pl.ds(512, 16), :].astype(F32)[0:1, :]
     for first in range(0, nodes, ROW_TILE):
         part = pl.ds(first, ROW_TILE)
         acc = [None] * 3
         for k in range(GROUP):
             at = k * nodes + first
-            z = [ups[c][at : at + ROW_TILE] for c in range(3)]
+            z = [
+                ups[c][at : at + ROW_TILE]
+                + h_ref[k, c, part, pl.ds(512, 128)].astype(F32)[:, 0:1] * last_row
+                for c in range(3)
+            ]
             power = z[0] * z[0] + z[1] * z[1] + z[2] * z[2] + 1.0
             s = sigmoid(power * lax.rsqrt(power))
             for c in range(3):
@@ -296,26 +332,37 @@
         for c in range(3):
             aggv_ref[c, part, :] += acc[c] * (1.0 / NEIGH)
 
-
-def message(near, edge_scalar, ev, mix, b_target, p_source, q_target, ve_row, vout):
-    nodes = b_target.shape[0]
-    table = p_source.shape[1]
-    whole = lambda shape: pl.BlockSpec(shape, lambda g: (0,) * len(shape))
+    @pl.when(pl.program_id(0) == pl.num_programs(0) - 1)
+    def _():
+        wait_all(keeps)
+
+
+def message(operands, w_node):
+    near, edge_scalar, ev, gain_row, node_scalar, node_vector, sent = operands[:7]
+    nodes = node_scalar.shape[0]
+    spaces = sent.shape[0]
+    table = nodes + spaces * CAP
+    rows = GROUP * nodes
+    once = pl.Buffered(1)
+    whole = lambda shape: pl.BlockSpec(shape, lambda g: (0,) * len(shape), pipeline_mode=once)
     slots = lambda *shape: pl.BlockSpec((GROUP,) + shape, lambda g: (g,) + (0,) * len(shape))
+    hbm = pl.BlockSpec(memory_space=pl.ANY)
+    bits = lambda *shape: pltpu.VMEM(shape, BF)
+    wide = lambda *shape: pltpu.VMEM(shape, F32)
+    kept = [(table, D_S), (3, table, D_V), (H_P, D_V), (H_P, D_V), (H_P, D_V), (H_P, D_S)]
+    outs = [
+        ((nodes, D_S), F32),
+        ((3, nodes, D_V), F32),
+        ((NEIGH, 3, nodes, H_P), BF),
+        ((NEIGH, nodes, H_P), BF),
+        ((NEIGH, nodes, D_S), BF),
+        ((NEIGH, 3, nodes, D_V), BF),
+    ] + [(shape, BF) for shape in kept]
+    blocks = (spaces, CAP, D_S + 3 * D_V)
     return pl.pallas_call(
         message_kernel,
         grid=(NEIGH // GROUP,),
-        in_specs=[
-            whole(near.shape),
-            whole(edge_scalar.shape),
-            whole(ev.shape),
-            whole((table + H_P, D_S)),
-            whole((nodes, D_S)),
-            whole((3, table, H_P)),
-            whole((3, nodes, H_P)),
-            whole(ve_row.shape),
-            whole((H_P, D_V)),
-        ],
+        in_specs=[whole(one.shape) for one in operands] + [hbm],
         out_specs=[
             whole((nodes, D_S)),
             whole((3, nodes, D_V)),
@@ -323,22 +370,24 @@
             slots(nodes, H_P),
             slots(nodes, D_S),
             slots(3, nodes, D_V),
+        ]
+        + [hbm] * len(kept),
+        out_shape=[jax.ShapeDtypeStruct(shape, kind) for shape, kind in outs],
+        scratch_shapes=[
+            bits(rows, table + H_P), wide(4, 128, nodes), wide(nodes, D_S), bits(3, table, H_P),
+            wide(3, nodes, H_P), bits(*kept[0]), bits(*kept[1]), bits(*kept[2]), bits(*kept[3]),
+            bits(*kept[4]), bits(table + H_P, D_S), bits(*kept[5]), bits(table, 128),
+            bits(*w_node.shape), wide(8, 128), wide(H_P, D_V), bits(*blocks), bits(*blocks),
+            pltpu.SemaphoreType.DMA((spaces - 1,)),
+            pltpu.SemaphoreType.DMA((spaces - 1,)),
+            pltpu.SemaphoreType.DMA,
+            pltpu.SemaphoreType.DMA((len(kept),)),
         ],
-        out_shape=[
-            jax.ShapeDtypeStruct((nodes, D_S), F32),
-            jax.ShapeDtypeStruct((3, nodes, D_V), F32),
-            jax.ShapeDtypeStruct((NEIGH, 3, nodes, H_P), BF),
-            jax.ShapeDtypeStruct((NEIGH, nodes, H_P), BF),
-            jax.ShapeDtypeStruct((NEIGH, nodes, D_S), BF),
-            jax.ShapeDtypeStruct((NEIGH, 3, nodes, D_V), BF),
-        ],
-        scratch_shapes=[
-            pltpu.VMEM((GROUP * nodes, table + H_P), BF),
-            pltpu.VMEM((4, 128, nodes), F32),
-        ],
-        compiler_params=pltpu.CompilerParams(vmem_limit_bytes=VMEM_LIMIT),
+        compiler_params=pltpu.CompilerParams(
+            collective_id=3, has_side_effects=True, vmem_limit_bytes=VMEM_LIMIT
+        ),
         name="message",
-    )(near, edge_scalar, ev, mix, b_target, p_source, q_target, ve_row, vout)
+    )(*operands, w_node)
 
 
 def edge_backward_kernel(
@@ -1039,7 +1088,7 @@
 
 def prepare_kernel(
     ns_ref, nv_ref, sent_ref, vn_ref, we_ref, vout_ref, norms_ref, wnode_hbm,
-    b_ref, p_ref, q_ref, ts_ref, tv_ref, vs_ref, vt_ref, vo_ref, mix_ref, wn_ref,
+    b_ref, p_ref, q_ref, ts_ref, tv_ref, vs_ref, vt_ref, vo_ref, mix_ref, wn_ref, pt_ref,
     wnode, row_scr, vt_scr, out_scr, in_scr, send_sem, recv_sem, load_sem,
 ):
     nodes = ns_ref.shape[0]
@@ -1077,9 +1126,19 @@
     vo_ref[pl.ds(0, 512), :] = vout_ref[pl.ds(0, 512), :]
     first = jnp.broadcast_to(vout_ref[pl.ds(512, 1), :].astype(F32), low.shape)
     vo_ref[pl.ds(512, H_P - 512), :] = jnp.where(low == 0, first, 0.0).astype(BF)
+
+    def project(parts, start):
+        last = None
+        for c in range(3):
+            whole = product_back(parts[c], vs_ref[...])
+            p_ref[c, pl.ds(start, parts[c].shape[0]), :] = whole.astype(BF)
+            tail = whole[:, 512:]
+            last = tail if last is None else last + pltpu.roll(tail, c, 1)
+        pt_ref[pl.ds(start, parts[0].shape[0]), :] = last.astype(BF)
+
+    project([nv_ref[c] for c in range(3)], 0)
     for c in range(3):
         q_ref[c] = product_back(nv_ref[c], vt_ref[...])
-        p_ref[c, pl.ds(0, nodes), :] = product_back(nv_ref[c], vs_ref[...]).astype(BF)
         tv_ref[c, pl.ds(0, nodes), :] = nv_ref[c]
     ts_ref[pl.ds(0, nodes), :] = ns_ref[...]
     first = jnp.broadcast_to(norms_ref[pl.ds(512, 1), :].astype(F32), (16, D_S))
@@ -1098,51 +1157,10 @@
     mix_ref[pl.ds(nodes, table - nodes), :] = product(
         got[:, :D_S], wnode[:, pl.ds(0, D_S)]
     ).astype(BF)
+    parts = [got[:, D_S + c * D_V : D_S + (c + 1) * D_V] for c in range(3)]
+    project(parts, nodes)
     for c in range(3):
-        rows = got[:, D_S + c * D_V : D_S + (c + 1) * D_V]
-        tv_ref[c, pl.ds(nodes, table - nodes), :] = rows
-        p_ref[c, pl.ds(nodes, table - nodes), :] = product_back(rows, vs_ref[...]).astype(BF)
-
-
-def prepare(node_scalar, node_vector, sent, vec_node, w_edge, vec_out, w_norms, w_node):
-    nodes = node_scalar.shape[0]
-    spaces = sent.shape[0]
-    table = nodes + spaces * CAP
-    hbm = pl.BlockSpec(memory_space=pl.ANY)
-    vmem = pl.BlockSpec(memory_space=pltpu.VMEM)
-    outs = [
-        ((nodes, D_S), F32),
-        ((3, table, H_P), BF),
-        ((3, nodes, H_P), F32),
-        ((table, D_S), BF),
-        ((3, table, D_V), BF),
-        ((H_P, D_V), BF),
-        ((H_P, D_V), BF),
-        ((H_P, D_V), BF),
-        ((table + H_P, D_S), BF),
-        ((H_P, D_S), BF),
-    ]
-    blocks = (spaces, CAP, D_S + 3 * D_V)
-    return pl.pallas_call(
-        prepare_kernel,
-        out_shape=[jax.ShapeDtypeStruct(shape, kind) for shape, kind in outs],
-        in_specs=[vmem] * 7 + [hbm],
-        out_specs=[vmem] * 10,
-        scratch_shapes=[
-            pltpu.VMEM(w_node.shape, BF),
-            pltpu.VMEM((8, 128), F32),
-            pltpu.VMEM((H_P, D_V), F32),
-            pltpu.VMEM(blocks, BF),
-            pltpu.VMEM(blocks, BF),
-            pltpu.SemaphoreType.DMA((spaces - 1,)),
-            pltpu.SemaphoreType.DMA((spaces - 1,)),
-            pltpu.SemaphoreType.DMA,
-        ],
-        compiler_params=pltpu.CompilerParams(
-            collective_id=3, has_side_effects=True, vmem_limit_bytes=VMEM_LIMIT
-        ),
-        name="prepare",
-    )(node_scalar, node_vector, sent, vec_node, w_edge, vec_out, w_norms, w_node)
+        tv_ref[c, pl.ds(nodes, table - nodes), :] = parts[c]
 
 
 def middle_kernel(
@@ -1438,7 +1456,7 @@
         (4, 0): [share_a.cut],
         (7, 0): [share_a.spread],
         (7, 1): [share_n.spread],
-        (8, 1): [share_s.cut],
+        (9, 0): [share_s.cut],
         (9, 1): [early_total],
         (10, 0): [share_b.cut],
         (10, 1): [share_s.spread, middle_total],
@@ -1510,6 +1528,10 @@
 
     @pl.when(step == half)
     def _():
+        share_n.cut()
+
+    @pl.when(step == half + 1)
+    def _():
         wait_all(pair_copies)
         grad_rows = pl.ds(0, table), pl.ds(table, nodes)
         for side, (left, lefto, pack) in enumerate(
@@ -1523,7 +1545,6 @@
                 for n in range(2):
                     pack[z, pl.ds(n * 128, 128), :] = block[:, n * 512 : (n + 1) * 512]
             if side == 0:
-                share_n.cut()
                 share_s.start()
         for z in range(quads):
             own = pl.ds(pl.multiple_of((2 * z + core) * 128, 128), 128)
@@ -1884,17 +1905,21 @@
         sent = send_rows[0]
         near = neighbours.T
         ev = edge_vector.reshape(3, local_rows, NEIGH).transpose(0, 2, 1).astype(F32)
-        gain_row = jnp.concatenate(
-            [norm_gain, attn_gain, ffn_gain, vec_edge[0], jnp.zeros((H_P - H_V,), BF)]
-        )
-        gain_row = gain_row.astype(F32)[None]
+        gain_row, at = 0.0, 0
+        for gain in (norm_gain, attn_gain, ffn_gain, vec_edge[0]):
+            after = D_S + 2 * D_MODEL + H_P - at - gain.shape[0]
+            gain_row = gain_row + jnp.pad(gain.astype(F32), (at, after))
+            at += gain.shape[0]
+        gain_row = gain_row[None]
         (
-            b_target, p_source, q_target, table_s, table_v, vec_source, vec_target, vout, mix, wn_mix,
-        ) = prepare(
-            node_scalar, node_vector, sent, vec_node.T, w_edge, vec_out, w_norms, w_node
-        )
-        agg_s, agg_v, hidden, lx, dsilu, update = message(
-            near, edge_scalar.T, ev, mix, b_target, p_source, q_target, gain_row, vout
+            agg_s, agg_v, hidden, lx, dsilu, update, table_s, table_v, vec_source, vec_target, vout,
+            wn_mix,
+        ) = message(
+            (
+                near, edge_scalar.T, ev, gain_row, node_scalar, node_vector, sent, vec_node.T, w_edge,
+                vec_out, w_norms,
+            ),
+            w_node,
         )
         (
             stream_out, gsone, gvone, gains, attention_share, node_share, early_share, table_o, node_o,

time: 218 us -> 201 us (0.922)
  Pallas kernels: 211 us -> 196 us
  local copies, waits for them, and re-layouts: 4.53 us -> 2.3 us
    pallas_call x1, Pallas kernels: 95.7 us -> 86.1 us  [backward(): pl.pallas_call(backward_kernel, grid=(2 * half,), in_specs=[whole(near.sh...]
    pallas_call x2 -> x1, Pallas kernels: 53.7 us -> 48 us  [message(): pl.pallas_call(message_kernel, grid=(NEIGH // GROUP,), in_specs=[whole(on...]
    concatenate x4 -> x0, local copies, waits for them, and re-layouts: 2.83 us -> none  [body(): jnp.concatenate([norm_gain, attn_gain, ffn_gain, vec_edge[0], jnp.zeros((...]
where the time goes in v2:
time: 201 us; the launch traced here: 200 us
  Pallas kernels  196 us (98%)
  local copies, waits for them, and re-layouts  2.3 us (1%)
    pallas_call x1, Pallas kernels, backward(): pl.pallas_call(backward_kernel, grid=(2 * half,), in_specs=[whole(near.sh...  86.1 us
    pallas_call x1, Pallas kernels, middle(): pl.pallas_call(middle_kernel, out_shape=[jax.ShapeDtypeStruct(shape, kind...  57.2 us
    pallas_call x1, Pallas kernels, message(): pl.pallas_call(message_kernel, grid=(NEIGH // GROUP,), in_specs=[whole(on...  48 us
    pallas_call x1, Pallas kernels, finish(): pl.pallas_call(finish_kernel, out_shape=[jax.ShapeDtypeStruct(shape, kind...  4.54 us

profile of v2, /device:TPU:0, one launch (start us, length us, event | category | flops | bytes accessed | tf_op | source)
XLA Modules:
  0.0 200.4 jit_solution(14515860301091029329)
XLA Ops:
  0.7 0.7 reduce
  1.4 0.7 convert_add_fusion
  2.1 0.6 broadcast_in_dim.6.ve_ref.gains_in
  2.7 1.0 reshape.45
  3.7 0.7 copy.45
  4.4 48.0 %message.1 = (f32[128,1024]{1,0:T(8,128)}, f32[3,128,256]{2,1,0:T(8,128)}, bf16[30,3,128,640]{3,2,1,0:T(8,128)(2,1)}, bf16[30,128,640]{2,1,0:T(8,128)(2,1)}, bf1...) custom-call(s32[30,128]{1,0:T(8,128)} %bitcast.11, ...), custom_call_target="tpu_custom_call" | custom-call | tf_op jit(solution)/shard_map/message/pallas_call | solution.py:362
  52.4 57.2 %middle.1 = (bf16[128,512]{1,0:T(8,128)(2,1)}, f32[128,1024]{1,0:T(8,128)}, f32[3,128,256]{2,1,0:T(8,128)}, f32[8,1024]{1,0:T(8,128)}, bf16[4,256,512]{2,1,0:T(8...) custom-call(bf16[128,1024]{1,0:T(8,128)(2,1)} %ns_hbm.3, ...), custom_call_target="tpu_custom_call" | custom-call | tf_op jit(solution)/shard_map/middle/pallas_call | solution.py:1291
  109.6 86.1 %backward.1 = (f32[128,1024]{1,0:T(8,128)}, f32[3,128,256]{2,1,0:T(8,128)}, bf16[4,512,512]{2,1,0:T(8,128)(2,1)}, bf16[8,16,1792]{2,1,0:T(8,128)(2,1)}) custom-call(s32[30,128]{1,0:T(8,128)} %bitcast.12, f32[3,30,128]{2,1,0:T(8,128)} %bitcast.9, bf16[30,128,640]{2,1,0:T(8,128)(2,1)} %get-tuple-element.65.lx_ref, ...), custom_call_target="tpu_custom_call" | custom-call | tf_op jit(solution)/shard_map/backward/pallas_call | solution.py:1723
  195.7 4.5 %finish.1 = (bf16[128,1024]{1,0:T(8,128)(2,1)}, bf16[3,128,256]{2,1,0:T(8,128)(2,1)}, f32[128,2048]{1,0:T(8,128)}, f32[32,128]{1,0:T(8,128)}, f32[513,128]{1,0:T...) custom-call(bf16[4,512,512]{2,1,0:T(8,128)(2,1)} %get-tuple-element., ...), custom_call_target="tpu_custom_call" | custom-call | tf_op jit(solution)/shard_map/finish/pallas_call | solution.py:1860
